TPU v7x, 256 devices: a whole 4x4x8 slice. The times are simulated.
256 devices in a mesh: dp: 128 (over y_lo, x, z, core), group: 2 (over y_hi).
Axes of the slice: x: 4, y: 4 (y_hi: 2, y_lo: 2; y = y_hi * 2 + y_lo), z: 8, core: 2. Of those that a mesh axis runs over, the one named last changes fastest.
Arguments:
- inputs: bfloat16 [256, 64, 5120], P('dp'), may hold values from -6 to 6
- out_grads: bfloat16 [256, 64, 8192], P('dp'), may hold values from -6 to 6
- proj_in: bfloat16 [5120, 64], replicated, may hold values from -0.078125 to 0.078125
- proj_out: bfloat16 [8192, 64], P(None, 'group'), may hold values from -0.0625 to 0.0625
- store: bfloat16 [131072, 4096], P('dp', 'group'), may hold values from -6 to 6
- valid: bfloat16 [2048, 4096], P('dp', 'group'), may hold values from -6 to 6
- owner: int32 [256], replicated, may hold values from 0 to 255, each once
Outputs:
- scores: bfloat16 [131072, 2048], P('dp', 'group')
Inputs may be any that keep to these rules, and one draw needn't show every extreme that they name: owner is a permutation of the 256 fresh slots.
All inputs are finite; a program needn't handle non-finite values.
Results may differ from a plain program's by a relative error of at most 0.0024.
Values may be sent and summed in bfloat16 or wider, within the bound.
No kernel may reach another device: no remote copies, remote signals or barrier semaphores. Data moves between devices by JAX's collectives and lax.ppermute only.
A program may use at most 128 MiB of HBM per device.

v0:
```python
import jax
import jax.numpy as jnp
from jax import lax
from jax.sharding import PartitionSpec as P


def against(slab, pieces):
    return lax.dot_general(
        slab, pieces, (((1,), (1,)), ((), ())), preferred_element_type=jnp.float32
    )


def local(inputs, out_grads, proj_in, proj_out, store, valid, owner):
    examples, length, width_in = inputs.shape
    width_out = out_grads.shape[2]
    lin = jnp.dot(
        inputs.reshape(examples * length, width_in), proj_in, preferred_element_type=jnp.float32
    ).astype(jnp.bfloat16)
    lout = jnp.dot(
        out_grads.reshape(examples * length, width_out),
        proj_out,
        preferred_element_type=jnp.float32,
    ).astype(jnp.bfloat16)
    lin = lin.reshape(examples, length, -1)
    lout = lout.reshape(examples, length, -1)
    sketch = jnp.einsum("nso,nsi->noi", lout, lin, preferred_element_type=jnp.float32) * length ** (
        -0.5
    )
    sketch = sketch.reshape(examples, -1).astype(jnp.bfloat16)
    half_width = sketch.shape[1]
    position = lax.axis_index("dp")
    everyone = lax.all_gather(sketch, "dp", axis=0, tiled=True)
    my_slots = position * examples + jnp.arange(examples, dtype=jnp.int32)
    picker = (owner[None, :] == my_slots[:, None]).astype(jnp.bfloat16)
    fresh = jnp.dot(picker, everyone, preferred_element_type=jnp.float32).astype(jnp.bfloat16)
    slab = jnp.concatenate([fresh, store[examples:]], axis=0)
    factor = (half_width * lax.axis_size("group")) ** (-0.5)
    partial_scores = against(slab, lax.all_gather(valid, "dp", axis=0, tiled=True)) * factor
    summed = lax.psum_scatter(partial_scores, "group", scatter_dimension=1, tiled=True)
    return summed.astype(jnp.bfloat16)


def solution(mesh):
    return jax.shard_map(
        local,
        mesh=mesh,
        in_specs=(
            P("dp", None, None),
            P("dp", None, None),
            P(),
            P(None, "group"),
            P("dp", "group"),
            P("dp", "group"),
            P(),
        ),
        out_specs=P("dp", "group"),
        check_vma=False,
    )
```

profile of v0, /device:TPU:1, one launch (start us, length us, event | category | flops | bytes accessed | tf_op | source)
XLA Modules:
  0.0 578.5 jit_solution(9552073787482592076)
XLA Ops:
  6.5 0.0 copy-start
  6.5 0.0 all-gather.6.cloned.1.call-start
  6.5 1.6 copy-done
  8.1 1.8 convolution_convert_fusion.2
  10.0 0.1 reshape.20
  10.1 2.1 convolution_convert_fusion.1
  12.1 0.1 copy.12
  12.2 0.1 fusion.3
  12.4 0.7 reshape.23
  13.1 0.0 all-gather.6.cloned.1.call-update
  13.1 0.0 all-gather.4.cloned.1.call-start
  13.2 0.7 all-gather.4.cloned.1.call-update
  13.9 0.0 reduce-scatter.2.cloned.1.call-start
  13.9 0.0 copy-start.1
  13.9 5.5 slice.3
  19.4 206.8 %all-gather.6.cloned.1.call-done = bf16[128,2,2048]{2,1,0:T(2,128)(2,1)} async-done(((bf16[1,2,2048]{2,1,0:T(2,128)(2,1)}), bf16[128,2,2048]{2,1,0:T(2,128)(2,1)}) %all-gather.6.cloned.1.call-update) | async-done | bytes 1048592 | tf_op jit(solution)/shard_map/all_gather | solution.py:32
  226.2 1.5 reshape.24
  227.6 0.0 copy-done.1
  227.6 0.3 convolution_convert_fusion
  227.9 220.6 %all-gather.4.cloned.1.call-done = bf16[2048,2048]{1,0:T(8,128)(2,1)} async-done(((bf16[16,2048]{1,0:T(8,128)(2,1)}), bf16[2048,2048]{1,0:T(8,128)(2,1)}) %all-gather.4.cloned.1.call-update) | async-done | bytes 8388624 | tf_op jit(solution)/shard_map/all_gather | solution.py:38
  448.5 14.6 %convolution_multiply_fusion = f32[1024,2048]{1,0:T(8,128)} fusion(bf16[2048,2048]{1,0:T(8,128)(2,1)} %all-gather.4.cloned.1.call-done, bf16[1022,2048]{1,0:T(8,128)(2,1)} %slice.3, bf16[2,2048]{1,0:T(2,128)(2,1)S(1)} %convolution_convert_fusion), kind=kOutput, calls=%fused_computation | convolution fusion | flops 8600420352 | bytes 20971520 | tf_op jit(solution)/shard_map/dot_general | solution.py:8
  463.1 0.0 reduce-scatter.2.cloned.1.call-update
  463.1 105.0 %reduce-scatter.2.cloned.1.call-done = f32[1024,1024]{1,0:T(8,128)} async-done(((f32[1024,2048]{1,0:T(8,128)}), f32[1024,1024]{1,0:T(8,128)}) %reduce-scatter.2.cloned.1.call-update) | async-done | bytes 4194320 | tf_op jit(solution)/shard_map/reduce_scatter | solution.py:39
  568.1 3.8 convert_element_type.24
  (1 shorter events, 0.0 us)
Async XLA Ops:
  6.5 1.6 copy-start
  6.5 219.6 %all-gather.6.cloned.1.call-start = ((), (), s32[]{:S(2)}) async-start(), calls=%async_computation.3 | async-start | bytes 1056768 | tf_op jit(solution)/shard_map/all_gather | solution.py:32
  13.1 435.4 %all-gather.4.cloned.1.call-start = ((), (), s32[]{:S(2)}) async-start(), calls=%async_computation.1 | async-start | bytes 8454144 | tf_op jit(solution)/shard_map/all_gather | solution.py:38
  13.9 554.2 %reduce-scatter.2.cloned.1.call-start = ((), (), s32[]{:S(2)}) async-start(), calls=%async_computation.2 | async-start | bytes 12582912 | tf_op jit(solution)/shard_map/reduce_scatter | solution.py:39
  13.9 213.7 %copy-start.1 = (s32[256]{0:T(256)S(1)}, s32[256]{0:T(256)}, u32[]{:S(2)}) copy-start(s32[256]{0:T(256)} %param.13) | copy-start | bytes 3076
Sparse Core Ops, SparseCore 0:
  13.2 212.8 all-gather.5
  228.0 220.4 all-gather.3
  463.2 104.8 reduce-scatter.1
where the time goes:
time: 579 us; the launch traced here: 578 us
  waiting for transfers between devices  533 us (92%)
  matrix products  18.9 us (3%)
  between operations  13.2 us (2%)
  local copies, waits for them, and re-layouts  9.44 us (2%)
    all_gather x1, waiting for transfers between devices, local(): lax.all_gather(valid, 'dp', axis=0, tiled=True)  221 us
    all_gather x1, waiting for transfers between devices, local(): everyone = lax.all_gather(sketch, 'dp', axis=0, tiled=True)  207 us
    reduce_scatter x1, waiting for transfers between devices, local(): lax.psum_scatter(partial_scores, 'group', scatter_dimension=1, tiled=True)  105 us
    dot_general x1, matrix products, against(): lax.dot_general(slab, pieces, (((1,), (1,)), ((), ())), preferred_element...  14.6 us
  transfers between devices with their start and end apart: 3, of which 3 were waited for; matrix products, arithmetic and copies ran while one was open for 1% of the time, Pallas kernels for 0%

commit v1 on v0

v1 whole, which is shorter than its diff:
```python
import jax
import jax.numpy as jnp
from jax import lax
from jax.sharding import Mesh, PartitionSpec as P

DP = ("yl", "x", "z", "c")
SIZES = {"yl": 2, "x": 4, "z": 8, "c": 2, "yh": 2}


def shifted(array, axis, by):
    size = SIZES[axis]
    return lax.ppermute(array, axis, [(i, (i + by) % size) for i in range(size)])


def dot_t(left, right):
    return lax.dot_general(
        left, right, (((1,), (1,)), ((), ())), preferred_element_type=jnp.float32
    )


def make_sketch(inputs, out_grads, proj_in, proj_out):
    examples, length, width_in = inputs.shape
    width_out = out_grads.shape[2]
    lin = jnp.dot(
        inputs.reshape(examples * length, width_in), proj_in, preferred_element_type=jnp.float32
    ).astype(jnp.bfloat16)
    lout = jnp.dot(
        out_grads.reshape(examples * length, width_out),
        proj_out,
        preferred_element_type=jnp.float32,
    ).astype(jnp.bfloat16)
    lin = lin.reshape(examples, length, -1)
    lout = lout.reshape(examples, length, -1)
    sketch = jnp.einsum("nso,nsi->noi", lout, lin, preferred_element_type=jnp.float32) * length ** (
        -0.5
    )
    return sketch.reshape(examples, -1).astype(jnp.bfloat16)


def local(inputs, out_grads, proj_in, proj_out, store, valid, owner):
    yl, x, z, c, yh = (lax.axis_index(a) for a in ("yl", "x", "z", "c", "yh"))
    nx, nz, nc = SIZES["x"], SIZES["z"], SIZES["c"]
    examples = inputs.shape[0]
    rows_v = valid.shape[0]

    received = shifted(store, "yh", 1)

    sketch = make_sketch(inputs, out_grads, proj_in, proj_out)
    half = sketch.shape[1]

    first = jnp.concatenate([valid, sketch], axis=0)
    first = jnp.concatenate([first, shifted(first, "yh", 1)], axis=1)
    other = shifted(first, "yl", 1)
    mine_v = jnp.where(yl == yh, first[:rows_v], other[:rows_v])
    second = jnp.concatenate([mine_v, first[rows_v:], other[rows_v:]], axis=0)

    pieces = [second] + [shifted(second, "x", k) for k in range(1, nx)]
    block = jnp.zeros((nx, rows_v, 2 * half), valid.dtype)
    for k, piece in enumerate(pieces):
        block = lax.dynamic_update_slice(block, piece[None, :rows_v], ((x - k) % nx, 0, 0))
    block = block.reshape(nx * rows_v, 2 * half)
    known = jnp.concatenate([piece[rows_v:] for piece in pieces], axis=0)

    def dp_index(yl_, x_, z_, c_):
        return ((yl_ * nx + x_) * nz + z_) * nc + c_

    from_x = (x - jnp.arange(nx, dtype=jnp.int32)) % nx
    from_yl = (yl + jnp.arange(2, dtype=jnp.int32)) % 2
    example = dp_index(from_yl[None, :, None], from_x[:, None, None], z, c) * examples
    example = (example + jnp.arange(examples, dtype=jnp.int32)).reshape(-1)
    slot_of = owner[example]
    to = dp_index(yl, x, jnp.arange(nz, dtype=jnp.int32)[:, None], jnp.arange(nc, dtype=jnp.int32))
    slot = (to[:, :, None] * examples + jnp.arange(examples, dtype=jnp.int32)).reshape(-1)
    picker = (slot[:, None] == slot_of[None, :]).astype(jnp.bfloat16)
    shares = jnp.dot(picker, known, preferred_element_type=jnp.float32).astype(jnp.bfloat16)
    shares = shares.reshape(nz, nc * examples, 2 * half)

    def share(offset):
        return lax.dynamic_index_in_dim(shares, (z + offset) % nz, 0, keepdims=False)

    rows_b = block.shape[0]
    cut = rows_b // 2
    full = jnp.zeros((nz, rows_b, 2 * half), valid.dtype)
    full = lax.dynamic_update_slice(full, block[None], (z, 0, 0))
    ahead, back = block, block
    ahead_s, back_s = share(4), share(-3)
    for k in range(1, 4):
        ahead_all = shifted(jnp.concatenate([ahead, ahead_s], axis=0), "z", 1)
        back_all = shifted(jnp.concatenate([back, back_s], axis=0), "z", -1)
        ahead, ahead_s = ahead_all[:rows_b], ahead_all[rows_b:] + share(4 - k)
        back, back_s = back_all[:rows_b], back_all[rows_b:] + share(k - 3)
        full = lax.dynamic_update_slice(full, ahead[None], ((z - k) % nz, 0, 0))
        full = lax.dynamic_update_slice(full, back[None], ((z + k) % nz, 0, 0))
    ahead_all = shifted(jnp.concatenate([ahead[:cut], ahead_s], axis=0), "z", 1)
    back_half = shifted(back[cut:], "z", -1)
    far = jnp.concatenate([ahead_all[:cut], back_half], axis=0)
    full = lax.dynamic_update_slice(full, far[None], ((z - 4) % nz, 0, 0))
    fresh = (ahead_all[cut:] + back_s).reshape(nc, examples, 2 * half)

    swap = jnp.concatenate(
        [
            full.reshape(nz * rows_b, 2 * half),
            lax.dynamic_index_in_dim(fresh, 1 - c, 0, keepdims=False),
        ],
        axis=0,
    )
    swapped = shifted(swap, "c", 1)
    fresh = lax.dynamic_index_in_dim(fresh, c, 0, keepdims=False) + swapped[nz * rows_b :]
    twin = swapped[: nz * rows_b].reshape(nz, nx, 1, rows_v, 2 * half)
    full = full.reshape(nz, nx, 1, rows_v, 2 * half)
    both = jnp.where(
        c == 0, jnp.concatenate([full, twin], axis=2), jnp.concatenate([twin, full], axis=2)
    )
    whole = both.transpose(1, 0, 2, 3, 4).reshape(nx * nz * nc * rows_v, 2 * half)

    factor = (2 * half) ** (-0.5)
    total = dot_t(store, whole[:, :half])
    total = lax.dynamic_update_slice(total, dot_t(fresh, whole), (0, 0))
    rest = dot_t(received, whole[:, half:])
    row = lax.broadcasted_iota(jnp.int32, total.shape, 0)
    return ((total + jnp.where(row < examples, 0.0, rest)) * factor).astype(jnp.bfloat16)


def solution(mesh):
    fine = Mesh(mesh.devices.reshape(2, 4, 8, 2, 2), ("yl", "x", "z", "c", "yh"))
    return jax.shard_map(
        local,
        mesh=fine,
        in_specs=(
            P(DP, None, None),
            P(DP, None, None),
            P(),
            P(None, "yh"),
            P(DP, "yh"),
            P(DP, "yh"),
            P(),
        ),
        out_specs=P(DP, "yh"),
        check_vma=False,
    )
```

time: 579 us -> 211 us (0.36)
  waiting for transfers between devices: 533 us -> 102 us
  starting transfers between devices: 0.08 us -> 35.5 us
  local copies, waits for them, and re-layouts: 9.44 us -> 28.9 us
  between operations: 13.2 us -> 0.36 us
  other arithmetic: 3.84 us -> 14.6 us
  matrix products: 18.9 us -> 29.1 us
    all_gather x2 -> x0, waiting for transfers between devices: 427 us -> none  [the longest x1 221 us: local(): lax.all_gather(valid, 'dp', axis=0, tiled=True)]
    reduce_scatter x1 -> x0, waiting for transfers between devices: 105 us -> none  [local(): lax.psum_scatter(partial_scores, 'group', scatter_dimension=1, tiled=True)]
    ppermute x0 -> x15, waiting for transfers between devices: none -> 102 us  [shifted(): lax.ppermute(array, axis, [(i, (i + by) % size) for i in range(size)])]
    ppermute x0 -> x15, starting transfers between devices: none -> 35.5 us  [shifted(): lax.ppermute(array, axis, [(i, (i + by) % size) for i in range(size)])]
    dot_general x5 -> x7, matrix products: 18.9 us -> 29.1 us  [the longest x3 24.8 us: dot_t(): lax.dot_general(left, right, (((1,), (1,)), ((), ())), preferred_element_...]
    dynamic_update_slice x0 -> x11, local copies, waits for them, and re-layouts: none -> 9.5 us  [the longest x1 3.51 us: local(): total = lax.dynamic_update_slice(total, dot_t(fresh, whole), (0, 0))]
    transpose x0 -> x1, other arithmetic: none -> 8.19 us  [local(): both.transpose(1, 0, 2, 3, 4).reshape(nx * nz * nc * rows_v, 2 * half)]
    transpose x0 -> x1, local copies, waits for them, and re-layouts: none -> 7.74 us  [local(): both.transpose(1, 0, 2, 3, 4).reshape(nx * nz * nc * rows_v, 2 * half)]
  transfers between devices with their start and end apart: 3 -> 15, of which waited for: 3 -> 12; matrix products, arithmetic and copies ran while one was open for 1% -> 22% of each run, Pallas kernels for 0% -> 0%
where the time goes in v1:
time: 211 us; the launch traced here: 210 us
  waiting for transfers between devices  102 us (48%)
  starting transfers between devices  35.5 us (17%)
  matrix products  29.1 us (14%)
  local copies, waits for them, and re-layouts  28.9 us (14%)
  other arithmetic  14.6 us (7%)
    ppermute x15, waiting for transfers between devices, shifted(): lax.ppermute(array, axis, [(i, (i + by) % size) for i in range(size)])  102 us
    ppermute x15, starting transfers between devices, shifted(): lax.ppermute(array, axis, [(i, (i + by) % size) for i in range(size)])  35.5 us
    dot_general x3, matrix products, dot_t(): lax.dot_general(left, right, (((1,), (1,)), ((), ())), preferred_element_...  24.8 us
    transpose x1, other arithmetic, local(): both.transpose(1, 0, 2, 3, 4).reshape(nx * nz * nc * rows_v, 2 * half)  8.19 us
    transpose x1, local copies, waits for them, and re-layouts, local(): both.transpose(1, 0, 2, 3, 4).reshape(nx * nz * nc * rows_v, 2 * half)  7.74 us
    concatenate x1, other arithmetic, local(): jnp.concatenate([full.reshape(nz * rows_b, 2 * half), lax.dynamic_index_i...  4.68 us
  transfers between devices with their start and end apart: 15, of which 12 were waited for; matrix products, arithmetic and copies ran while one was open for 22% of the time, Pallas kernels for 0%

profile of v1, /device:TPU:1, one launch (start us, length us, event | category | flops | bytes accessed | tf_op | source)
XLA Modules:
  0.0 210.1 jit_solution(12618859416689273917)
XLA Ops:
  0.0 1.0 constant_dynamic-update-slice_fusion.1
  1.0 2.0 convolution_convert_fusion.1
  3.2 1.8 convolution_convert_fusion.2
  5.1 0.1 fusion.12
  5.4 3.8 %collective-permute-start = (bf16[18,2048]{1,0:T(8,128)(2,1)S(1)}, bf16[18,2048]{1,0:T(8,128)(2,1)S(1)}, u32[]{:S(2)}, u32[]{:S(2)}) collective-permute-start(bf16[18,2048]{1,0:T(8,128)(2,1)S(1)} %constant_dynamic-update-slice_fusion), channel_id=1, source_target_pairs={{0,1},{1,0},{2,3},{3,2},{4,5},{5,4},{6,7},{7,6},{8,9},{9,8},{10,11... | collective-permute-start | bytes 221192 | tf_op jit(solution)/shard_map/ppermute | solution.py:12
  9.6 1.6 collective-permute-done
  11.2 1.4 collective-permute-start.1
  12.7 3.1 %collective-permute-done.1 = bf16[18,4096]{1,0:T(8,128)(2,1)S(1)} collective-permute-done((bf16[18,4096]{1,0:T(8,128)(2,1)S(1)}, bf16[18,4096]{1,0:T(8,128)(2,1)S(1)}, u32[]{:S(2)}, u32[]{:S(2)}) %collective-permute-start.1) | collective-permute-done | bytes 147488 | tf_op jit(solution)/shard_map/ppermute | solution.py:12
  16.0 1.3 collective-permute-start.2
  17.3 2.5 %collective-permute-start.3 = (bf16[20,4096]{1,0:T(8,128)(2,1)S(1)}, bf16[20,4096]{1,0:T(8,128)(2,1)S(1)}, u32[]{:S(2)}, u32[]{:S(2)}) collective-permute-start(bf16[20,4096]{1,0:T(8,128)(2,1)S(1)} %pad_maximum_fusion.9), channel_id=1, source_target_pairs={{0,64},{32,96},{64,0},{96,32},{1,65},{33,97},{65,1},{97,33},{2,66}... | collective-permute-start | bytes 491528 | tf_op jit(solution)/shard_map/ppermute | solution.py:12
  19.8 1.1 collective-permute-start.4
  21.1 0.7 gather_fusion
  21.8 3.9 %collective-permute-done.3 = bf16[20,4096]{1,0:T(8,128)(2,1)S(1)} collective-permute-done((bf16[20,4096]{1,0:T(8,128)(2,1)S(1)}, bf16[20,4096]{1,0:T(8,128)(2,1)S(1)}, u32[]{:S(2)}, u32[]{:S(2)}) %collective-permute-start.3) | collective-permute-done | bytes 163872 | tf_op jit(solution)/shard_map/ppermute | solution.py:12
  25.8 0.3 convolution_convert_fusion
  26.5 1.7 collective-permute-start.5
  28.2 4.1 %collective-permute-start.6 = (bf16[68,4096]{1,0:T(8,128)(2,1)S(1)}, bf16[68,4096]{1,0:T(8,128)(2,1)S(1)}, u32[]{:S(2)}, u32[]{:S(2)}) collective-permute-start(bf16[68,4096]{1,0:T(8,128)(2,1)S(1)} %get-tuple-element.8), channel_id=1, source_target_pairs={{0,28},{4,0},{8,4},{12,8},{16,12},{20,16},{24,20},{28,24},{1,29},{... | collective-permute-start | bytes 1671176 | tf_op jit(solution)/shard_map/ppermute | solution.py:12
  32.3 2.5 %broadcast_in_dim.52 = bf16[8,64,4096]{2,1,0:T(8,128)(2,1)} broadcast(bf16[]{:T(256)} %constant.162.clone.1), dimensions={} | broadcast | bytes 4194306 | tf_op jit(solution)/shard_map/broadcast_in_dim | solution.py:83
  34.8 0.9 bitcast_dynamic-update-slice_fusion.4
  35.7 5.9 %collective-permute-done.5 = bf16[68,4096]{1,0:T(8,128)(2,1)S(1)} collective-permute-done((bf16[68,4096]{1,0:T(8,128)(2,1)S(1)}, bf16[68,4096]{1,0:T(8,128)(2,1)S(1)}, u32[]{:S(2)}, u32[]{:S(2)}) %collective-permute-start.5) | collective-permute-done | bytes 557088 | tf_op jit(solution)/shard_map/ppermute | solution.py:12
  41.8 0.9 bitcast_dynamic-update-slice_fusion.3
  42.7 0.8 bitcast_dynamic-update-slice_fusion.2
  43.5 9.8 %collective-permute-done.7 = bf16[68,4096]{1,0:T(8,128)(2,1)S(1)} collective-permute-done((bf16[68,4096]{1,0:T(8,128)(2,1)S(1)}, bf16[68,4096]{1,0:T(8,128)(2,1)S(1)}, u32[]{:S(2)}, u32[]{:S(2)}) %collective-permute-start.7) | collective-permute-done | bytes 557088 | tf_op jit(solution)/shard_map/ppermute | solution.py:12
  53.4 1.3 collective-permute-start.8
  54.8 0.4 collective-permute-start.9
  55.1 0.8 bitcast_dynamic-update-slice_fusion.1
  56.0 6.7 %collective-permute-done.8 = bf16[68,4096]{1,0:T(8,128)(2,1)S(1)} collective-permute-done((bf16[68,4096]{1,0:T(8,128)(2,1)S(1)}, bf16[68,4096]{1,0:T(8,128)(2,1)S(1)}, u32[]{:S(2)}, u32[]{:S(2)}) %collective-permute-start.8) | collective-permute-done | bytes 557088 | tf_op jit(solution)/shard_map/ppermute | solution.py:12
  62.7 2.1 %collective-permute-done.9 = bf16[68,4096]{1,0:T(8,128)(2,1)S(1)} collective-permute-done((bf16[68,4096]{1,0:T(8,128)(2,1)S(1)}, bf16[68,4096]{1,0:T(8,128)(2,1)S(1)}, u32[]{:S(2)}, u32[]{:S(2)}) %collective-permute-start.9) | collective-permute-done | bytes 557088 | tf_op jit(solution)/shard_map/ppermute | solution.py:12
  64.9 1.8 collective-permute-start.10
  66.8 0.8 bitcast_dynamic-update-slice_fusion
  67.7 0.8 fusion.14
  68.5 8.3 %collective-permute-done.11 = bf16[36,4096]{1,0:T(8,128)(2,1)S(1)} collective-permute-done((bf16[36,4096]{1,0:T(8,128)(2,1)S(1)}, bf16[36,4096]{1,0:T(8,128)(2,1)S(1)}, u32[]{:S(2)}, u32[]{:S(2)}) %collective-permute-start.11) | collective-permute-done | bytes 294944 | tf_op jit(solution)/shard_map/ppermute | solution.py:12
  76.8 2.6 %collective-permute-start.12 = (bf16[32,4096]{1,0:T(8,128)(2,1)S(1)}, bf16[32,4096]{1,0:T(8,128)(2,1)S(1)}, u32[]{:S(2)}, u32[]{:S(2)}) collective-permute-start(bf16[32,4096]{1,0:T(8,128)(2,1)S(1)} %slice.151), channel_id=1, source_target_pairs={{0,28},{4,0},{8,4},{12,8},{16,12},{20,16},{24,20},{28,24},{1,29},{... | collective-permute-start | bytes 786440 | tf_op jit(solution)/shard_map/ppermute | solution.py:12
  79.5 0.9 fusion.13
  80.3 5.3 %collective-permute-done.12 = bf16[32,4096]{1,0:T(8,128)(2,1)S(1)} collective-permute-done((bf16[32,4096]{1,0:T(8,128)(2,1)S(1)}, bf16[32,4096]{1,0:T(8,128)(2,1)S(1)}, u32[]{:S(2)}, u32[]{:S(2)}) %collective-permute-start.12) | collective-permute-done | bytes 262176 | tf_op jit(solution)/shard_map/ppermute | solution.py:12
  85.6 0.8 fusion.15
  86.4 4.7 %pad_maximum_fusion = bf16[514,4096]{1,0:T(8,128)(2,1)} fusion(bf16[2,4096]{1,0:T(2,128)(2,1)S(1)} %dynamic-slice_bitcast_fusion.2, bf16[512,4096]{1,0:T(8,128)(2,1)} %bitcast.25), kind=kLoop, calls=%fused_computation.4 | loop fusion | flops 8421376 | bytes 8421376 | tf_op jit(solution)/shard_map/concatenate | solution.py:100
  91.1 10.4 %collective-permute-start.13 = (bf16[514,4096]{1,0:T(8,128)(2,1)}, bf16[514,4096]{1,0:T(8,128)(2,1)}, u32[]{:S(2)}, u32[]{:S(2)}) collective-permute-start(bf16[514,4096]{1,0:T(8,128)(2,1)} %pad_maximum_fusion), channel_id=1, source_target_pairs={{0,2},{2,0},{1,3},{3,1},{4,6},{6,4},{5,7},{7,5},{8,10},{10,8},{9,1... | collective-permute-start | bytes 12632072 | tf_op jit(solution)/shard_map/ppermute | solution.py:12
  101.5 2.9 %collective-permute-start.14 = (bf16[1024,2048]{1,0:T(8,128)(2,1)}, bf16[1024,2048]{1,0:T(8,128)(2,1)}, u32[]{:S(2)}, u32[]{:S(2)}) collective-permute-start(bf16[1024,2048]{1,0:T(8,128)(2,1)} %param.11), channel_id=1, source_target_pairs={{0,1},{1,0},{2,3},{3,2},{4,5},{5,4},{6,7},{7,6},{8,9},{9,8},{10,11... | collective-permute-start | bytes 12582920 | tf_op jit(solution)/shard_map/ppermute | solution.py:12
  104.4 4.3 %collective-permute-done.13 = bf16[514,4096]{1,0:T(8,128)(2,1)} collective-permute-done((bf16[514,4096]{1,0:T(8,128)(2,1)}, bf16[514,4096]{1,0:T(8,128)(2,1)}, u32[]{:S(2)}, u32[]{:S(2)}) %collective-permute-start.13) | collective-permute-done | bytes 4210720 | tf_op jit(solution)/shard_map/ppermute | solution.py:12
  108.7 2.5 %slice.154 = bf16[512,4096]{1,0:T(8,128)(2,1)S(1)} slice(bf16[514,4096]{1,0:T(8,128)(2,1)} %collective-permute-done.13), slice={[0:512], [0:4096]} | slice | bytes 8388608 | tf_op jit(solution)/shard_map/slice | solution.py:109
  111.2 8.2 %fusion = bf16[4,8,2,16,4096]{4,3,0,1,2:T(8,128)(2,1)} fusion(bf16[8,4,1,16,4096]{4,3,1,0,2:T(8,128)(2,1)S(1)} %bitcast.92, bf16[8,4,1,16,4096]{4,3,1,0,2:T(8,128)(2,1)} %bitcast.24, pred[]{:T(512)S(6)} %eq.43), kind=kLoop, calls=%fused_computation.2 | loop fusion | flops 12582912 | bytes 16777216 | tf_op jit(solution)/shard_map/transpose | solution.py:114
  119.4 7.7 %copy.18 = bf16[4,8,2,16,4096]{4,3,2,1,0:T(8,128)(2,1)} copy(bf16[4,8,2,16,4096]{4,3,0,1,2:T(8,128)(2,1)} %fusion) | data formatting | bytes 16777216 | tf_op jit(solution)/shard_map/transpose | solution.py:114
  127.1 5.9 %fusion.23 = f32[2,1024]{0,1:T(8,128)S(1)} fusion(bf16[1024,4096]{1,0:T(8,128)(2,1)} %bitcast.93, bf16[514,4096]{1,0:T(8,128)(2,1)} %collective-permute-done.13, bf16[2,2,4096]{2,1,0:T(2,128)(2,1)S(1)} %reshape.191, s32[]{:T(128)S(6)} %select_n.211), kind=kOutput, calls=%fused_computation.61 | convolution fusion | flops 16809984 | bytes 8429572 | tf_op jit(solution)/shard_map/dot_general | solution.py:16
  133.0 8.3 %fusion.7 = f32[1024,1024]{0,1:T(8,128)} fusion(bf16[1024,2048]{1,0:T(8,128)(2,1)} %param.11, bf16[1024,4096]{1,0:T(8,128)(2,1)S(1)} %bitcast.95), kind=kOutput, calls=%fused_computation.12 | convolution fusion | flops 4294967296 | bytes 12582912 | tf_op jit(solution)/shard_map/dot_general | solution.py:16
  141.3 3.5 %dynamic_update_slice.51 = f32[1024,1024]{0,1:T(8,128)} dynamic-update-slice(f32[1024,1024]{0,1:T(8,128)} %fusion.7, f32[2,1024]{0,1:T(8,128)S(1)} %fusion.23, s32[]{:T(128)} %constant.161.clone.1, s32[]{:T(128)} %constant.161.clone.1) | dynamic-update-slice | bytes 16388 | tf_op jit(solution)/shard_map/dynamic_update_slice | solution.py:118
  144.8 50.7 %collective-permute-done.14 = bf16[1024,2048]{1,0:T(8,128)(2,1)} collective-permute-done((bf16[1024,2048]{1,0:T(8,128)(2,1)}, bf16[1024,2048]{1,0:T(8,128)(2,1)}, u32[]{:S(2)}, u32[]{:S(2)}) %collective-permute-start.14) | collective-permute-done | bytes 4194336 | tf_op jit(solution)/shard_map/ppermute | solution.py:12
  195.5 10.6 %fusion.6 = bf16[1024,1024]{0,1:T(8,128)(2,1)} fusion(f32[1024,1024]{0,1:T(8,128)} %dynamic_update_slice.51, pred[1024]{0:T(1024)(128)(4,1)S(1)} %iota_compare_fusion, bf16[1024,2048]{1,0:T(8,128)(2,1)} %collective-permute-done.14, bf16[1024,4096]{1,0:T(8,128)(2,1)} %bitcast.94), kind=kOutput, calls=%fused_computation.11 | convolution fusion | flops 4299161600 | bytes 14681088 | tf_op jit(solution)/shard_map/dot_general | solution.py:16
  206.2 3.9 %copy.20 = bf16[1024,1024]{1,0:T(8,128)(2,1)} copy(bf16[1024,1024]{0,1:T(8,128)(2,1)} %fusion.6) | data formatting | bytes 4194304 | tf_op jit(solution)/shard_map/convert_element_type | solution.py:121
  (64 shorter events, 2.3 us)
Async XLA Ops:
  0.0 3.2 %copy-start = (bf16[2,64,8192]{2,1,0:T(8,128)(2,1)S(1)}, bf16[2,64,8192]{2,1,0:T(8,128)(2,1)}, u32[]{:S(2)}) copy-start(bf16[2,64,8192]{2,1,0:T(8,128)(2,1)} %param.8) | copy-start | bytes 6291460
  0.0 21.1 %copy-start.2 = (s32[256]{0:T(256)S(1)}, s32[256]{0:T(256)}, u32[]{:S(2)}) copy-start(s32[256]{0:T(256)} %param.13) | copy-start | bytes 3076
  5.4 5.8 %collective-permute-start = (bf16[18,2048]{1,0:T(8,128)(2,1)S(1)}, bf16[18,2048]{1,0:T(8,128)(2,1)S(1)}, u32[]{:S(2)}, u32[]{:S(2)}) collective-permute-start(bf16[18,2048]{1,0:T(8,128)(2,1)S(1)} %constant_dynamic-update-slice_fusion), channel_id=1, source_target_pairs={{0,1},{1,0},{2,3},{3,2},{4,5},{5,4},{6,7},{7,6},{8,9},{9,8},{10,11... | collective-permute-start | bytes 221192 | tf_op jit(solution)/shard_map/ppermute | solution.py:12
  11.2 4.6 %collective-permute-start.1 = (bf16[18,4096]{1,0:T(8,128)(2,1)S(1)}, bf16[18,4096]{1,0:T(8,128)(2,1)S(1)}, u32[]{:S(2)}, u32[]{:S(2)}) collective-permute-start(bf16[18,4096]{1,0:T(8,128)(2,1)S(1)} %pad_maximum_fusion.8), channel_id=1, source_target_pairs={{0,128},{128,0},{1,129},{129,1},{2,130},{130,2},{3,131},{131,3},{4... | collective-permute-start | bytes 442376 | tf_op jit(solution)/shard_map/ppermute | solution.py:12
  16.0 5.8 %collective-permute-start.2 = (bf16[20,4096]{1,0:T(8,128)(2,1)S(1)}, bf16[20,4096]{1,0:T(8,128)(2,1)S(1)}, u32[]{:S(2)}, u32[]{:S(2)}) collective-permute-start(bf16[20,4096]{1,0:T(8,128)(2,1)S(1)} %pad_maximum_fusion.9), channel_id=1, source_target_pairs={{0,32},{32,64},{64,96},{96,0},{1,33},{33,65},{65,97},{97,1},{2,34}... | collective-permute-start | bytes 491528 | tf_op jit(solution)/shard_map/ppermute | solution.py:12
  17.3 8.3 %collective-permute-start.3 = (bf16[20,4096]{1,0:T(8,128)(2,1)S(1)}, bf16[20,4096]{1,0:T(8,128)(2,1)S(1)}, u32[]{:S(2)}, u32[]{:S(2)}) collective-permute-start(bf16[20,4096]{1,0:T(8,128)(2,1)S(1)} %pad_maximum_fusion.9), channel_id=1, source_target_pairs={{0,64},{32,96},{64,0},{96,32},{1,65},{33,97},{65,1},{97,33},{2,66}... | collective-permute-start | bytes 491528 | tf_op jit(solution)/shard_map/ppermute | solution.py:12
  19.8 5.9 %collective-permute-start.4 = (bf16[20,4096]{1,0:T(8,128)(2,1)S(1)}, bf16[20,4096]{1,0:T(8,128)(2,1)S(1)}, u32[]{:S(2)}, u32[]{:S(2)}) collective-permute-start(bf16[20,4096]{1,0:T(8,128)(2,1)S(1)} %pad_maximum_fusion.9), channel_id=1, source_target_pairs={{0,96},{32,0},{64,32},{96,64},{1,97},{33,1},{65,33},{97,65},{2,98}... | collective-permute-start | bytes 491528 | tf_op jit(solution)/shard_map/ppermute | solution.py:12
  26.5 15.1 %collective-permute-start.5 = (bf16[68,4096]{1,0:T(8,128)(2,1)S(1)}, bf16[68,4096]{1,0:T(8,128)(2,1)S(1)}, u32[]{:S(2)}, u32[]{:S(2)}) collective-permute-start(bf16[68,4096]{1,0:T(8,128)(2,1)S(1)} %get-tuple-element.7), channel_id=1, source_target_pairs={{0,4},{4,8},{8,12},{12,16},{16,20},{20,24},{24,28},{28,0},{1,5},{5... | collective-permute-start | bytes 1671176 | tf_op jit(solution)/shard_map/ppermute | solution.py:12
  28.2 13.6 %collective-permute-start.6 = (bf16[68,4096]{1,0:T(8,128)(2,1)S(1)}, bf16[68,4096]{1,0:T(8,128)(2,1)S(1)}, u32[]{:S(2)}, u32[]{:S(2)}) collective-permute-start(bf16[68,4096]{1,0:T(8,128)(2,1)S(1)} %get-tuple-element.8), channel_id=1, source_target_pairs={{0,28},{4,0},{8,4},{12,8},{16,12},{20,16},{24,20},{28,24},{1,29},{... | collective-permute-start | bytes 1671176 | tf_op jit(solution)/shard_map/ppermute | solution.py:12
  41.7 11.7 %collective-permute-start.7 = (bf16[68,4096]{1,0:T(8,128)(2,1)S(1)}, bf16[68,4096]{1,0:T(8,128)(2,1)S(1)}, u32[]{:S(2)}, u32[]{:S(2)}) collective-permute-start(bf16[68,4096]{1,0:T(8,128)(2,1)S(1)} %pad_maximum_fusion.3), channel_id=1, source_target_pairs={{0,4},{4,8},{8,12},{12,16},{16,20},{20,24},{24,28},{28,0},{1,5},{5... | collective-permute-start | bytes 1671176 | tf_op jit(solution)/shard_map/ppermute | solution.py:12
  53.4 9.2 %collective-permute-start.8 = (bf16[68,4096]{1,0:T(8,128)(2,1)S(1)}, bf16[68,4096]{1,0:T(8,128)(2,1)S(1)}, u32[]{:S(2)}, u32[]{:S(2)}) collective-permute-start(bf16[68,4096]{1,0:T(8,128)(2,1)S(1)} %pad_maximum_fusion.4), channel_id=1, source_target_pairs={{0,28},{4,0},{8,4},{12,8},{16,12},{20,16},{24,20},{28,24},{1,29},{... | collective-permute-start | bytes 1671176 | tf_op jit(solution)/shard_map/ppermute | solution.py:12
  54.8 10.0 %collective-permute-start.9 = (bf16[68,4096]{1,0:T(8,128)(2,1)S(1)}, bf16[68,4096]{1,0:T(8,128)(2,1)S(1)}, u32[]{:S(2)}, u32[]{:S(2)}) collective-permute-start(bf16[68,4096]{1,0:T(8,128)(2,1)S(1)} %pad_maximum_fusion.5), channel_id=1, source_target_pairs={{0,4},{4,8},{8,12},{12,16},{16,20},{20,24},{24,28},{28,0},{1,5},{5... | collective-permute-start | bytes 1671176 | tf_op jit(solution)/shard_map/ppermute | solution.py:12
  64.9 11.9 %collective-permute-start.10 = (bf16[68,4096]{1,0:T(8,128)(2,1)S(1)}, bf16[68,4096]{1,0:T(8,128)(2,1)S(1)}, u32[]{:S(2)}, u32[]{:S(2)}) collective-permute-start(bf16[68,4096]{1,0:T(8,128)(2,1)S(1)} %pad_maximum_fusion.6), channel_id=1, source_target_pairs={{0,28},{4,0},{8,4},{12,8},{16,12},{20,16},{24,20},{28,24},{1,29},{... | collective-permute-start | bytes 1671176 | tf_op jit(solution)/shard_map/ppermute | solution.py:12
  66.7 10.0 %collective-permute-start.11 = (bf16[36,4096]{1,0:T(8,128)(2,1)S(1)}, bf16[36,4096]{1,0:T(8,128)(2,1)S(1)}, u32[]{:S(2)}, u32[]{:S(2)}) collective-permute-start(bf16[36,4096]{1,0:T(8,128)(2,1)S(1)} %pad_maximum_fusion.7), channel_id=1, source_target_pairs={{0,4},{4,8},{8,12},{12,16},{16,20},{20,24},{24,28},{28,0},{1,5},{5... | collective-permute-start | bytes 884744 | tf_op jit(solution)/shard_map/ppermute | solution.py:12
  76.8 8.8 %collective-permute-start.12 = (bf16[32,4096]{1,0:T(8,128)(2,1)S(1)}, bf16[32,4096]{1,0:T(8,128)(2,1)S(1)}, u32[]{:S(2)}, u32[]{:S(2)}) collective-permute-start(bf16[32,4096]{1,0:T(8,128)(2,1)S(1)} %slice.151), channel_id=1, source_target_pairs={{0,28},{4,0},{8,4},{12,8},{16,12},{20,16},{24,20},{28,24},{1,29},{... | collective-permute-start | bytes 786440 | tf_op jit(solution)/shard_map/ppermute | solution.py:12
  91.1 17.6 %collective-permute-start.13 = (bf16[514,4096]{1,0:T(8,128)(2,1)}, bf16[514,4096]{1,0:T(8,128)(2,1)}, u32[]{:S(2)}, u32[]{:S(2)}) collective-permute-start(bf16[514,4096]{1,0:T(8,128)(2,1)} %pad_maximum_fusion), channel_id=1, source_target_pairs={{0,2},{2,0},{1,3},{3,1},{4,6},{6,4},{5,7},{7,5},{8,10},{10,8},{9,1... | collective-permute-start | bytes 12632072 | tf_op jit(solution)/shard_map/ppermute | solution.py:12
  101.5 94.0 %collective-permute-start.14 = (bf16[1024,2048]{1,0:T(8,128)(2,1)}, bf16[1024,2048]{1,0:T(8,128)(2,1)}, u32[]{:S(2)}, u32[]{:S(2)}) collective-permute-start(bf16[1024,2048]{1,0:T(8,128)(2,1)} %param.11), channel_id=1, source_target_pairs={{0,1},{1,0},{2,3},{3,2},{4,5},{5,4},{6,7},{7,6},{8,9},{9,8},{10,11... | collective-permute-start | bytes 12582920 | tf_op jit(solution)/shard_map/ppermute | solution.py:12
  127.1 5.9 %copy-start.3 = (bf16[4,8,2,16,4096]{4,3,2,1,0:T(8,128)(2,1)S(1)}, bf16[4,8,2,16,4096]{4,3,2,1,0:T(8,128)(2,1)}, u32[]{:S(2)}) copy-start(bf16[4,8,2,16,4096]{4,3,2,1,0:T(8,128)(2,1)} %copy.18) | copy-start | bytes 25165828
  195.5 14.6 %copy-start.1 = (bf16[2,64,8192]{2,1,0:T(8,128)(2,1)S(1)}, bf16[2,64,8192]{2,1,0:T(8,128)(2,1)}, u32[]{:S(2)}) copy-start(bf16[2,64,8192]{2,1,0:T(8,128)(2,1)} %param.8) | copy-start | bytes 6291460

commit v2 on v0

v2 whole, which is shorter than its diff:
```python
import functools

import jax
import jax.numpy as jnp
from jax import lax
from jax.experimental import pallas as pl
from jax.experimental.pallas import tpu as pltpu
from jax.sharding import Mesh, PartitionSpec as P

DP = ("yl", "x", "z", "c")
SIZES = {"yl": 2, "x": 4, "z": 8, "c": 2, "yh": 2}
SCALE_ROWS = 16
BLOCK = 256
TINY = 1e-37


def shifted(array, axis, by):
    size = SIZES[axis]
    return lax.ppermute(array, axis, [(i, (i + by) % size) for i in range(size)])


def paired(array, axis, bit):
    size = SIZES[axis]
    return lax.ppermute(array, axis, [(i, i ^ bit) for i in range(size)])


def dot_t(left, right):
    return lax.dot_general(
        left, right, (((1,), (1,)), ((), ())), preferred_element_type=jnp.float32
    )


def make_sketch(inputs, out_grads, proj_in, proj_out):
    examples, length, width_in = inputs.shape
    width_out = out_grads.shape[2]
    lin = jnp.dot(
        inputs.reshape(examples * length, width_in), proj_in, preferred_element_type=jnp.float32
    ).astype(jnp.bfloat16)
    lout = jnp.dot(
        out_grads.reshape(examples * length, width_out),
        proj_out,
        preferred_element_type=jnp.float32,
    ).astype(jnp.bfloat16)
    lin = lin.reshape(examples, length, -1)
    lout = lout.reshape(examples, length, -1)
    sketch = jnp.einsum("nso,nsi->noi", lout, lin, preferred_element_type=jnp.float32) * length ** (
        -0.5
    )
    return sketch.reshape(examples, -1).astype(jnp.bfloat16)


def partial_kernel(own_ref, twin_ref, store_ref, out_ref):
    n = own_ref.shape[0]
    store = store_ref[...]
    a = dot_t(own_ref[...], store)
    b = dot_t(twin_ref[...], store)
    top = jnp.maximum(
        jnp.max(jnp.abs(a), axis=0, keepdims=True), jnp.max(jnp.abs(b), axis=0, keepdims=True)
    )
    power = jnp.ceil(jnp.log2(jnp.maximum(top, TINY)))
    scale = jnp.exp2(-power)
    out_ref[:n] = a * scale
    out_ref[n : 2 * n] = b * scale
    out_ref[2 * n :] = jnp.broadcast_to(power, (SCALE_ROWS, power.shape[1]))


def partial_scores(own, twin, store):
    n, width = own.shape
    rows = store.shape[0]
    return pl.pallas_call(
        partial_kernel,
        grid=(rows // BLOCK,),
        in_specs=[
            pl.BlockSpec((n, width), lambda i: (0, 0)),
            pl.BlockSpec((n, width), lambda i: (0, 0)),
            pl.BlockSpec((BLOCK, width), lambda i: (i, 0)),
        ],
        out_specs=pl.BlockSpec((2 * n + SCALE_ROWS, BLOCK), lambda i: (0, i)),
        out_shape=jax.ShapeDtypeStruct((2 * n + SCALE_ROWS, rows), jnp.float32),
        compiler_params=pltpu.CompilerParams(vmem_limit_bytes=32 * 1024 * 1024),
        cost_estimate=pl.CostEstimate(
            flops=4 * n * width * rows, bytes_accessed=8 * rows * width, transcendentals=0
        ),
    )(own, twin, store)


def own_kernel(store_ref, valid_ref, out_ref):
    out_ref[...] = dot_t(store_ref[...], valid_ref[...])


def own_scores(store, valid):
    rows, width = store.shape
    columns = valid.shape[0]
    return pl.pallas_call(
        own_kernel,
        grid=(rows // BLOCK,),
        in_specs=[
            pl.BlockSpec((BLOCK, width), lambda i: (i, 0)),
            pl.BlockSpec((columns, width), lambda i: (0, 0)),
        ],
        out_specs=pl.BlockSpec((BLOCK, columns), lambda i: (i, 0)),
        out_shape=jax.ShapeDtypeStruct((rows, columns), jnp.float32),
        compiler_params=pltpu.CompilerParams(vmem_limit_bytes=32 * 1024 * 1024),
        cost_estimate=pl.CostEstimate(
            flops=2 * rows * width * columns,
            bytes_accessed=2 * (rows + columns) * width + 4 * rows * columns,
            transcendentals=0,
        ),
    )(store, valid)


def finish_kernel(factor, examples, own_ref, received_ref, fresh_ref, out_ref):
    out_ref[...] = ((own_ref[...] + received_ref[...].T) * factor).astype(out_ref.dtype)

    @pl.when(pl.program_id(0) == 0)
    def _():
        n = fresh_ref.shape[0]
        row = lax.broadcasted_iota(jnp.int32, fresh_ref.shape, 0)
        kept = own_ref[:n] + received_ref[:, :128].T[:n]
        value = jnp.where(row < examples, fresh_ref[...], kept)
        out_ref[:n] = (value * factor).astype(out_ref.dtype)


def finish(own, received, fresh, factor, examples):
    rows, columns = own.shape
    return pl.pallas_call(
        functools.partial(finish_kernel, factor, examples),
        grid=(rows // BLOCK,),
        in_specs=[
            pl.BlockSpec((BLOCK, columns), lambda i: (i, 0)),
            pl.BlockSpec((columns, BLOCK), lambda i: (0, i)),
            pl.BlockSpec(fresh.shape, lambda i: (0, 0)),
        ],
        out_specs=pl.BlockSpec((BLOCK, columns), lambda i: (i, 0)),
        out_shape=jax.ShapeDtypeStruct((rows, columns), jnp.bfloat16),
        compiler_params=pltpu.CompilerParams(vmem_limit_bytes=32 * 1024 * 1024),
        cost_estimate=pl.CostEstimate(
            flops=rows * columns, bytes_accessed=10 * rows * columns, transcendentals=0
        ),
    )(own, received, fresh)


def local(inputs, out_grads, proj_in, proj_out, store, valid, owner):
    yl, x, z, c, yh = (lax.axis_index(a) for a in ("yl", "x", "z", "c", "yh"))
    nx, nz, nc = SIZES["x"], SIZES["z"], SIZES["c"]
    examples = inputs.shape[0]
    rows_v, half = valid.shape
    rows_b = nx * rows_v

    valid_other = shifted(valid, "yl", 1)
    v_out = jnp.where(yl == yh, valid_other, valid)
    v_own = jnp.where(yl == yh, valid, valid_other)

    known = make_sketch(inputs, out_grads, proj_in, proj_out)
    known = jnp.concatenate([known, paired(known, "yl", 1)], axis=0)
    known = jnp.concatenate([known, paired(known, "x", 1)], axis=0)
    known = jnp.concatenate([known, paired(known, "x", 2)], axis=0)

    first = jnp.stack([v_out, v_own])
    pieces = [first] + [shifted(first, "x", k) for k in range(1, nx)]
    block = jnp.zeros((2, nx, rows_v, half), valid.dtype)
    for k, piece in enumerate(pieces):
        block = lax.dynamic_update_slice(block, piece[:, None], (0, (x - k) % nx, 0, 0))
    a0, b0 = block[0].reshape(rows_b, half), block[1].reshape(rows_b, half)

    def dp_index(yl_, x_, z_, c_):
        return ((yl_ * nx + x_) * nz + z_) * nc + c_

    each = jnp.arange(examples, dtype=jnp.int32)
    from_x = x ^ jnp.arange(nx, dtype=jnp.int32)
    from_yl = yl ^ jnp.arange(2, dtype=jnp.int32)
    example = dp_index(from_yl[None, :, None], from_x[:, None, None], z, c) * examples + each
    slot_of = owner[example.reshape(-1)]
    to = dp_index(yl, x, jnp.arange(nz, dtype=jnp.int32)[:, None], jnp.arange(nc, dtype=jnp.int32))
    slot = (to[:, :, None] * examples + each).reshape(-1)
    picker = (slot[:, None] == slot_of[None, :]).astype(jnp.bfloat16)
    shares = jnp.dot(picker, known, preferred_element_type=jnp.float32).astype(jnp.bfloat16)
    shares = shares.reshape(nz, nc * examples, half)

    def share(offset):
        return lax.dynamic_index_in_dim(shares, (z + offset) % nz, 0, keepdims=False)

    full = {
        "out": jnp.zeros((nx, nz, nc, rows_v, half), valid.dtype),
        "own": jnp.zeros((nx, nz, nc, rows_v, half), valid.dtype),
    }

    def fill(name, piece, z_from, c_from):
        full[name] = lax.dynamic_update_slice(
            full[name], piece.reshape(nx, 1, 1, rows_v, half), (0, z_from % nz, c_from, 0, 0)
        )

    received = [jnp.zeros((nx, nz, nc, rows_v, store.shape[0]), jnp.float32)]

    def swap(outs, owns, extra=None):
        blocks = [b for b, _ in outs] + [b for b, _ in owns]
        sent = blocks if extra is None else blocks + [extra]
        got = shifted(jnp.concatenate(sent, axis=0), "c", 1)
        for name, items, base in (("out", outs, 0), ("own", owns, len(outs))):
            for j, (b, z_from) in enumerate(items):
                fill(name, b, z_from, c)
                at = (base + j) * rows_b
                fill(name, got[at : at + rows_b], z_from, 1 - c)
        if outs:
            mine = jnp.concatenate([b for b, _ in outs], axis=0)
            n = mine.shape[0]
            part = partial_scores(mine, got[:n], store).astype(jnp.float16)
            part = shifted(part, "yh", 1).astype(jnp.float32)
            part = part[: 2 * n] * jnp.exp2(part[2 * n : 2 * n + 1])
            for side, c_from in ((0, c), (1, 1 - c)):
                for j, (_, z_from) in enumerate(outs):
                    at = side * n + j * rows_b
                    piece = part[at : at + rows_b].reshape(nx, 1, 1, rows_v, -1)
                    received[0] = lax.dynamic_update_slice(
                        received[0], piece, (0, z_from % nz, c_from, 0, 0)
                    )
        return got[len(blocks) * rows_b :]

    def both_ways(ahead, back):
        return (
            shifted(jnp.concatenate(ahead, axis=0), "z", 1),
            shifted(jnp.concatenate(back, axis=0), "z", -1),
        )

    cut = rows_b // 2
    swap([(a0, z)], [])
    up, down = both_ways([a0], [a0])
    a_up, a_down = up, down
    swap([(a_up, z - 1), (a_down, z + 1)], [(b0, z)])

    up, down = both_ways([a_up, b0, share(4)], [a_down, b0, share(-3)])
    a_up, b_up, s_up = up[:rows_b], up[rows_b : 2 * rows_b], up[2 * rows_b :] + share(3)
    a_down, b_down, s_down = (
        down[:rows_b],
        down[rows_b : 2 * rows_b],
        down[2 * rows_b :] + share(-2),
    )
    swap([(a_up, z - 2), (a_down, z + 2)], [(b_up, z - 1), (b_down, z + 1)])

    up, down = both_ways([a_up, b_up, s_up], [a_down, b_down, s_down])
    a_up, b_up, s_up = up[:rows_b], up[rows_b : 2 * rows_b], up[2 * rows_b :] + share(2)
    a_down, b_down, s_down = (
        down[:rows_b],
        down[rows_b : 2 * rows_b],
        down[2 * rows_b :] + share(-1),
    )
    swap([(a_up, z - 3), (a_down, z + 3)], [(b_up, z - 2), (b_down, z + 2)])

    up, down = both_ways([a_up[:cut], b_up, s_up], [a_down[cut:], b_down, s_down])
    a_far = jnp.concatenate([up[:cut], down[:cut]], axis=0)
    b_up, s_up = up[cut : cut + rows_b], up[cut + rows_b :] + share(1)
    b_down, s_down = down[cut : cut + rows_b], down[cut + rows_b :] + share(0)
    swap([(a_far, z - 4)], [(b_up, z - 3), (b_down, z + 3)])

    up, down = both_ways([b_up[:cut], s_up], [b_down[cut:]])
    b_far = jnp.concatenate([up[:cut], down], axis=0)
    fresh = (up[cut:] + s_down).reshape(nc, examples, half)
    got = swap([], [(b_far, z - 4)], lax.dynamic_index_in_dim(fresh, 1 - c, 0, keepdims=False))
    fresh = lax.dynamic_index_in_dim(fresh, c, 0, keepdims=False) + got

    fresh = jnp.pad(fresh, ((0, 16 - examples), (0, 0)))
    whole_out = full["out"].reshape(nx * nz * nc * rows_v, half)
    whole_own = full["own"].reshape(nx * nz * nc * rows_v, half)
    fresh_scores = dot_t(fresh, whole_own) + shifted(dot_t(fresh, whole_out), "yh", 1)

    own = own_scores(store, whole_own)
    partner = received[0].reshape(nx * nz * nc * rows_v, store.shape[0])
    return finish(own, partner, fresh_scores, (2 * half) ** (-0.5), examples)


def solution(mesh):
    fine = Mesh(mesh.devices.reshape(2, 4, 8, 2, 2), ("yl", "x", "z", "c", "yh"))
    return jax.shard_map(
        local,
        mesh=fine,
        in_specs=(
            P(DP, None, None),
            P(DP, None, None),
            P(),
            P(None, "yh"),
            P(DP, "yh"),
            P(DP, "yh"),
            P(),
        ),
        out_specs=P(DP, "yh"),
        check_vma=False,
    )
```

time: 579 us -> 153 us (0.26)
  waiting for transfers between devices: 533 us -> 55.7 us
  starting transfers between devices: 0.08 us -> 49 us
  Pallas kernels: 0 us -> 25.4 us
  matrix products: 18.9 us -> 6.61 us
  between operations: 13.2 us -> 1.33 us
    all_gather x2 -> x0, waiting for transfers between devices: 427 us -> none  [the longest x1 221 us: local(): lax.all_gather(valid, 'dp', axis=0, tiled=True)]
    reduce_scatter x1 -> x0, waiting for transfers between devices: 105 us -> none  [local(): lax.psum_scatter(partial_scores, 'group', scatter_dimension=1, tiled=True)]
    ppermute x0 -> x29, waiting for transfers between devices: none -> 55.7 us  [the longest x26 51.7 us: shifted(): lax.ppermute(array, axis, [(i, (i + by) % size) for i in range(size)])]
    ppermute x0 -> x29, starting transfers between devices: none -> 49 us  [the longest x26 44.7 us: shifted(): lax.ppermute(array, axis, [(i, (i + by) % size) for i in range(size)])]
    pallas_call x0 -> x7, Pallas kernels: none -> 25.4 us  [the longest x5 17.2 us: partial_scores(): pl.pallas_call(partial_kernel, grid=(rows // BLOCK,), in_specs=[pl.BlockS...]
    dot_general x5 -> x6, matrix products: 18.9 us -> 6.61 us  [the longest x2 2.37 us: dot_t(): lax.dot_general(left, right, (((1,), (1,)), ((), ())), preferred_element_...]
  transfers between devices with their start and end apart: 3 -> 29, of which waited for: 3 -> 16; matrix products, arithmetic and copies ran while one was open for 1% -> 12% of each run, Pallas kernels for 0% -> 15%
where the time goes in v2:
time: 153 us
  waiting for transfers between devices  55.7 us (36%)
  starting transfers between devices  49 us (32%)
  Pallas kernels  25.4 us (17%)
  local copies, waits for them, and re-layouts  7.94 us (5%)
  matrix products  6.61 us (4%)
  other arithmetic  6.55 us (4%)
    ppermute x26, waiting for transfers between devices, shifted(): lax.ppermute(array, axis, [(i, (i + by) % size) for i in range(size)])  51.7 us
    ppermute x26, starting transfers between devices, shifted(): lax.ppermute(array, axis, [(i, (i + by) % size) for i in range(size)])  44.7 us
    pallas_call x5, Pallas kernels, partial_scores(): pl.pallas_call(partial_kernel, grid=(rows // BLOCK,), in_specs=[pl.BlockS...  17.2 us
    pallas_call x1, Pallas kernels, own_scores(): pl.pallas_call(own_kernel, grid=(rows // BLOCK,), in_specs=[pl.BlockSpec(...  5.16 us
    ppermute x3, starting transfers between devices, paired(): return lax.ppermute(array, axis, [(i, i ^ bit) for i in range(size)])  4.3 us
    ppermute x3, waiting for transfers between devices, paired(): return lax.ppermute(array, axis, [(i, i ^ bit) for i in range(size)])  4.02 us
  transfers between devices with their start and end apart: 29, of which 16 were waited for; matrix products, arithmetic and copies ran while one was open for 12% of the time, Pallas kernels for 15%

profile of v2, /device:TPU:1, one launch (start us, length us, event | category | flops | bytes accessed | tf_op | source)
XLA Modules:
  0.0 152.6 jit_solution(12597024169990798825)
XLA Ops:
  0.0 2.2 %collective-permute-start = (bf16[16,2048]{1,0:T(8,128)(2,1)}, bf16[16,2048]{1,0:T(8,128)(2,1)S(1)}, u32[]{:S(2)}, u32[]{:S(2)}) collective-permute-start(bf16[16,2048]{1,0:T(8,128)(2,1)} %param.12), channel_id=1, source_target_pairs={{0,128},{128,0},{1,129},{129,1},{2,130},{130,2},{3,131},{131,3},{4... | collective-permute-start | bytes 196616 | tf_op jit(solution)/shard_map/ppermute | solution.py:19
  2.2 2.0 %convolution_convert_fusion.1 = bf16[128,64]{0,1:T(8,128)(2,1)S(1)} fusion(bf16[128,5120]{1,0:T(8,128)(2,1)} %bitcast.238, bf16[5120,64]{0,1:T(8,128)(2,1)} %param.9), kind=kOutput, calls=%fused_computation.5 | convolution fusion | flops 83894272 | bytes 1982464 | tf_op jit(solution)/shard_map/dot_general | solution.py:36
  4.4 1.8 %convolution_convert_fusion.2 = bf16[128,32]{0,1:T(8,128)(2,1)S(1)} fusion(bf16[128,8192]{1,0:T(8,128)(2,1)S(1)} %bitcast.212, bf16[8192,32]{0,1:T(8,128)(2,1)} %param.10), kind=kOutput, calls=%fused_computation.6 | convolution fusion | flops 67112960 | bytes 2629632 | tf_op jit(solution)/shard_map/dot_general | solution.py:39
  7.2 2.0 %collective-permute-done.7 = bf16[2,2048]{1,0:T(2,128)(2,1)S(1)} collective-permute-done((bf16[2,2048]{1,0:T(2,128)(2,1)S(1)}, bf16[2,2048]{1,0:T(2,128)(2,1)S(1)}, u32[]{:S(2)}, u32[]{:S(2)}) %collective-permute-start.7) | collective-permute-done | bytes 8224 | tf_op jit(solution)/shard_map/ppermute | solution.py:24
  9.1 1.3 collective-permute-start.8
  10.4 1.4 collective-permute-done.8
  11.8 2.8 %collective-permute-start.9 = (bf16[8,2048]{1,0:T(8,128)(2,1)S(1)}, bf16[8,2048]{1,0:T(8,128)(2,1)S(1)}, u32[]{:S(2)}, u32[]{:S(2)}) collective-permute-start(bf16[8,2048]{1,0:T(8,128)(2,1)S(1)} %pad_maximum_fusion.18), channel_id=1, source_target_pairs={{0,64},{32,96},{64,0},{96,32},{1,65},{33,97},{65,1},{97,33},{2,66}... | collective-permute-start | bytes 98312 | tf_op jit(solution)/shard_map/ppermute | solution.py:24
  16.6 1.3 collective-permute-start.1
  17.9 2.5 %collective-permute-start.2 = (bf16[2,16,2048]{2,1,0:T(8,128)(2,1)S(1)}, bf16[2,16,2048]{2,1,0:T(8,128)(2,1)S(1)}, u32[]{:S(2)}, u32[]{:S(2)}) collective-permute-start(bf16[2,16,2048]{2,1,0:T(8,128)(2,1)S(1)} %pad_maximum_fusion.17), channel_id=1, source_target_pairs={{0,64},{32,96},{64,0},{96,32},{1,65},{33,97},{65,1},{97,33},{2,66}... | collective-permute-start | bytes 393224 | tf_op jit(solution)/shard_map/ppermute | solution.py:19
  20.3 1.1 collective-permute-start.3
  21.7 2.4 %collective-permute-done.2 = bf16[2,16,2048]{2,1,0:T(8,128)(2,1)S(1)} collective-permute-done((bf16[2,16,2048]{2,1,0:T(8,128)(2,1)S(1)}, bf16[2,16,2048]{2,1,0:T(8,128)(2,1)S(1)}, u32[]{:S(2)}, u32[]{:S(2)}) %collective-permute-start.2) | collective-permute-done | bytes 131104 | tf_op jit(solution)/shard_map/ppermute | solution.py:19
  24.2 6.2 %collective-permute-start.22 = (bf16[64,2048]{1,0:T(8,128)(2,1)S(1)}, bf16[64,2048]{1,0:T(8,128)(2,1)S(1)}, u32[]{:S(2)}, u32[]{:S(2)}) collective-permute-start(bf16[64,2048]{1,0:T(8,128)(2,1)S(1)} %bitcast.219), channel_id=1, source_target_pairs={{0,2},{2,0},{1,3},{3,1},{4,6},{6,4},{5,7},{7,5},{8,10},{10,8},{9,1... | collective-permute-start | bytes 786440 | tf_op jit(solution)/shard_map/ppermute | solution.py:19
  30.4 1.7 %collective-permute-start.4 = (bf16[64,2048]{1,0:T(8,128)(2,1)S(1)}, bf16[64,2048]{1,0:T(8,128)(2,1)S(1)}, u32[]{:S(2)}, u32[]{:S(2)}) collective-permute-start(bf16[64,2048]{1,0:T(8,128)(2,1)S(1)} %bitcast.220), channel_id=1, source_target_pairs={{0,4},{4,8},{8,12},{12,16},{16,20},{20,24},{24,28},{28,0},{1,5},{5... | collective-permute-start | bytes 786440 | tf_op jit(solution)/shard_map/ppermute | solution.py:19
  32.1 3.9 %collective-permute-start.5 = (bf16[64,2048]{1,0:T(8,128)(2,1)S(1)}, bf16[64,2048]{1,0:T(8,128)(2,1)S(1)}, u32[]{:S(2)}, u32[]{:S(2)}) collective-permute-start(bf16[64,2048]{1,0:T(8,128)(2,1)S(1)} %bitcast.221), channel_id=1, source_target_pairs={{0,28},{4,0},{8,4},{12,8},{16,12},{20,16},{24,20},{28,24},{1,29},{... | collective-permute-start | bytes 786440 | tf_op jit(solution)/shard_map/ppermute | solution.py:19
  37.1 5.5 %collective-permute-done.4 = bf16[64,2048]{1,0:T(8,128)(2,1)S(1)} collective-permute-done((bf16[64,2048]{1,0:T(8,128)(2,1)S(1)}, bf16[64,2048]{1,0:T(8,128)(2,1)S(1)}, u32[]{:S(2)}, u32[]{:S(2)}) %collective-permute-start.4) | collective-permute-done | bytes 262176 | tf_op jit(solution)/shard_map/ppermute | solution.py:19
  43.6 2.7 %collective-permute-start.11 = (bf16[132,2048]{1,0:T(8,128)(2,1)S(1)}, bf16[132,2048]{1,0:T(8,128)(2,1)S(1)}, u32[]{:S(2)}, u32[]{:S(2)}) collective-permute-start(bf16[132,2048]{1,0:T(8,128)(2,1)S(1)} %get-tuple-element.49), channel_id=1, source_target_pairs={{0,28},{4,0},{8,4},{12,8},{16,12},{20,16},{24,20},{28,24},{1,29},{... | collective-permute-start | bytes 1622024 | tf_op jit(solution)/shard_map/ppermute | solution.py:19
  46.4 3.2 %shard_map.74 = f32[144,1024]{1,0:T(8,128)S(1)} custom-call(bf16[64,2048]{1,0:T(8,128)(2,1)S(1)} %bitcast.222, bf16[64,2048]{1,0:T(8,128)(2,1)S(1)} %collective-permute-done.22.twin_ref, bf16[1024,2048]{1,0:T(8,128)(2,1)S(1)} %copy-done.2), custom_call_target="tpu_custom_call" | custom-call | flops 536870912 | bytes 16777216 | tf_op jit(solution)/shard_map/pallas_call | solution.py:70
  49.7 2.9 %collective-permute-start.23 = (f16[144,1024]{1,0:T(8,128)(2,1)S(1)}, f16[144,1024]{1,0:T(8,128)(2,1)S(1)}, u32[]{:S(2)}, u32[]{:S(2)}) collective-permute-start(f16[144,1024]{1,0:T(8,128)(2,1)S(1)} %convert_element_type.53), channel_id=1, source_target_pairs={{0,1},{1,0},{2,3},{3,2},{4,5},{5,4},{6,7},{7,6},{8,9},{9,8},{10,11... | collective-permute-start | bytes 884744 | tf_op jit(solution)/shard_map/ppermute | solution.py:19
  52.7 6.9 %collective-permute-done.23 = f16[144,1024]{1,0:T(8,128)(2,1)S(1)} collective-permute-done((f16[144,1024]{1,0:T(8,128)(2,1)S(1)}, f16[144,1024]{1,0:T(8,128)(2,1)S(1)}, u32[]{:S(2)}, u32[]{:S(2)}) %collective-permute-start.23) | collective-permute-done | bytes 294944 | tf_op jit(solution)/shard_map/ppermute | solution.py:19
  60.5 1.4 collective-permute-start.12
  62.7 3.6 %shard_map.75 = f32[272,1024]{1,0:T(8,128)S(1)} custom-call(bf16[128,2048]{1,0:T(8,128)(2,1)S(1)} %pad_maximum_fusion.8.own_ref, bf16[128,2048]{1,0:T(8,128)(2,1)S(1)} %slice.340.twin_ref, bf16[1024,2048]{1,0:T(8,128)(2,1)S(1)} %copy-done.2), custom_call_target="tpu_custom_call" | custom-call | flops 1073741824 | bytes 16777216 | tf_op jit(solution)/shard_map/pallas_call | solution.py:70
  66.4 2.7 %collective-permute-start.24 = (f16[272,1024]{1,0:T(8,128)(2,1)S(1)}, f16[272,1024]{1,0:T(8,128)(2,1)S(1)}, u32[]{:S(2)}, u32[]{:S(2)}) collective-permute-start(f16[272,1024]{1,0:T(8,128)(2,1)S(1)} %convert_element_type.55), channel_id=1, source_target_pairs={{0,1},{1,0},{2,3},{3,2},{4,5},{5,4},{6,7},{7,6},{8,9},{9,8},{10,11... | collective-permute-start | bytes 1671176 | tf_op jit(solution)/shard_map/ppermute | solution.py:19
  69.3 8.3 %collective-permute-done.13 = bf16[132,2048]{1,0:T(8,128)(2,1)S(1)} collective-permute-done((bf16[132,2048]{1,0:T(8,128)(2,1)S(1)}, bf16[132,2048]{1,0:T(8,128)(2,1)S(1)}, u32[]{:S(2)}, u32[]{:S(2)}) %collective-permute-start.13) | collective-permute-done | bytes 540704 | tf_op jit(solution)/shard_map/ppermute | solution.py:19
  78.0 1.4 collective-permute-start.16
  79.4 2.4 %collective-permute-done.24 = f16[272,1024]{1,0:T(8,128)(2,1)S(1)} collective-permute-done((f16[272,1024]{1,0:T(8,128)(2,1)S(1)}, f16[272,1024]{1,0:T(8,128)(2,1)S(1)}, u32[]{:S(2)}, u32[]{:S(2)}) %collective-permute-start.24) | collective-permute-done | bytes 557088 | tf_op jit(solution)/shard_map/ppermute | solution.py:19
  82.4 7.2 %collective-permute-done.16 = bf16[100,2048]{1,0:T(8,128)(2,1)S(1)} collective-permute-done((bf16[100,2048]{1,0:T(8,128)(2,1)S(1)}, bf16[100,2048]{1,0:T(8,128)(2,1)S(1)}, u32[]{:S(2)}, u32[]{:S(2)}) %collective-permute-start.16) | collective-permute-done | bytes 409632 | tf_op jit(solution)/shard_map/ppermute | solution.py:19
  89.7 3.6 %shard_map.76 = f32[272,1024]{1,0:T(8,128)S(1)} custom-call(bf16[128,2048]{1,0:T(8,128)(2,1)S(1)} %pad_maximum_fusion.9.own_ref, bf16[128,2048]{1,0:T(8,128)(2,1)S(1)} %slice.347.twin_ref, bf16[1024,2048]{1,0:T(8,128)(2,1)S(1)} %copy-done.2), custom_call_target="tpu_custom_call" | custom-call | flops 1073741824 | bytes 16777216 | tf_op jit(solution)/shard_map/pallas_call | solution.py:70
  94.2 2.6 %collective-permute-start.25 = (f16[272,1024]{1,0:T(8,128)(2,1)}, f16[272,1024]{1,0:T(8,128)(2,1)}, u32[]{:S(2)}, u32[]{:S(2)}) collective-permute-start(f16[272,1024]{1,0:T(8,128)(2,1)} %convert_element_type.57), channel_id=1, source_target_pairs={{0,1},{1,0},{2,3},{3,2},{4,5},{5,4},{6,7},{7,6},{8,9},{9,8},{10,11... | collective-permute-start | bytes 1671176 | tf_op jit(solution)/shard_map/ppermute | solution.py:19
  97.2 1.3 pad_maximum_fusion.1
  98.6 2.3 %collective-permute-start.15 = (bf16[256,2048]{1,0:T(8,128)(2,1)}, bf16[256,2048]{1,0:T(8,128)(2,1)S(1)}, u32[]{:S(2)}, u32[]{:S(2)}) collective-permute-start(bf16[256,2048]{1,0:T(8,128)(2,1)} %pad_maximum_fusion.1), channel_id=1, source_target_pairs={{0,2},{2,0},{1,3},{3,1},{4,6},{6,4},{5,7},{7,5},{8,10},{10,8},{9,1... | collective-permute-start | bytes 3145736 | tf_op jit(solution)/shard_map/ppermute | solution.py:19
  101.1 1.5 collective-permute-start.19
  102.6 5.7 %collective-permute-done.19 = bf16[36,2048]{1,0:T(8,128)(2,1)S(1)} collective-permute-done((bf16[36,2048]{1,0:T(8,128)(2,1)S(1)}, bf16[36,2048]{1,0:T(8,128)(2,1)S(1)}, u32[]{:S(2)}, u32[]{:S(2)}) %collective-permute-start.19) | collective-permute-done | bytes 147488 | tf_op jit(solution)/shard_map/ppermute | solution.py:19
  108.3 4.2 %collective-permute-done.17 = bf16[100,2048]{1,0:T(8,128)(2,1)S(1)} collective-permute-done((bf16[100,2048]{1,0:T(8,128)(2,1)S(1)}, bf16[100,2048]{1,0:T(8,128)(2,1)S(1)}, u32[]{:S(2)}, u32[]{:S(2)}) %collective-permute-start.17) | collective-permute-done | bytes 409632 | tf_op jit(solution)/shard_map/ppermute | solution.py:19
  114.3 1.3 collective-permute-start.20
  115.6 1.1 convert_element_type.58
  117.2 2.3 %collective-permute-done.20 = bf16[32,2048]{1,0:T(8,128)(2,1)S(1)} collective-permute-done((bf16[32,2048]{1,0:T(8,128)(2,1)S(1)}, bf16[32,2048]{1,0:T(8,128)(2,1)S(1)}, u32[]{:S(2)}, u32[]{:S(2)}) %collective-permute-start.20) | collective-permute-done | bytes 131104 | tf_op jit(solution)/shard_map/ppermute | solution.py:19
  120.7 1.2 collective-permute-done.21
  121.9 3.6 %shard_map.77 = f32[272,1024]{1,0:T(8,128)S(1)} custom-call(bf16[128,2048]{1,0:T(8,128)(2,1)S(1)} %pad_maximum_fusion.10.own_ref, bf16[128,2048]{1,0:T(8,128)(2,1)S(1)} %slice.354.twin_ref, bf16[1024,2048]{1,0:T(8,128)(2,1)S(1)} %copy-done.3), custom_call_target="tpu_custom_call" | custom-call | flops 1073741824 | bytes 16777216 | tf_op jit(solution)/shard_map/pallas_call | solution.py:70
  126.2 1.5 copy-done.5
  127.9 1.2 fusion.36
  129.0 3.3 %shard_map.78 = f32[144,1024]{1,0:T(8,128)S(1)} custom-call(bf16[64,2048]{1,0:T(8,128)(2,1)S(1)} %pad_maximum_fusion.15.own_ref, bf16[64,2048]{1,0:T(8,128)(2,1)S(1)} %get-tuple-element.28.twin_ref, bf16[1024,2048]{1,0:T(8,128)(2,1)S(1)} %copy-done.3), custom_call_target="tpu_custom_call" | custom-call | flops 536870912 | bytes 16777216 | tf_op jit(solution)/shard_map/pallas_call | solution.py:70
  132.3 1.2 fusion.3
  133.5 1.2 collective-permute-start.28
  134.8 1.9 %collective-permute-start.27 = (f16[144,1024]{1,0:T(8,128)(2,1)S(1)}, f16[144,1024]{1,0:T(8,128)(2,1)S(1)}, u32[]{:S(2)}, u32[]{:S(2)}) collective-permute-start(f16[144,1024]{1,0:T(8,128)(2,1)S(1)} %convert_element_type.61), channel_id=1, source_target_pairs={{0,1},{1,0},{2,3},{3,2},{4,5},{5,4},{6,7},{7,6},{8,9},{9,8},{10,11... | collective-permute-start | bytes 884744 | tf_op jit(solution)/shard_map/ppermute | solution.py:19
  136.8 5.2 %shard_map.73.own_ref = f32[1024,1024]{1,0:T(8,128)S(1)} custom-call(bf16[1024,2048]{1,0:T(8,128)(2,1)S(1)} %copy-done.3, bf16[1024,2048]{1,0:T(8,128)(2,1)S(1)} %bitcast.213), custom_call_target="tpu_custom_call" | custom-call | flops 4294967296 | bytes 12582912 | tf_op jit(solution)/shard_map/pallas_call | solution.py:94
  142.4 1.2 convolution_add_fusion.fresh_ref
  143.6 5.1 %collective-permute-done.27 = f16[144,1024]{1,0:T(8,128)(2,1)S(1)} collective-permute-done((f16[144,1024]{1,0:T(8,128)(2,1)S(1)}, f16[144,1024]{1,0:T(8,128)(2,1)S(1)}, u32[]{:S(2)}, u32[]{:S(2)}) %collective-permute-start.27) | collective-permute-done | bytes 294944 | tf_op jit(solution)/shard_map/ppermute | solution.py:19
  149.5 3.1 %shard_map.79 = bf16[1024,1024]{1,0:T(8,128)(2,1)} custom-call(f32[1024,1024]{1,0:T(8,128)S(1)} %shard_map.73.own_ref, f32[1024,1024]{1,0:T(8,128)S(1)} %bitcast.215, f32[16,1024]{1,0:T(8,128)S(1)} %convolution_add_fusion.fresh_ref), custom_call_target="tpu_custom_call" | custom-call | flops 1048576 | bytes 10485760 | tf_op jit(solution)/shard_map/pallas_call | solution.py:126
  (197 shorter events, 15.2 us)
Async XLA Ops:
  0.0 4.4 %copy-start = (bf16[2,64,8192]{2,1,0:T(8,128)(2,1)S(1)}, bf16[2,64,8192]{2,1,0:T(8,128)(2,1)}, u32[]{:S(2)}) copy-start(bf16[2,64,8192]{2,1,0:T(8,128)(2,1)} %param.8) | copy-start | bytes 6291460
  0.0 16.5 %copy-start.12 = (bf16[16,2048]{1,0:T(8,128)(2,1)S(1)}, bf16[16,2048]{1,0:T(8,128)(2,1)}, u32[]{:S(2)}) copy-start(bf16[16,2048]{1,0:T(8,128)(2,1)} %param.12) | copy-start | bytes 196612
  0.0 14.8 %copy-start.8 = (s32[256]{0:T(256)S(1)}, s32[256]{0:T(256)}, u32[]{:S(2)}) copy-start(s32[256]{0:T(256)} %param.13) | copy-start | bytes 3076
  0.0 16.5 %collective-permute-start = (bf16[16,2048]{1,0:T(8,128)(2,1)}, bf16[16,2048]{1,0:T(8,128)(2,1)S(1)}, u32[]{:S(2)}, u32[]{:S(2)}) collective-permute-start(bf16[16,2048]{1,0:T(8,128)(2,1)} %param.12), channel_id=1, source_target_pairs={{0,128},{128,0},{1,129},{129,1},{2,130},{130,2},{3,131},{131,3},{4... | collective-permute-start | bytes 196616 | tf_op jit(solution)/shard_map/ppermute | solution.py:19
  6.6 2.5 %collective-permute-start.7 = (bf16[2,2048]{1,0:T(2,128)(2,1)S(1)}, bf16[2,2048]{1,0:T(2,128)(2,1)S(1)}, u32[]{:S(2)}, u32[]{:S(2)}) collective-permute-start(bf16[2,2048]{1,0:T(2,128)(2,1)S(1)} %convert_element_type.51), channel_id=1, source_target_pairs={{0,128},{128,0},{1,129},{129,1},{2,130},{130,2},{3,131},{131,3},{4... | collective-permute-start | bytes 24584 | tf_op jit(solution)/shard_map/ppermute | solution.py:24
  9.1 2.7 %collective-permute-start.8 = (bf16[4,2048]{1,0:T(4,128)(2,1)S(1)}, bf16[4,2048]{1,0:T(4,128)(2,1)S(1)}, u32[]{:S(2)}, u32[]{:S(2)}) collective-permute-start(bf16[4,2048]{1,0:T(4,128)(2,1)S(1)} %pad_maximum_fusion.19), channel_id=1, source_target_pairs={{0,32},{32,0},{64,96},{96,64},{1,33},{33,1},{65,97},{97,65},{2,34}... | collective-permute-start | bytes 49160 | tf_op jit(solution)/shard_map/ppermute | solution.py:24
  11.8 4.4 %collective-permute-start.9 = (bf16[8,2048]{1,0:T(8,128)(2,1)S(1)}, bf16[8,2048]{1,0:T(8,128)(2,1)S(1)}, u32[]{:S(2)}, u32[]{:S(2)}) collective-permute-start(bf16[8,2048]{1,0:T(8,128)(2,1)S(1)} %pad_maximum_fusion.18), channel_id=1, source_target_pairs={{0,64},{32,96},{64,0},{96,32},{1,65},{33,97},{65,1},{97,33},{2,66}... | collective-permute-start | bytes 98312 | tf_op jit(solution)/shard_map/ppermute | solution.py:24
  16.6 5.1 %collective-permute-start.1 = (bf16[2,16,2048]{2,1,0:T(8,128)(2,1)S(1)}, bf16[2,16,2048]{2,1,0:T(8,128)(2,1)S(1)}, u32[]{:S(2)}, u32[]{:S(2)}) collective-permute-start(bf16[2,16,2048]{2,1,0:T(8,128)(2,1)S(1)} %pad_maximum_fusion.17), channel_id=1, source_target_pairs={{0,32},{32,64},{64,96},{96,0},{1,33},{33,65},{65,97},{97,1},{2,34}... | collective-permute-start | bytes 393224 | tf_op jit(solution)/shard_map/ppermute | solution.py:19
  17.9 6.2 %collective-permute-start.2 = (bf16[2,16,2048]{2,1,0:T(8,128)(2,1)S(1)}, bf16[2,16,2048]{2,1,0:T(8,128)(2,1)S(1)}, u32[]{:S(2)}, u32[]{:S(2)}) collective-permute-start(bf16[2,16,2048]{2,1,0:T(8,128)(2,1)S(1)} %pad_maximum_fusion.17), channel_id=1, source_target_pairs={{0,64},{32,96},{64,0},{96,32},{1,65},{33,97},{65,1},{97,33},{2,66}... | collective-permute-start | bytes 393224 | tf_op jit(solution)/shard_map/ppermute | solution.py:19
  20.3 3.8 %collective-permute-start.3 = (bf16[2,16,2048]{2,1,0:T(8,128)(2,1)S(1)}, bf16[2,16,2048]{2,1,0:T(8,128)(2,1)S(1)}, u32[]{:S(2)}, u32[]{:S(2)}) collective-permute-start(bf16[2,16,2048]{2,1,0:T(8,128)(2,1)S(1)} %pad_maximum_fusion.17), channel_id=1, source_target_pairs={{0,96},{32,0},{64,32},{96,64},{1,97},{33,1},{65,33},{97,65},{2,98}... | collective-permute-start | bytes 393224 | tf_op jit(solution)/shard_map/ppermute | solution.py:19
  24.2 22.2 %collective-permute-start.22 = (bf16[64,2048]{1,0:T(8,128)(2,1)S(1)}, bf16[64,2048]{1,0:T(8,128)(2,1)S(1)}, u32[]{:S(2)}, u32[]{:S(2)}) collective-permute-start(bf16[64,2048]{1,0:T(8,128)(2,1)S(1)} %bitcast.219), channel_id=1, source_target_pairs={{0,2},{2,0},{1,3},{3,1},{4,6},{6,4},{5,7},{7,5},{8,10},{10,8},{9,1... | collective-permute-start | bytes 786440 | tf_op jit(solution)/shard_map/ppermute | solution.py:19
  30.4 12.2 %collective-permute-start.4 = (bf16[64,2048]{1,0:T(8,128)(2,1)S(1)}, bf16[64,2048]{1,0:T(8,128)(2,1)S(1)}, u32[]{:S(2)}, u32[]{:S(2)}) collective-permute-start(bf16[64,2048]{1,0:T(8,128)(2,1)S(1)} %bitcast.220), channel_id=1, source_target_pairs={{0,4},{4,8},{8,12},{12,16},{16,20},{20,24},{24,28},{28,0},{1,5},{5... | collective-permute-start | bytes 786440 | tf_op jit(solution)/shard_map/ppermute | solution.py:19
  32.1 10.5 %collective-permute-start.5 = (bf16[64,2048]{1,0:T(8,128)(2,1)S(1)}, bf16[64,2048]{1,0:T(8,128)(2,1)S(1)}, u32[]{:S(2)}, u32[]{:S(2)}) collective-permute-start(bf16[64,2048]{1,0:T(8,128)(2,1)S(1)} %bitcast.221), channel_id=1, source_target_pairs={{0,28},{4,0},{8,4},{12,8},{16,12},{20,16},{24,20},{28,24},{1,29},{... | collective-permute-start | bytes 786440 | tf_op jit(solution)/shard_map/ppermute | solution.py:19
  36.5 9.8 %copy-start.2 = (bf16[1024,2048]{1,0:T(8,128)(2,1)S(1)}, bf16[1024,2048]{1,0:T(8,128)(2,1)}, u32[]{:S(2)}) copy-start(bf16[1024,2048]{1,0:T(8,128)(2,1)} %store_ref.11) | copy-start | bytes 12582916
  42.7 20.0 %collective-permute-start.6 = (bf16[192,2048]{1,0:T(8,128)(2,1)S(1)}, bf16[192,2048]{1,0:T(8,128)(2,1)S(1)}, u32[]{:S(2)}, u32[]{:S(2)}) collective-permute-start(bf16[192,2048]{1,0:T(8,128)(2,1)S(1)} %pad_maximum_fusion.2), channel_id=1, source_target_pairs={{0,2},{2,0},{1,3},{3,1},{4,6},{6,4},{5,7},{7,5},{8,10},{10,8},{9,1... | collective-permute-start | bytes 2359304 | tf_op jit(solution)/shard_map/ppermute | solution.py:19
  43.6 16.8 %collective-permute-start.10 = (bf16[132,2048]{1,0:T(8,128)(2,1)S(1)}, bf16[132,2048]{1,0:T(8,128)(2,1)S(1)}, u32[]{:S(2)}, u32[]{:S(2)}) collective-permute-start(bf16[132,2048]{1,0:T(8,128)(2,1)S(1)} %get-tuple-element.50), channel_id=1, source_target_pairs={{0,4},{4,8},{8,12},{12,16},{16,20},{20,24},{24,28},{28,0},{1,5},{5... | collective-permute-start | bytes 1622024 | tf_op jit(solution)/shard_map/ppermute | solution.py:19
  43.6 16.7 %collective-permute-start.11 = (bf16[132,2048]{1,0:T(8,128)(2,1)S(1)}, bf16[132,2048]{1,0:T(8,128)(2,1)S(1)}, u32[]{:S(2)}, u32[]{:S(2)}) collective-permute-start(bf16[132,2048]{1,0:T(8,128)(2,1)S(1)} %get-tuple-element.49), channel_id=1, source_target_pairs={{0,28},{4,0},{8,4},{12,8},{16,12},{20,16},{24,20},{28,24},{1,29},{... | collective-permute-start | bytes 1622024 | tf_op jit(solution)/shard_map/ppermute | solution.py:19
  49.7 9.9 %collective-permute-start.23 = (f16[144,1024]{1,0:T(8,128)(2,1)S(1)}, f16[144,1024]{1,0:T(8,128)(2,1)S(1)}, u32[]{:S(2)}, u32[]{:S(2)}) collective-permute-start(f16[144,1024]{1,0:T(8,128)(2,1)S(1)} %convert_element_type.53), channel_id=1, source_target_pairs={{0,1},{1,0},{2,3},{3,2},{4,5},{5,4},{6,7},{7,6},{8,9},{9,8},{10,11... | collective-permute-start | bytes 884744 | tf_op jit(solution)/shard_map/ppermute | solution.py:19
  60.5 29.1 %collective-permute-start.12 = (bf16[256,2048]{1,0:T(8,128)(2,1)S(1)}, bf16[256,2048]{1,0:T(8,128)(2,1)S(1)}, u32[]{:S(2)}, u32[]{:S(2)}) collective-permute-start(bf16[256,2048]{1,0:T(8,128)(2,1)S(1)} %pad_maximum_fusion), channel_id=1, source_target_pairs={{0,2},{2,0},{1,3},{3,1},{4,6},{6,4},{5,7},{7,5},{8,10},{10,8},{9,1... | collective-permute-start | bytes 3145736 | tf_op jit(solution)/shard_map/ppermute | solution.py:19
  62.1 15.5 %collective-permute-start.13 = (bf16[132,2048]{1,0:T(8,128)(2,1)S(1)}, bf16[132,2048]{1,0:T(8,128)(2,1)S(1)}, u32[]{:S(2)}, u32[]{:S(2)}) collective-permute-start(bf16[132,2048]{1,0:T(8,128)(2,1)S(1)} %pad_maximum_fusion.6), channel_id=1, source_target_pairs={{0,4},{4,8},{8,12},{12,16},{16,20},{20,24},{24,28},{28,0},{1,5},{5... | collective-permute-start | bytes 1622024 | tf_op jit(solution)/shard_map/ppermute | solution.py:19
  66.4 15.5 %collective-permute-start.24 = (f16[272,1024]{1,0:T(8,128)(2,1)S(1)}, f16[272,1024]{1,0:T(8,128)(2,1)S(1)}, u32[]{:S(2)}, u32[]{:S(2)}) collective-permute-start(f16[272,1024]{1,0:T(8,128)(2,1)S(1)} %convert_element_type.55), channel_id=1, source_target_pairs={{0,1},{1,0},{2,3},{3,2},{4,5},{5,4},{6,7},{7,6},{8,9},{9,8},{10,11... | collective-permute-start | bytes 1671176 | tf_op jit(solution)/shard_map/ppermute | solution.py:19
  77.7 19.5 %collective-permute-start.14 = (bf16[132,2048]{1,0:T(8,128)(2,1)S(1)}, bf16[132,2048]{1,0:T(8,128)(2,1)S(1)}, u32[]{:S(2)}, u32[]{:S(2)}) collective-permute-start(bf16[132,2048]{1,0:T(8,128)(2,1)S(1)} %pad_maximum_fusion.7), channel_id=1, source_target_pairs={{0,28},{4,0},{8,4},{12,8},{16,12},{20,16},{24,20},{28,24},{1,29},{... | collective-permute-start | bytes 1622024 | tf_op jit(solution)/shard_map/ppermute | solution.py:19
  78.0 11.5 %collective-permute-start.16 = (bf16[100,2048]{1,0:T(8,128)(2,1)S(1)}, bf16[100,2048]{1,0:T(8,128)(2,1)S(1)}, u32[]{:S(2)}, u32[]{:S(2)}) collective-permute-start(bf16[100,2048]{1,0:T(8,128)(2,1)S(1)} %pad_maximum_fusion.11), channel_id=1, source_target_pairs={{0,4},{4,8},{8,12},{12,16},{16,20},{20,24},{24,28},{28,0},{1,5},{5... | collective-permute-start | bytes 1228808 | tf_op jit(solution)/shard_map/ppermute | solution.py:19
  82.4 10.9 %copy-start.6 = (f32[4,8,2,16,1024]{4,3,2,1,0:T(8,128)}, f32[4,8,2,16,1024]{4,3,2,1,0:T(8,128)S(1)}, u32[]{:S(2)}) copy-start(f32[4,8,2,16,1024]{4,3,2,1,0:T(8,128)S(1)} %constant_dynamic-update-slice_fusion.25) | copy-start | bytes 12582916
  94.2 21.4 %collective-permute-start.25 = (f16[272,1024]{1,0:T(8,128)(2,1)}, f16[272,1024]{1,0:T(8,128)(2,1)}, u32[]{:S(2)}, u32[]{:S(2)}) collective-permute-start(f16[272,1024]{1,0:T(8,128)(2,1)} %convert_element_type.57), channel_id=1, source_target_pairs={{0,1},{1,0},{2,3},{3,2},{4,5},{5,4},{6,7},{7,6},{8,9},{9,8},{10,11... | collective-permute-start | bytes 1671176 | tf_op jit(solution)/shard_map/ppermute | solution.py:19
  97.0 11.3 %copy-start.9 = (bf16[4,8,2,16,2048]{4,3,2,1,0:T(8,128)(2,1)}, bf16[4,8,2,16,2048]{4,3,2,1,0:T(8,128)(2,1)S(1)}, u32[]{:S(2)}) copy-start(bf16[4,8,2,16,2048]{4,3,2,1,0:T(8,128)(2,1)S(1)} %constant_dynamic-update-slice_fusion.5) | copy-start | bytes 12582916
  97.2 16.3 %copy-start.4 = (bf16[4,8,2,16,2048]{4,3,2,1,0:T(8,128)(2,1)}, bf16[4,8,2,16,2048]{4,3,2,1,0:T(8,128)(2,1)S(1)}, u32[]{:S(2)}) copy-start(bf16[4,8,2,16,2048]{4,3,2,1,0:T(8,128)(2,1)S(1)} %constant_dynamic-update-slice_fusion.40) | copy-start | bytes 12582916
  98.6 23.3 %collective-permute-start.15 = (bf16[256,2048]{1,0:T(8,128)(2,1)}, bf16[256,2048]{1,0:T(8,128)(2,1)S(1)}, u32[]{:S(2)}, u32[]{:S(2)}) collective-permute-start(bf16[256,2048]{1,0:T(8,128)(2,1)} %pad_maximum_fusion.1), channel_id=1, source_target_pairs={{0,2},{2,0},{1,3},{3,1},{4,6},{6,4},{5,7},{7,5},{8,10},{10,8},{9,1... | collective-permute-start | bytes 3145736 | tf_op jit(solution)/shard_map/ppermute | solution.py:19
  100.9 11.5 %collective-permute-start.17 = (bf16[100,2048]{1,0:T(8,128)(2,1)S(1)}, bf16[100,2048]{1,0:T(8,128)(2,1)S(1)}, u32[]{:S(2)}, u32[]{:S(2)}) collective-permute-start(bf16[100,2048]{1,0:T(8,128)(2,1)S(1)} %pad_maximum_fusion.12), channel_id=1, source_target_pairs={{0,28},{4,0},{8,4},{12,8},{16,12},{20,16},{24,20},{28,24},{1,29},{... | collective-permute-start | bytes 1228808 | tf_op jit(solution)/shard_map/ppermute | solution.py:19
  101.1 7.2 %collective-permute-start.19 = (bf16[36,2048]{1,0:T(8,128)(2,1)S(1)}, bf16[36,2048]{1,0:T(8,128)(2,1)S(1)}, u32[]{:S(2)}, u32[]{:S(2)}) collective-permute-start(bf16[36,2048]{1,0:T(8,128)(2,1)S(1)} %pad_maximum_fusion.16), channel_id=1, source_target_pairs={{0,4},{4,8},{8,12},{12,16},{16,20},{20,24},{24,28},{28,0},{1,5},{5... | collective-permute-start | bytes 442376 | tf_op jit(solution)/shard_map/ppermute | solution.py:19
  113.5 14.4 %collective-permute-start.18 = (bf16[192,2048]{1,0:T(8,128)(2,1)}, bf16[192,2048]{1,0:T(8,128)(2,1)}, u32[]{:S(2)}, u32[]{:S(2)}) collective-permute-start(bf16[192,2048]{1,0:T(8,128)(2,1)} %pad_maximum_fusion.3), channel_id=1, source_target_pairs={{0,2},{2,0},{1,3},{3,1},{4,6},{6,4},{5,7},{7,5},{8,10},{10,8},{9,1... | collective-permute-start | bytes 2359304 | tf_op jit(solution)/shard_map/ppermute | solution.py:19
  114.3 2.8 %copy-start.7 = (f32[4,8,2,16,1024]{4,3,2,1,0:T(8,128)S(1)}, f32[4,8,2,16,1024]{4,3,2,1,0:T(8,128)}, u32[]{:S(2)}) copy-start(f32[4,8,2,16,1024]{4,3,2,1,0:T(8,128)} %copy-done.6) | copy-start | bytes 12582916
  114.3 5.2 %collective-permute-start.20 = (bf16[32,2048]{1,0:T(8,128)(2,1)S(1)}, bf16[32,2048]{1,0:T(8,128)(2,1)S(1)}, u32[]{:S(2)}, u32[]{:S(2)}) collective-permute-start(bf16[32,2048]{1,0:T(8,128)(2,1)S(1)} %get-tuple-element.47), channel_id=1, source_target_pairs={{0,28},{4,0},{8,4},{12,8},{16,12},{20,16},{24,20},{28,24},{1,29},{... | collective-permute-start | bytes 393224 | tf_op jit(solution)/shard_map/ppermute | solution.py:19
  116.8 5.1 %copy-start.3 = (bf16[1024,2048]{1,0:T(8,128)(2,1)S(1)}, bf16[1024,2048]{1,0:T(8,128)(2,1)}, u32[]{:S(2)}) copy-start(bf16[1024,2048]{1,0:T(8,128)(2,1)} %store_ref.11) | copy-start | bytes 12582916
  119.5 2.3 %collective-permute-start.21 = (bf16[66,2048]{1,0:T(8,128)(2,1)S(1)}, bf16[66,2048]{1,0:T(8,128)(2,1)S(1)}, u32[]{:S(2)}, u32[]{:S(2)}) collective-permute-start(bf16[66,2048]{1,0:T(8,128)(2,1)S(1)} %pad_maximum_fusion.13), channel_id=1, source_target_pairs={{0,2},{2,0},{1,3},{3,1},{4,6},{6,4},{5,7},{7,5},{8,10},{10,8},{9,1... | collective-permute-start | bytes 811016 | tf_op jit(solution)/shard_map/ppermute | solution.py:19
  121.8 3.8 %copy-start.11 = (bf16[66,2048]{1,0:T(8,128)(2,1)}, bf16[66,2048]{1,0:T(8,128)(2,1)S(1)}, u32[]{:S(2)}) copy-start(bf16[66,2048]{1,0:T(8,128)(2,1)S(1)} %collective-permute-done.21) | copy-start | bytes 811012
  121.9 4.2 %copy-start.10 = (bf16[4,8,2,16,2048]{4,3,2,1,0:T(8,128)(2,1)S(1)}, bf16[4,8,2,16,2048]{4,3,2,1,0:T(8,128)(2,1)}, u32[]{:S(2)}) copy-start(bf16[4,8,2,16,2048]{4,3,2,1,0:T(8,128)(2,1)} %copy-done.9) | copy-start | bytes 12582916
  125.5 2.2 %copy-start.5 = (bf16[4,8,2,16,2048]{4,3,2,1,0:T(8,128)(2,1)S(1)}, bf16[4,8,2,16,2048]{4,3,2,1,0:T(8,128)(2,1)}, u32[]{:S(2)}) copy-start(bf16[4,8,2,16,2048]{4,3,2,1,0:T(8,128)(2,1)} %copy-done.4) | copy-start | bytes 12582916
  125.6 23.3 %collective-permute-start.26 = (f16[272,1024]{1,0:T(8,128)(2,1)S(1)}, f16[272,1024]{1,0:T(8,128)(2,1)S(1)}, u32[]{:S(2)}, u32[]{:S(2)}) collective-permute-start(f16[272,1024]{1,0:T(8,128)(2,1)S(1)} %convert_element_type.59), channel_id=1, source_target_pairs={{0,1},{1,0},{2,3},{3,2},{4,5},{5,4},{6,7},{7,6},{8,9},{9,8},{10,11... | collective-permute-start | bytes 1671176 | tf_op jit(solution)/shard_map/ppermute | solution.py:19
  132.3 4.5 %slice-start = ((bf16[66,2048]{1,0:T(8,128)(2,1)}), bf16[64,2048]{1,0:T(8,128)(2,1)S(1)}, s32[]{:S(2)}) async-start(bf16[66,2048]{1,0:T(8,128)(2,1)} %copy-done.11), calls=%async_computation | async-start | bytes 524288 | tf_op jit(solution)/shard_map/slice | solution.py:203
  133.5 8.9 %collective-permute-start.28 = (f32[16,1024]{1,0:T(8,128)S(1)}, f32[16,1024]{1,0:T(8,128)S(1)}, u32[]{:S(2)}, u32[]{:S(2)}) collective-permute-start(f32[16,1024]{1,0:T(8,128)S(1)} %fusion.3), channel_id=1, source_target_pairs={{0,1},{1,0},{2,3},{3,2},{4,5},{5,4},{6,7},{7,6},{8,9},{9,8},{10,11... | collective-permute-start | bytes 196616 | tf_op jit(solution)/shard_map/ppermute | solution.py:19
  134.8 14.0 %collective-permute-start.27 = (f16[144,1024]{1,0:T(8,128)(2,1)S(1)}, f16[144,1024]{1,0:T(8,128)(2,1)S(1)}, u32[]{:S(2)}, u32[]{:S(2)}) collective-permute-start(f16[144,1024]{1,0:T(8,128)(2,1)S(1)} %convert_element_type.61), channel_id=1, source_target_pairs={{0,1},{1,0},{2,3},{3,2},{4,5},{5,4},{6,7},{7,6},{8,9},{9,8},{10,11... | collective-permute-start | bytes 884744 | tf_op jit(solution)/shard_map/ppermute | solution.py:19
  149.5 3.1 %copy-start.1 = (bf16[2,64,8192]{2,1,0:T(8,128)(2,1)S(1)}, bf16[2,64,8192]{2,1,0:T(8,128)(2,1)}, u32[]{:S(2)}) copy-start(bf16[2,64,8192]{2,1,0:T(8,128)(2,1)} %param.8) | copy-start | bytes 6291460

commit v3 on v0

v3 whole, which is shorter than its diff:
```python
import functools

import jax
import jax.numpy as jnp
from jax import lax
from jax.experimental import pallas as pl
from jax.experimental.pallas import tpu as pltpu
from jax.sharding import Mesh, PartitionSpec as P

DP = ("yl", "x", "z", "c")
SIZES = {"yl": 2, "x": 4, "z": 8, "c": 2, "yh": 2}
MIB = 1024 * 1024
BLOCK = 256
FILL_FLOPS = 20_000_000_000


def shifted(array, axis, by):
    size = SIZES[axis]
    return lax.ppermute(array, axis, [(i, (i + by) % size) for i in range(size)])


def paired(array, axis, bit):
    size = SIZES[axis]
    return lax.ppermute(array, axis, [(i, i ^ bit) for i in range(size)])


def dot_t(left, right):
    return lax.dot_general(
        left, right, (((1,), (1,)), ((), ())), preferred_element_type=jnp.float32
    )


def make_sketch(inputs, out_grads, proj_in, proj_out):
    examples, length, width_in = inputs.shape
    width_out = out_grads.shape[2]
    lin = jnp.dot(
        inputs.reshape(examples * length, width_in), proj_in, preferred_element_type=jnp.float32
    ).astype(jnp.bfloat16)
    lout = jnp.dot(
        out_grads.reshape(examples * length, width_out),
        proj_out,
        preferred_element_type=jnp.float32,
    ).astype(jnp.bfloat16)
    lin = lin.reshape(examples, length, -1)
    lout = lout.reshape(examples, length, -1)
    sketch = jnp.einsum("nso,nsi->noi", lout, lin, preferred_element_type=jnp.float32) * length ** (
        -0.5
    )
    return sketch.reshape(examples, -1).astype(jnp.bfloat16)


def own_kernel(store_ref, valid_ref, fresh_ref, out_ref, fresh_out_ref):
    out_ref[...] = dot_t(valid_ref[...], store_ref[...])

    @pl.when(pl.program_id(0) == 0)
    def _():
        fresh_out_ref[...] = dot_t(fresh_ref[...], valid_ref[...])


def own_scores(store, valid, fresh):
    rows, half = store.shape
    columns = valid.shape[0]
    return pl.pallas_call(
        own_kernel,
        grid=(rows // BLOCK,),
        in_specs=[
            pl.BlockSpec((BLOCK, half), lambda i: (i, 0)),
            pl.BlockSpec((columns, half), lambda i: (0, 0), pipeline_mode=pl.Buffered(1)),
            pl.BlockSpec(fresh.shape, lambda i: (0, 0)),
        ],
        out_specs=[
            pl.BlockSpec((columns, BLOCK), lambda i: (0, i)),
            pl.BlockSpec((fresh.shape[0], columns), lambda i: (0, 0)),
        ],
        out_shape=[
            jax.ShapeDtypeStruct((columns, rows), jnp.float32),
            jax.ShapeDtypeStruct((fresh.shape[0], columns), jnp.float32),
        ],
        compiler_params=pltpu.CompilerParams(vmem_limit_bytes=20 * MIB),
        cost_estimate=pl.CostEstimate(flops=0, bytes_accessed=0, transcendentals=0),
    )(store, valid, fresh)


def last_kernel(factor, examples, other_ref, valid_ref, own_ref, fresh_other, fresh_own, out_ref):
    total = own_ref[...] + dot_t(valid_ref[...], other_ref[...])
    out_ref[...] = (total.T * factor).astype(out_ref.dtype)

    @pl.when(pl.program_id(0) == 0)
    def _():
        n = fresh_own.shape[0]
        value = fresh_own[...] + dot_t(fresh_other[...], valid_ref[...])
        value = (value * factor).astype(out_ref.dtype)
        row = lax.broadcasted_iota(jnp.int32, value.shape, 0)
        out_ref[:n] = jnp.where(row < examples, value, out_ref[:n])


def last_scores(other, valid, own, fresh_other, fresh_own, factor, examples):
    rows, half = other.shape
    columns = valid.shape[0]
    return pl.pallas_call(
        functools.partial(last_kernel, factor, examples),
        grid=(rows // BLOCK,),
        in_specs=[
            pl.BlockSpec((BLOCK, half), lambda i: (i, 0)),
            pl.BlockSpec((columns, half), lambda i: (0, 1), pipeline_mode=pl.Buffered(1)),
            pl.BlockSpec((columns, BLOCK), lambda i: (0, i)),
            pl.BlockSpec(fresh_other.shape, lambda i: (0, 0)),
            pl.BlockSpec(fresh_own.shape, lambda i: (0, 0)),
        ],
        out_specs=pl.BlockSpec((BLOCK, columns), lambda i: (i, 0)),
        out_shape=jax.ShapeDtypeStruct((rows, columns), jnp.bfloat16),
        compiler_params=pltpu.CompilerParams(vmem_limit_bytes=24 * MIB),
        cost_estimate=pl.CostEstimate(flops=0, bytes_accessed=0, transcendentals=0),
    )(other, valid, own, fresh_other, fresh_own)


def fill_kernel(table_ref, mine_ref, twin_ref, *refs):
    out_ref = refs[-1]
    n = pl.num_programs(0) // 2

    @pl.when(pl.program_id(0) < n)
    def _():
        out_ref[:, 0, 0] = mine_ref[0]

    @pl.when(pl.program_id(0) >= n)
    def _():
        out_ref[:, 0, 0] = twin_ref[0]


def filled(whole, shape, mine, twin, table):
    nx, _, _, rows_v, width = shape
    n = mine.shape[0] // (nx * rows_v)
    operands = [table, mine.reshape(n, nx, rows_v, width), twin.reshape(n, nx, rows_v, width)]
    specs = [
        pl.BlockSpec((1, nx, rows_v, width), lambda s, t: (jnp.minimum(s, n - 1), 0, 0, 0)),
        pl.BlockSpec((1, nx, rows_v, width), lambda s, t: (jnp.maximum(s - n, 0), 0, 0, 0)),
    ]
    if whole is not None:
        operands.append(whole)
        specs.append(pl.BlockSpec(memory_space=pl.ANY))
    return pl.pallas_call(
        fill_kernel,
        grid_spec=pltpu.PrefetchScalarGridSpec(
            num_scalar_prefetch=1,
            grid=(2 * n,),
            in_specs=specs,
            out_specs=pl.BlockSpec(
                (nx, 1, 1, rows_v, width), lambda s, t: (0, t[2 * s], t[2 * s + 1], 0, 0)
            ),
        ),
        out_shape=jax.ShapeDtypeStruct(shape, mine.dtype),
        input_output_aliases={} if whole is None else {3: 0},
        compiler_params=pltpu.CompilerParams(vmem_limit_bytes=16 * MIB),
        cost_estimate=pl.CostEstimate(
            flops=FILL_FLOPS, bytes_accessed=4 * n * nx * rows_v * width, transcendentals=0
        ),
    )(*operands)


def local(inputs, out_grads, proj_in, proj_out, store, valid, owner):
    yl, x, z, c, yh = (lax.axis_index(a) for a in ("yl", "x", "z", "c", "yh"))
    nx, nz, nc = SIZES["x"], SIZES["z"], SIZES["c"]
    examples = inputs.shape[0]
    rows_v, half = valid.shape
    rows_b = nx * rows_v
    rows_s = nc * examples

    def at(y):
        return (y % 2) * 2 + y // 2

    near = lax.ppermute(valid, ("yl", "yh"), [(at(i), at(j)) for i, j in ((0, 1), (1, 3), (2, 0), (3, 2))])
    cross = lax.ppermute(valid, ("yl", "yh"), [(at(1), at(2)), (at(2), at(1))])
    here = jnp.concatenate(
        [jnp.where(yl == yh, valid, near), jnp.where(yl == yh, near, cross)], axis=1
    )

    known = make_sketch(inputs, out_grads, proj_in, proj_out)
    known = jnp.concatenate([known, paired(known, "yl", 1)], axis=0)

    known, waited = lax.optimization_barrier((known, store))
    other = shifted(waited, "yh", 1)

    known = jnp.concatenate([known, paired(known, "x", 1)], axis=0)
    known, here = lax.optimization_barrier((known, here))

    pieces = [here] + [shifted(here, "x", k) for k in range(1, nx)]
    block = jnp.zeros((nx, rows_v, 2 * half), valid.dtype)
    for k, piece in enumerate(pieces):
        block = lax.dynamic_update_slice(block, piece[None], ((x - k) % nx, 0, 0))
    block = block.reshape(rows_b, 2 * half)

    whole = [None]

    def fill_all(mine, twin, steps):
        froms = [((z + step) % nz, c) for step in steps] + [((z + step) % nz, 1 - c) for step in steps]
        table = jnp.stack([part for pair in froms for part in pair]).astype(jnp.int32)
        shape = (nx, nz, nc, rows_v, 2 * half)
        whole[0] = filled(whole[0], shape, mine, twin, table)

    def both_ways(ahead, back):
        ahead, back = lax.optimization_barrier((ahead, back))
        return lax.optimization_barrier((shifted(ahead, "z", 1), shifted(back, "z", -1)))

    twin = shifted(block, "c", 1)
    up, down = both_ways(block, block)
    fill_all(block, twin, (0,))

    known = jnp.concatenate([known, paired(known, "x", 2)], axis=0)

    def dp_index(yl_, x_, z_, c_):
        return ((yl_ * nx + x_) * nz + z_) * nc + c_

    each = jnp.arange(examples, dtype=jnp.int32)
    from_x = x ^ jnp.arange(nx, dtype=jnp.int32)
    from_yl = yl ^ jnp.arange(2, dtype=jnp.int32)
    example = dp_index(from_yl[None, :, None], from_x[:, None, None], z, c) * examples + each
    slot_of = owner[example.reshape(-1)]
    to_z = (z + jnp.arange(nz, dtype=jnp.int32)) % nz
    to = dp_index(yl, x, to_z[:, None], jnp.arange(nc, dtype=jnp.int32))
    slot = (to[:, :, None] * examples + each).reshape(-1)
    picker = (slot[:, None] == slot_of[None, :]).astype(jnp.bfloat16)
    shares = jnp.dot(picker, known, preferred_element_type=jnp.float32).astype(jnp.bfloat16)
    shares = jnp.pad(shares, ((0, 0), (0, half)))

    def share(offset):
        first = (offset % nz) * rows_s
        return shares[first : first + rows_s]

    for k in (1, 2, 3):
        mine = jnp.concatenate([up[:rows_b], down[:rows_b]], axis=0)
        twin = shifted(mine, "c", 1)
        s_up, s_down = share(4 - k), share(k - 4)
        if k > 1:
            s_up, s_down = s_up + up[rows_b:], s_down + down[rows_b:]
        if k < 3:
            ahead, back = up[:rows_b], down[:rows_b]
        else:
            ahead, back = up[: rows_b // 2], down[rows_b // 2 : rows_b]
        up, down = both_ways(
            jnp.concatenate([ahead, s_up], axis=0), jnp.concatenate([back, s_down], axis=0)
        )
        fill_all(mine, twin, (-k, k))
        if k == 1:
            s_far = shifted(share(4), "z", 4)
    cut = rows_b // 2
    far = jnp.concatenate([up[:cut], down[:cut]], axis=0)
    fresh = (up[cut:] + down[cut:]) + (s_far + share(0))
    fresh = fresh.reshape(nc, examples, 2 * half)
    leave = jnp.where(c == 0, fresh[1], fresh[0])
    got = shifted(jnp.concatenate([far, leave], axis=0), "c", 1)
    fill_all(far, got[:rows_b], (4,))
    fresh = jnp.where(c == 0, fresh[0], fresh[1]) + got[rows_b:]

    fresh = jnp.pad(fresh[:, :half], ((0, 16 - examples), (0, 0)))
    fresh_other = shifted(fresh, "yh", 1)
    valid_all = whole[0].reshape(nx * nz * nc * rows_v, 2 * half)
    own, fresh_own = own_scores(store, valid_all, fresh)
    other, own = lax.optimization_barrier((other, own))
    return last_scores(
        other, valid_all, own, fresh_other, fresh_own, (2 * half) ** (-0.5), examples
    )


def solution(mesh):
    fine = Mesh(mesh.devices.reshape(2, 4, 8, 2, 2), ("yl", "x", "z", "c", "yh"))
    return jax.shard_map(
        local,
        mesh=fine,
        in_specs=(
            P(DP, None, None),
            P(DP, None, None),
            P(),
            P(None, "yh"),
            P(DP, "yh"),
            P(DP, "yh"),
            P(),
        ),
        out_specs=P(DP, "yh"),
        check_vma=False,
    )
```

time: 579 us -> 116 us (0.20)
  waiting for transfers between devices: 533 us -> 37.8 us
  starting transfers between devices: 0.08 us -> 47.9 us
  Pallas kernels: 0 us -> 19.4 us
  matrix products: 18.9 us -> 3.22 us
  between operations: 13.2 us -> 0.58 us
    all_gather x2 -> x0, waiting for transfers between devices: 427 us -> none  [the longest x1 221 us: local(): lax.all_gather(valid, 'dp', axis=0, tiled=True)]
    reduce_scatter x1 -> x0, waiting for transfers between devices: 105 us -> none  [local(): lax.psum_scatter(partial_scores, 'group', scatter_dimension=1, tiled=True)]
    ppermute x0 -> x24, starting transfers between devices: none -> 47.9 us  [the longest x19 40 us: shifted(): lax.ppermute(array, axis, [(i, (i + by) % size) for i in range(size)])]
    ppermute x0 -> x24, waiting for transfers between devices: none -> 37.8 us  [the longest x19 37.3 us: shifted(): lax.ppermute(array, axis, [(i, (i + by) % size) for i in range(size)])]
    pallas_call x0 -> x7, Pallas kernels: none -> 19.4 us  [the longest x1 8.08 us: last_scores(): pl.pallas_call(functools.partial(last_kernel, factor, examples), grid=(ro...]
    dot_general x5 -> x4, matrix products: 18.9 us -> 3.22 us  [the longest x1 2.05 us: make_sketch(): jnp.dot(inputs.reshape(examples * length, width_in), proj_in, preferred_e...]
  transfers between devices with their start and end apart: 3 -> 24, of which waited for: 3 -> 11; matrix products, arithmetic and copies ran while one was open for 1% -> 5% of each run, Pallas kernels for 0% -> 10%
where the time goes in v3:
time: 116 us; the launch traced here: 114 us
  starting transfers between devices  47.9 us (41%)
  waiting for transfers between devices  37.8 us (33%)
  Pallas kernels  19.4 us (17%)
  local copies, waits for them, and re-layouts  4.04 us (3%)
  matrix products  3.22 us (3%)
  other arithmetic  1.21 us (1%)
    ppermute x19, starting transfers between devices, shifted(): lax.ppermute(array, axis, [(i, (i + by) % size) for i in range(size)])  40 us
    ppermute x19, waiting for transfers between devices, shifted(): lax.ppermute(array, axis, [(i, (i + by) % size) for i in range(size)])  37.3 us
    pallas_call x1, Pallas kernels, last_scores(): pl.pallas_call(functools.partial(last_kernel, factor, examples), grid=(ro...  8.08 us
    pallas_call x1, Pallas kernels, own_scores(): pl.pallas_call(own_kernel, grid=(rows // BLOCK,), in_specs=[pl.BlockSpec(...  6.98 us
    ppermute x3, starting transfers between devices, paired(): return lax.ppermute(array, axis, [(i, i ^ bit) for i in range(size)])  5.12 us
    pallas_call x5, Pallas kernels, filled(): pl.pallas_call(fill_kernel, grid_spec=pltpu.PrefetchScalarGridSpec(num_sc...  4.38 us
  transfers between devices with their start and end apart: 24, of which 11 were waited for; matrix products, arithmetic and copies ran while one was open for 5% of the time, Pallas kernels for 10%

profile of v3, /device:TPU:1, one launch (start us, length us, event | category | flops | bytes accessed | tf_op | source)
XLA Modules:
  0.0 114.2 jit_solution(6917864850684510727)
XLA Ops:
  0.0 2.1 %collective-permute-start.3 = (bf16[16,2048]{1,0:T(8,128)(2,1)}, bf16[16,2048]{1,0:T(8,128)(2,1)S(1)}, u32[]{:S(2)}, u32[]{:S(2)}) collective-permute-start(bf16[16,2048]{1,0:T(8,128)(2,1)} %param.12), channel_id=1, source_target_pairs={{0,128},{128,129},{1,0},{129,1},{2,130},{130,131},{3,2},{131,3},{4... | collective-permute-start | bytes 196616 | tf_op jit(solution)/shard_map/ppermute | solution.py:171
  2.1 0.7 collective-permute-start.4
  2.8 2.0 %convolution_convert_fusion.1 = bf16[128,64]{0,1:T(8,128)(2,1)S(1)} fusion(bf16[128,5120]{1,0:T(8,128)(2,1)} %bitcast.58, bf16[5120,64]{0,1:T(8,128)(2,1)} %param.9), kind=kOutput, calls=%fused_computation.4 | convolution fusion | flops 83894272 | bytes 1982464 | tf_op jit(solution)/shard_map/dot_general | solution.py:36
  5.0 0.8 convolution_convert_fusion.2
  5.9 0.1 fusion
  6.2 3.3 %collective-permute-start = (bf16[2,2048]{1,0:T(2,128)(2,1)S(1)}, bf16[2,2048]{1,0:T(2,128)(2,1)S(1)}, u32[]{:S(2)}, u32[]{:S(2)}) collective-permute-start(bf16[2,2048]{1,0:T(2,128)(2,1)S(1)} %convert_element_type.23), channel_id=1, source_target_pairs={{0,128},{128,0},{1,129},{129,1},{2,130},{130,2},{3,131},{131,3},{4... | collective-permute-start | bytes 24584 | tf_op jit(solution)/shard_map/ppermute | solution.py:24
  10.0 0.5 collective-permute-done
  10.5 1.3 %collective-permute-start.2 = (bf16[4,2048]{1,0:T(4,128)(2,1)S(1)}, bf16[4,2048]{1,0:T(4,128)(2,1)S(1)}, u32[]{:S(2)}, u32[]{:S(2)}) collective-permute-start(bf16[4,2048]{1,0:T(4,128)(2,1)S(1)} %pad_maximum_fusion.12), channel_id=1, source_target_pairs={{0,32},{32,0},{64,96},{96,64},{1,33},{33,1},{65,97},{97,65},{2,34}... | collective-permute-start | bytes 49160 | tf_op jit(solution)/shard_map/ppermute | solution.py:24
  12.2 0.7 gather_fusion
  13.1 3.3 %collective-permute-start.1 = (bf16[1024,2048]{1,0:T(8,128)(2,1)}, bf16[1024,2048]{1,0:T(8,128)(2,1)S(1)}, u32[]{:S(2)}, u32[]{:S(2)}) collective-permute-start(bf16[1024,2048]{1,0:T(8,128)(2,1)} %store_ref.1), channel_id=1, source_target_pairs={{0,1},{1,0},{2,3},{3,2},{4,5},{5,4},{6,7},{7,6},{8,9},{9,8},{10,11... | collective-permute-start | bytes 12582920 | tf_op jit(solution)/shard_map/ppermute | solution.py:19
  16.4 0.3 collective-permute-start.5
  16.8 2.7 %collective-permute-start.6 = (bf16[16,4096]{1,0:T(8,128)(2,1)S(1)}, bf16[16,4096]{1,0:T(8,128)(2,1)S(1)}, u32[]{:S(2)}, u32[]{:S(2)}) collective-permute-start(bf16[16,4096]{1,0:T(8,128)(2,1)S(1)} %pad_maximum_fusion.10), channel_id=1, source_target_pairs={{0,64},{32,96},{64,0},{96,32},{1,65},{33,97},{65,1},{97,33},{2,66}... | collective-permute-start | bytes 393224 | tf_op jit(solution)/shard_map/ppermute | solution.py:19
  19.5 1.5 %collective-permute-start.7 = (bf16[16,4096]{1,0:T(8,128)(2,1)S(1)}, bf16[16,4096]{1,0:T(8,128)(2,1)S(1)}, u32[]{:S(2)}, u32[]{:S(2)}) collective-permute-start(bf16[16,4096]{1,0:T(8,128)(2,1)S(1)} %pad_maximum_fusion.10), channel_id=1, source_target_pairs={{0,96},{32,0},{64,32},{96,64},{1,97},{33,1},{65,33},{97,65},{2,98}... | collective-permute-start | bytes 393224 | tf_op jit(solution)/shard_map/ppermute | solution.py:19
  21.0 0.5 collective-permute-start.10
  21.6 0.2 collective-permute-done.5
  21.8 1.7 %collective-permute-done.6 = bf16[16,4096]{1,0:T(8,128)(2,1)S(1)} collective-permute-done((bf16[16,4096]{1,0:T(8,128)(2,1)S(1)}, bf16[16,4096]{1,0:T(8,128)(2,1)S(1)}, u32[]{:S(2)}, u32[]{:S(2)}) %collective-permute-start.6) | collective-permute-done | bytes 131104 | tf_op jit(solution)/shard_map/ppermute | solution.py:19
  23.6 0.2 collective-permute-done.7
  23.8 1.7 %collective-permute-start.8 = (bf16[64,4096]{1,0:T(8,128)(2,1)S(1)}, bf16[64,4096]{1,0:T(8,128)(2,1)S(1)}, u32[]{:S(2)}, u32[]{:S(2)}) collective-permute-start(bf16[64,4096]{1,0:T(8,128)(2,1)S(1)} %bitcast.47), channel_id=1, source_target_pairs={{0,4},{4,8},{8,12},{12,16},{16,20},{20,24},{24,28},{28,0},{1,5},{5... | collective-permute-start | bytes 1572872 | tf_op jit(solution)/shard_map/ppermute | solution.py:19
  25.5 4.0 %collective-permute-start.9 = (bf16[64,4096]{1,0:T(8,128)(2,1)S(1)}, bf16[64,4096]{1,0:T(8,128)(2,1)S(1)}, u32[]{:S(2)}, u32[]{:S(2)}) collective-permute-start(bf16[64,4096]{1,0:T(8,128)(2,1)S(1)} %bitcast.48), channel_id=1, source_target_pairs={{0,28},{4,0},{8,4},{12,8},{16,12},{20,16},{24,20},{28,24},{1,29},{... | collective-permute-start | bytes 1572872 | tf_op jit(solution)/shard_map/ppermute | solution.py:19
  29.6 0.2 convolution_convert_fusion
  29.8 4.0 %collective-permute-start.17 = (bf16[4,4096]{1,0:T(4,128)(2,1)S(1)}, bf16[4,4096]{1,0:T(4,128)(2,1)S(1)}, u32[]{:S(2)}, u32[]{:S(2)}) collective-permute-start(bf16[4,4096]{1,0:T(4,128)(2,1)S(1)} %get-tuple-element.53), channel_id=1, source_target_pairs={{0,16},{4,20},{8,24},{12,28},{16,0},{20,4},{24,8},{28,12},{1,17},{... | collective-permute-start | bytes 98312 | tf_op jit(solution)/shard_map/ppermute | solution.py:19
  33.8 5.0 %collective-permute-start.22 = (bf16[64,4096]{1,0:T(8,128)(2,1)S(1)}, bf16[64,4096]{1,0:T(8,128)(2,1)S(1)}, u32[]{:S(2)}, u32[]{:S(2)}) collective-permute-start(bf16[64,4096]{1,0:T(8,128)(2,1)S(1)} %bitcast.49), channel_id=1, source_target_pairs={{0,2},{2,0},{1,3},{3,1},{4,6},{6,4},{5,7},{7,5},{8,10},{10,8},{9,1... | collective-permute-start | bytes 1572872 | tf_op jit(solution)/shard_map/ppermute | solution.py:19
  38.9 4.3 %collective-permute-start.21 = (bf16[128,4096]{1,0:T(8,128)(2,1)S(1)}, bf16[128,4096]{1,0:T(8,128)(2,1)S(1)}, u32[]{:S(2)}, u32[]{:S(2)}) collective-permute-start(bf16[128,4096]{1,0:T(8,128)(2,1)S(1)} %constant_dynamic-update-slice_fusion), channel_id=1, source_target_pairs={{0,2},{2,0},{1,3},{3,1},{4,6},{6,4},{5,7},{7,5},{8,10},{10,8},{9,1... | collective-permute-start | bytes 3145736 | tf_op jit(solution)/shard_map/ppermute | solution.py:19
  43.4 3.2 %collective-permute-start.12 = (bf16[68,4096]{1,0:T(8,128)(2,1)S(1)}, bf16[68,4096]{1,0:T(8,128)(2,1)S(1)}, u32[]{:S(2)}, u32[]{:S(2)}) collective-permute-start(bf16[68,4096]{1,0:T(8,128)(2,1)S(1)} %get-tuple-element.38), channel_id=1, source_target_pairs={{0,28},{4,0},{8,4},{12,8},{16,12},{20,16},{24,20},{28,24},{1,29},{... | collective-permute-start | bytes 1671176 | tf_op jit(solution)/shard_map/ppermute | solution.py:19
  46.6 0.8 shard_map.73.refs_0_
  47.4 12.8 %collective-permute-done.11 = bf16[68,4096]{1,0:T(8,128)(2,1)S(1)} collective-permute-done((bf16[68,4096]{1,0:T(8,128)(2,1)S(1)}, bf16[68,4096]{1,0:T(8,128)(2,1)S(1)}, u32[]{:S(2)}, u32[]{:S(2)}) %collective-permute-start.11) | collective-permute-done | bytes 557088 | tf_op jit(solution)/shard_map/ppermute | solution.py:19
  60.4 0.9 collective-permute-start.20
  61.4 2.2 %collective-permute-start.13 = (bf16[68,4096]{1,0:T(8,128)(2,1)S(1)}, bf16[68,4096]{1,0:T(8,128)(2,1)S(1)}, u32[]{:S(2)}, u32[]{:S(2)}) collective-permute-start(bf16[68,4096]{1,0:T(8,128)(2,1)S(1)} %pad_maximum_fusion.4), channel_id=1, source_target_pairs={{0,4},{4,8},{8,12},{12,16},{16,20},{20,24},{24,28},{28,0},{1,5},{5... | collective-permute-start | bytes 1671176 | tf_op jit(solution)/shard_map/ppermute | solution.py:19
  63.6 0.8 collective-permute-start.14
  64.3 1.0 shard_map.74.refs_0_
  65.3 12.5 %collective-permute-done.13 = bf16[68,4096]{1,0:T(8,128)(2,1)S(1)} collective-permute-done((bf16[68,4096]{1,0:T(8,128)(2,1)S(1)}, bf16[68,4096]{1,0:T(8,128)(2,1)S(1)}, u32[]{:S(2)}, u32[]{:S(2)}) %collective-permute-start.13) | collective-permute-done | bytes 557088 | tf_op jit(solution)/shard_map/ppermute | solution.py:19
  77.8 0.4 collective-permute-done.14
  78.2 0.8 copy-done.3
  79.2 1.8 %collective-permute-start.15 = (bf16[36,4096]{1,0:T(8,128)(2,1)S(1)}, bf16[36,4096]{1,0:T(8,128)(2,1)S(1)}, u32[]{:S(2)}, u32[]{:S(2)}) collective-permute-start(bf16[36,4096]{1,0:T(8,128)(2,1)S(1)} %pad_maximum_fusion.8), channel_id=1, source_target_pairs={{0,4},{4,8},{8,12},{12,16},{16,20},{20,24},{24,28},{28,0},{1,5},{5... | collective-permute-start | bytes 884744 | tf_op jit(solution)/shard_map/ppermute | solution.py:19
  80.9 1.0 collective-permute-start.16
  82.0 6.5 %collective-permute-done.15 = bf16[36,4096]{1,0:T(8,128)(2,1)S(1)} collective-permute-done((bf16[36,4096]{1,0:T(8,128)(2,1)S(1)}, bf16[36,4096]{1,0:T(8,128)(2,1)S(1)}, u32[]{:S(2)}, u32[]{:S(2)}) %collective-permute-start.15) | collective-permute-done | bytes 294944 | tf_op jit(solution)/shard_map/ppermute | solution.py:19
  88.6 2.0 %collective-permute-start.19 = (bf16[128,4096]{1,0:T(8,128)(2,1)S(1)}, bf16[128,4096]{1,0:T(8,128)(2,1)S(1)}, u32[]{:S(2)}, u32[]{:S(2)}) collective-permute-start(bf16[128,4096]{1,0:T(8,128)(2,1)S(1)} %pad_maximum_fusion), channel_id=1, source_target_pairs={{0,2},{2,0},{1,3},{3,1},{4,6},{6,4},{5,7},{7,5},{8,10},{10,8},{9,1... | collective-permute-start | bytes 3145736 | tf_op jit(solution)/shard_map/ppermute | solution.py:19
  90.8 0.6 collective-permute-start.18
  91.4 1.0 shard_map.75.refs_0_
  92.4 1.4 %collective-permute-done.18 = bf16[66,4096]{1,0:T(8,128)(2,1)S(1)} collective-permute-done((bf16[66,4096]{1,0:T(8,128)(2,1)S(1)}, bf16[66,4096]{1,0:T(8,128)(2,1)S(1)}, u32[]{:S(2)}, u32[]{:S(2)}) %collective-permute-start.18) | collective-permute-done | bytes 540704 | tf_op jit(solution)/shard_map/ppermute | solution.py:19
  93.8 0.7 collective-permute-start.23
  94.5 1.0 shard_map.76.refs_0_
  95.5 0.8 shard_map.77
  96.2 1.4 %copy-done.1 = bf16[1024,2048]{1,0:T(8,128)(2,1)S(1)} copy-done((bf16[1024,2048]{1,0:T(8,128)(2,1)S(1)}, bf16[1024,2048]{1,0:T(8,128)(2,1)}, u32[]{:S(2)}) %copy-start.1) | copy-done | bytes 4194328
  97.6 7.0 %shard_map.78 = (f32[1024,1024]{1,0:T(8,128)S(1)}, f32[16,1024]{1,0:T(8,128)S(1)}) custom-call(bf16[1024,2048]{1,0:T(8,128)(2,1)S(1)} %copy-done.1, bf16[1024,4096]{1,0:T(8,128)(2,1)S(1)} %bitcast.43, bf16[16,2048]{1,0:T(8,128)(2,1)S(1)} %pad.9.fresh_ref), custom_call_target="tpu_custom_call" | custom-call | tf_op jit(solution)/shard_map/pallas_call | solution.py:63
  104.6 0.1 collective-permute-done.1.other_ref
  104.7 1.4 %collective-permute-done.23.fresh_other = bf16[16,2048]{1,0:T(8,128)(2,1)S(1)} collective-permute-done((bf16[16,2048]{1,0:T(8,128)(2,1)S(1)}, bf16[16,2048]{1,0:T(8,128)(2,1)S(1)}, u32[]{:S(2)}, u32[]{:S(2)}) %collective-permute-start.23) | collective-permute-done | bytes 65568 | tf_op jit(solution)/shard_map/ppermute | solution.py:19
  106.2 8.1 %shard_map.79 = bf16[1024,1024]{1,0:T(8,128)(2,1)} custom-call(bf16[1024,2048]{1,0:T(8,128)(2,1)S(1)} %collective-permute-done.1.other_ref, bf16[1024,4096]{1,0:T(8,128)(2,1)S(1)} %bitcast.44, f32[1024,1024]{1,0:T(8,128)S(1)} %get-tuple-element.51.own_ref, bf16[16,2048]{1,0:T(8,128)(2,1)S(1)} %collective-permute-done.23.fresh_other, ...), custom_call_target="tpu_custom_call" | custom-call | tf_op jit(solution)/shard_map/pallas_call | solution.py:100
  (84 shorter events, 2.5 us)
Async XLA Ops:
  0.0 5.0 %copy-start = (bf16[2,64,8192]{2,1,0:T(8,128)(2,1)S(1)}, bf16[2,64,8192]{2,1,0:T(8,128)(2,1)}, u32[]{:S(2)}) copy-start(bf16[2,64,8192]{2,1,0:T(8,128)(2,1)} %param.8) | copy-start | bytes 6291460
  0.0 5.0 %copy-start.5 = (bf16[8192,32]{0,1:T(8,128)(2,1)S(1)}, bf16[8192,32]{0,1:T(8,128)(2,1)}, u32[]{:S(2)}) copy-start(bf16[8192,32]{0,1:T(8,128)(2,1)} %param.10) | copy-start | bytes 1572868
  0.0 16.3 %collective-permute-start.3 = (bf16[16,2048]{1,0:T(8,128)(2,1)}, bf16[16,2048]{1,0:T(8,128)(2,1)S(1)}, u32[]{:S(2)}, u32[]{:S(2)}) collective-permute-start(bf16[16,2048]{1,0:T(8,128)(2,1)} %param.12), channel_id=1, source_target_pairs={{0,128},{128,129},{1,0},{129,1},{2,130},{130,131},{3,2},{131,3},{4... | collective-permute-start | bytes 196616 | tf_op jit(solution)/shard_map/ppermute | solution.py:171
  2.1 14.2 %collective-permute-start.4 = (bf16[16,2048]{1,0:T(8,128)(2,1)}, bf16[16,2048]{1,0:T(8,128)(2,1)S(1)}, u32[]{:S(2)}, u32[]{:S(2)}) collective-permute-start(bf16[16,2048]{1,0:T(8,128)(2,1)} %param.12), channel_id=1, source_target_pairs={{128,1},{1,128},{130,3},{3,130},{132,5},{5,132},{134,7},{7,134},{1... | collective-permute-start | bytes 196616 | tf_op jit(solution)/shard_map/ppermute | solution.py:172
  5.0 7.2 %copy-start.2 = (s32[256]{0:T(256)S(1)}, s32[256]{0:T(256)}, u32[]{:S(2)}) copy-start(s32[256]{0:T(256)} %param.13) | copy-start | bytes 3076
  5.0 11.4 %copy-start.6 = (bf16[16,2048]{1,0:T(8,128)(2,1)S(1)}, bf16[16,2048]{1,0:T(8,128)(2,1)}, u32[]{:S(2)}) copy-start(bf16[16,2048]{1,0:T(8,128)(2,1)} %param.12) | copy-start | bytes 196612
  6.2 4.3 %collective-permute-start = (bf16[2,2048]{1,0:T(2,128)(2,1)S(1)}, bf16[2,2048]{1,0:T(2,128)(2,1)S(1)}, u32[]{:S(2)}, u32[]{:S(2)}) collective-permute-start(bf16[2,2048]{1,0:T(2,128)(2,1)S(1)} %convert_element_type.23), channel_id=1, source_target_pairs={{0,128},{128,0},{1,129},{129,1},{2,130},{130,2},{3,131},{131,3},{4... | collective-permute-start | bytes 24584 | tf_op jit(solution)/shard_map/ppermute | solution.py:24
  10.5 5.8 %collective-permute-start.2 = (bf16[4,2048]{1,0:T(4,128)(2,1)S(1)}, bf16[4,2048]{1,0:T(4,128)(2,1)S(1)}, u32[]{:S(2)}, u32[]{:S(2)}) collective-permute-start(bf16[4,2048]{1,0:T(4,128)(2,1)S(1)} %pad_maximum_fusion.12), channel_id=1, source_target_pairs={{0,32},{32,0},{64,96},{96,64},{1,33},{33,1},{65,97},{97,65},{2,34}... | collective-permute-start | bytes 49160 | tf_op jit(solution)/shard_map/ppermute | solution.py:24
  13.1 91.7 %collective-permute-start.1 = (bf16[1024,2048]{1,0:T(8,128)(2,1)}, bf16[1024,2048]{1,0:T(8,128)(2,1)S(1)}, u32[]{:S(2)}, u32[]{:S(2)}) collective-permute-start(bf16[1024,2048]{1,0:T(8,128)(2,1)} %store_ref.1), channel_id=1, source_target_pairs={{0,1},{1,0},{2,3},{3,2},{4,5},{5,4},{6,7},{7,6},{8,9},{9,8},{10,11... | collective-permute-start | bytes 12582920 | tf_op jit(solution)/shard_map/ppermute | solution.py:19
  16.4 5.4 %collective-permute-start.5 = (bf16[16,4096]{1,0:T(8,128)(2,1)S(1)}, bf16[16,4096]{1,0:T(8,128)(2,1)S(1)}, u32[]{:S(2)}, u32[]{:S(2)}) collective-permute-start(bf16[16,4096]{1,0:T(8,128)(2,1)S(1)} %pad_maximum_fusion.10), channel_id=1, source_target_pairs={{0,32},{32,64},{64,96},{96,0},{1,33},{33,65},{65,97},{97,1},{2,34}... | collective-permute-start | bytes 393224 | tf_op jit(solution)/shard_map/ppermute | solution.py:19
  16.8 6.8 %collective-permute-start.6 = (bf16[16,4096]{1,0:T(8,128)(2,1)S(1)}, bf16[16,4096]{1,0:T(8,128)(2,1)S(1)}, u32[]{:S(2)}, u32[]{:S(2)}) collective-permute-start(bf16[16,4096]{1,0:T(8,128)(2,1)S(1)} %pad_maximum_fusion.10), channel_id=1, source_target_pairs={{0,64},{32,96},{64,0},{96,32},{1,65},{33,97},{65,1},{97,33},{2,66}... | collective-permute-start | bytes 393224 | tf_op jit(solution)/shard_map/ppermute | solution.py:19
  19.5 4.3 %collective-permute-start.7 = (bf16[16,4096]{1,0:T(8,128)(2,1)S(1)}, bf16[16,4096]{1,0:T(8,128)(2,1)S(1)}, u32[]{:S(2)}, u32[]{:S(2)}) collective-permute-start(bf16[16,4096]{1,0:T(8,128)(2,1)S(1)} %pad_maximum_fusion.10), channel_id=1, source_target_pairs={{0,96},{32,0},{64,32},{96,64},{1,97},{33,1},{65,33},{97,65},{2,98}... | collective-permute-start | bytes 393224 | tf_op jit(solution)/shard_map/ppermute | solution.py:19
  21.0 8.5 %collective-permute-start.10 = (bf16[8,2048]{1,0:T(8,128)(2,1)S(1)}, bf16[8,2048]{1,0:T(8,128)(2,1)S(1)}, u32[]{:S(2)}, u32[]{:S(2)}) collective-permute-start(bf16[8,2048]{1,0:T(8,128)(2,1)S(1)} %pad_maximum_fusion.11), channel_id=1, source_target_pairs={{0,64},{32,96},{64,0},{96,32},{1,65},{33,97},{65,1},{97,33},{2,66}... | collective-permute-start | bytes 98312 | tf_op jit(solution)/shard_map/ppermute | solution.py:24
  23.8 15.0 %collective-permute-start.8 = (bf16[64,4096]{1,0:T(8,128)(2,1)S(1)}, bf16[64,4096]{1,0:T(8,128)(2,1)S(1)}, u32[]{:S(2)}, u32[]{:S(2)}) collective-permute-start(bf16[64,4096]{1,0:T(8,128)(2,1)S(1)} %bitcast.47), channel_id=1, source_target_pairs={{0,4},{4,8},{8,12},{12,16},{16,20},{20,24},{24,28},{28,0},{1,5},{5... | collective-permute-start | bytes 1572872 | tf_op jit(solution)/shard_map/ppermute | solution.py:19
  25.5 13.3 %collective-permute-start.9 = (bf16[64,4096]{1,0:T(8,128)(2,1)S(1)}, bf16[64,4096]{1,0:T(8,128)(2,1)S(1)}, u32[]{:S(2)}, u32[]{:S(2)}) collective-permute-start(bf16[64,4096]{1,0:T(8,128)(2,1)S(1)} %bitcast.48), channel_id=1, source_target_pairs={{0,28},{4,0},{8,4},{12,8},{16,12},{20,16},{24,20},{28,24},{1,29},{... | collective-permute-start | bytes 1572872 | tf_op jit(solution)/shard_map/ppermute | solution.py:19
  29.8 60.8 %collective-permute-start.17 = (bf16[4,4096]{1,0:T(4,128)(2,1)S(1)}, bf16[4,4096]{1,0:T(4,128)(2,1)S(1)}, u32[]{:S(2)}, u32[]{:S(2)}) collective-permute-start(bf16[4,4096]{1,0:T(4,128)(2,1)S(1)} %get-tuple-element.53), channel_id=1, source_target_pairs={{0,16},{4,20},{8,24},{12,28},{16,0},{20,4},{24,8},{28,12},{1,17},{... | collective-permute-start | bytes 98312 | tf_op jit(solution)/shard_map/ppermute | solution.py:19
  33.8 9.6 %collective-permute-start.22 = (bf16[64,4096]{1,0:T(8,128)(2,1)S(1)}, bf16[64,4096]{1,0:T(8,128)(2,1)S(1)}, u32[]{:S(2)}, u32[]{:S(2)}) collective-permute-start(bf16[64,4096]{1,0:T(8,128)(2,1)S(1)} %bitcast.49), channel_id=1, source_target_pairs={{0,2},{2,0},{1,3},{3,1},{4,6},{6,4},{5,7},{7,5},{8,10},{10,8},{9,1... | collective-permute-start | bytes 1572872 | tf_op jit(solution)/shard_map/ppermute | solution.py:19
  38.9 24.6 %collective-permute-start.21 = (bf16[128,4096]{1,0:T(8,128)(2,1)S(1)}, bf16[128,4096]{1,0:T(8,128)(2,1)S(1)}, u32[]{:S(2)}, u32[]{:S(2)}) collective-permute-start(bf16[128,4096]{1,0:T(8,128)(2,1)S(1)} %constant_dynamic-update-slice_fusion), channel_id=1, source_target_pairs={{0,2},{2,0},{1,3},{3,1},{4,6},{6,4},{5,7},{7,5},{8,10},{10,8},{9,1... | collective-permute-start | bytes 3145736 | tf_op jit(solution)/shard_map/ppermute | solution.py:19
  43.3 16.9 %collective-permute-start.11 = (bf16[68,4096]{1,0:T(8,128)(2,1)S(1)}, bf16[68,4096]{1,0:T(8,128)(2,1)S(1)}, u32[]{:S(2)}, u32[]{:S(2)}) collective-permute-start(bf16[68,4096]{1,0:T(8,128)(2,1)S(1)} %get-tuple-element.37), channel_id=1, source_target_pairs={{0,4},{4,8},{8,12},{12,16},{16,20},{20,24},{24,28},{28,0},{1,5},{5... | collective-permute-start | bytes 1671176 | tf_op jit(solution)/shard_map/ppermute | solution.py:19
  43.4 16.8 %collective-permute-start.12 = (bf16[68,4096]{1,0:T(8,128)(2,1)S(1)}, bf16[68,4096]{1,0:T(8,128)(2,1)S(1)}, u32[]{:S(2)}, u32[]{:S(2)}) collective-permute-start(bf16[68,4096]{1,0:T(8,128)(2,1)S(1)} %get-tuple-element.38), channel_id=1, source_target_pairs={{0,28},{4,0},{8,4},{12,8},{16,12},{20,16},{24,20},{28,24},{1,29},{... | collective-permute-start | bytes 1671176 | tf_op jit(solution)/shard_map/ppermute | solution.py:19
  60.4 31.0 %collective-permute-start.20 = (bf16[128,4096]{1,0:T(8,128)(2,1)S(1)}, bf16[128,4096]{1,0:T(8,128)(2,1)S(1)}, u32[]{:S(2)}, u32[]{:S(2)}) collective-permute-start(bf16[128,4096]{1,0:T(8,128)(2,1)S(1)} %pad_maximum_fusion.1), channel_id=1, source_target_pairs={{0,2},{2,0},{1,3},{3,1},{4,6},{6,4},{5,7},{7,5},{8,10},{10,8},{9,1... | collective-permute-start | bytes 3145736 | tf_op jit(solution)/shard_map/ppermute | solution.py:19
  61.4 16.4 %collective-permute-start.13 = (bf16[68,4096]{1,0:T(8,128)(2,1)S(1)}, bf16[68,4096]{1,0:T(8,128)(2,1)S(1)}, u32[]{:S(2)}, u32[]{:S(2)}) collective-permute-start(bf16[68,4096]{1,0:T(8,128)(2,1)S(1)} %pad_maximum_fusion.4), channel_id=1, source_target_pairs={{0,4},{4,8},{8,12},{12,16},{16,20},{20,24},{24,28},{28,0},{1,5},{5... | collective-permute-start | bytes 1671176 | tf_op jit(solution)/shard_map/ppermute | solution.py:19
  63.6 14.6 %collective-permute-start.14 = (bf16[68,4096]{1,0:T(8,128)(2,1)S(1)}, bf16[68,4096]{1,0:T(8,128)(2,1)S(1)}, u32[]{:S(2)}, u32[]{:S(2)}) collective-permute-start(bf16[68,4096]{1,0:T(8,128)(2,1)S(1)} %pad_maximum_fusion.5), channel_id=1, source_target_pairs={{0,28},{4,0},{8,4},{12,8},{16,12},{20,16},{24,20},{28,24},{1,29},{... | collective-permute-start | bytes 1671176 | tf_op jit(solution)/shard_map/ppermute | solution.py:19
  77.8 1.2 %copy-start.4 = (bf16[68,4096]{1,0:T(8,128)(2,1)}, bf16[68,4096]{1,0:T(8,128)(2,1)S(1)}, u32[]{:S(2)}) copy-start(bf16[68,4096]{1,0:T(8,128)(2,1)S(1)} %collective-permute-done.13) | copy-start | bytes 1671172
  78.2 0.8 copy-start.3
  79.1 2.9 %slice-start = ((bf16[68,4096]{1,0:T(8,128)(2,1)}), bf16[64,4096]{1,0:T(8,128)(2,1)S(1)}, s32[]{:S(2)}) async-start(bf16[68,4096]{1,0:T(8,128)(2,1)} %copy-done.3), calls=%async_computation | async-start | bytes 1048576 | tf_op jit(solution)/shard_map/slice | solution.py:230
  79.1 2.8 %slice-start.1 = ((bf16[68,4096]{1,0:T(8,128)(2,1)}), bf16[64,4096]{1,0:T(8,128)(2,1)S(1)}, s32[]{:S(2)}) async-start(bf16[68,4096]{1,0:T(8,128)(2,1)} %copy-done.4), calls=%async_computation.1 | async-start | bytes 1048576 | tf_op jit(solution)/shard_map/slice | solution.py:230
  79.2 9.4 %collective-permute-start.15 = (bf16[36,4096]{1,0:T(8,128)(2,1)S(1)}, bf16[36,4096]{1,0:T(8,128)(2,1)S(1)}, u32[]{:S(2)}, u32[]{:S(2)}) collective-permute-start(bf16[36,4096]{1,0:T(8,128)(2,1)S(1)} %pad_maximum_fusion.8), channel_id=1, source_target_pairs={{0,4},{4,8},{8,12},{12,16},{16,20},{20,24},{24,28},{28,0},{1,5},{5... | collective-permute-start | bytes 884744 | tf_op jit(solution)/shard_map/ppermute | solution.py:19
  80.9 9.7 %collective-permute-start.16 = (bf16[36,4096]{1,0:T(8,128)(2,1)S(1)}, bf16[36,4096]{1,0:T(8,128)(2,1)S(1)}, u32[]{:S(2)}, u32[]{:S(2)}) collective-permute-start(bf16[36,4096]{1,0:T(8,128)(2,1)S(1)} %pad_maximum_fusion.9), channel_id=1, source_target_pairs={{0,28},{4,0},{8,4},{12,8},{16,12},{20,16},{24,20},{28,24},{1,29},{... | collective-permute-start | bytes 884744 | tf_op jit(solution)/shard_map/ppermute | solution.py:19
  88.6 5.9 %collective-permute-start.19 = (bf16[128,4096]{1,0:T(8,128)(2,1)S(1)}, bf16[128,4096]{1,0:T(8,128)(2,1)S(1)}, u32[]{:S(2)}, u32[]{:S(2)}) collective-permute-start(bf16[128,4096]{1,0:T(8,128)(2,1)S(1)} %pad_maximum_fusion), channel_id=1, source_target_pairs={{0,2},{2,0},{1,3},{3,1},{4,6},{6,4},{5,7},{7,5},{8,10},{10,8},{9,1... | collective-permute-start | bytes 3145736 | tf_op jit(solution)/shard_map/ppermute | solution.py:19
  90.8 2.9 %collective-permute-start.18 = (bf16[66,4096]{1,0:T(8,128)(2,1)S(1)}, bf16[66,4096]{1,0:T(8,128)(2,1)S(1)}, u32[]{:S(2)}, u32[]{:S(2)}) collective-permute-start(bf16[66,4096]{1,0:T(8,128)(2,1)S(1)} %pad_maximum_fusion.6), channel_id=1, source_target_pairs={{0,2},{2,0},{1,3},{3,1},{4,6},{6,4},{5,7},{7,5},{8,10},{10,8},{9,1... | collective-permute-start | bytes 1622024 | tf_op jit(solution)/shard_map/ppermute | solution.py:19
  93.8 12.4 %collective-permute-start.23 = (bf16[16,2048]{1,0:T(8,128)(2,1)S(1)}, bf16[16,2048]{1,0:T(8,128)(2,1)S(1)}, u32[]{:S(2)}, u32[]{:S(2)}) collective-permute-start(bf16[16,2048]{1,0:T(8,128)(2,1)S(1)} %pad.9.fresh_ref), channel_id=1, source_target_pairs={{0,1},{1,0},{2,3},{3,2},{4,5},{5,4},{6,7},{7,6},{8,9},{9,8},{10,11... | collective-permute-start | bytes 196616 | tf_op jit(solution)/shard_map/ppermute | solution.py:19
  95.5 2.2 %copy-start.1 = (bf16[1024,2048]{1,0:T(8,128)(2,1)S(1)}, bf16[1024,2048]{1,0:T(8,128)(2,1)}, u32[]{:S(2)}) copy-start(bf16[1024,2048]{1,0:T(8,128)(2,1)} %store_ref.1) | copy-start | bytes 12582916

commit v4 on v3

--- a/solution.py
+++ b/solution.py
@@ -50,66 +50,62 @@
 
 
 def own_kernel(store_ref, valid_ref, fresh_ref, out_ref, fresh_out_ref):
-    out_ref[...] = dot_t(valid_ref[...], store_ref[...])
-
-    @pl.when(pl.program_id(0) == 0)
-    def _():
-        fresh_out_ref[...] = dot_t(fresh_ref[...], valid_ref[...])
+    out_ref[...] = dot_t(store_ref[...], valid_ref[...])
+    fresh_out_ref[...] = dot_t(fresh_ref[...], valid_ref[...])
 
 
 def own_scores(store, valid, fresh):
     rows, half = store.shape
     columns = valid.shape[0]
+    whole = lambda array: pl.BlockSpec(array.shape, lambda i: (0, 0), pipeline_mode=pl.Buffered(1))
     return pl.pallas_call(
         own_kernel,
-        grid=(rows // BLOCK,),
+        grid=(columns // BLOCK,),
         in_specs=[
+            whole(store),
             pl.BlockSpec((BLOCK, half), lambda i: (i, 0)),
-            pl.BlockSpec((columns, half), lambda i: (0, 0), pipeline_mode=pl.Buffered(1)),
-            pl.BlockSpec(fresh.shape, lambda i: (0, 0)),
+            whole(fresh),
         ],
         out_specs=[
-            pl.BlockSpec((columns, BLOCK), lambda i: (0, i)),
-            pl.BlockSpec((fresh.shape[0], columns), lambda i: (0, 0)),
+            pl.BlockSpec((rows, BLOCK), lambda i: (0, i)),
+            pl.BlockSpec((fresh.shape[0], BLOCK), lambda i: (0, i)),
         ],
         out_shape=[
-            jax.ShapeDtypeStruct((columns, rows), jnp.float32),
+            jax.ShapeDtypeStruct((rows, columns), jnp.float32),
             jax.ShapeDtypeStruct((fresh.shape[0], columns), jnp.float32),
         ],
-        compiler_params=pltpu.CompilerParams(vmem_limit_bytes=20 * MIB),
+        compiler_params=pltpu.CompilerParams(vmem_limit_bytes=16 * MIB),
         cost_estimate=pl.CostEstimate(flops=0, bytes_accessed=0, transcendentals=0),
     )(store, valid, fresh)
 
 
 def last_kernel(factor, examples, other_ref, valid_ref, own_ref, fresh_other, fresh_own, out_ref):
-    total = own_ref[...] + dot_t(valid_ref[...], other_ref[...])
-    out_ref[...] = (total.T * factor).astype(out_ref.dtype)
-
-    @pl.when(pl.program_id(0) == 0)
-    def _():
-        n = fresh_own.shape[0]
-        value = fresh_own[...] + dot_t(fresh_other[...], valid_ref[...])
-        value = (value * factor).astype(out_ref.dtype)
-        row = lax.broadcasted_iota(jnp.int32, value.shape, 0)
-        out_ref[:n] = jnp.where(row < examples, value, out_ref[:n])
+    total = own_ref[...] + dot_t(other_ref[...], valid_ref[...])
+    out_ref[...] = (total * factor).astype(out_ref.dtype)
+    n = fresh_own.shape[0]
+    value = fresh_own[...] + dot_t(fresh_other[...], valid_ref[...])
+    value = (value * factor).astype(out_ref.dtype)
+    row = lax.broadcasted_iota(jnp.int32, value.shape, 0)
+    out_ref[:n] = jnp.where(row < examples, value, out_ref[:n])
 
 
 def last_scores(other, valid, own, fresh_other, fresh_own, factor, examples):
     rows, half = other.shape
     columns = valid.shape[0]
+    whole = lambda array: pl.BlockSpec(array.shape, lambda i: (0, 0), pipeline_mode=pl.Buffered(1))
     return pl.pallas_call(
         functools.partial(last_kernel, factor, examples),
-        grid=(rows // BLOCK,),
+        grid=(columns // BLOCK,),
         in_specs=[
-            pl.BlockSpec((BLOCK, half), lambda i: (i, 0)),
-            pl.BlockSpec((columns, half), lambda i: (0, 1), pipeline_mode=pl.Buffered(1)),
-            pl.BlockSpec((columns, BLOCK), lambda i: (0, i)),
-            pl.BlockSpec(fresh_other.shape, lambda i: (0, 0)),
-            pl.BlockSpec(fresh_own.shape, lambda i: (0, 0)),
-        ],
-        out_specs=pl.BlockSpec((BLOCK, columns), lambda i: (i, 0)),
+            whole(other),
+            pl.BlockSpec((BLOCK, half), lambda i: (i, 1)),
+            pl.BlockSpec((rows, BLOCK), lambda i: (0, i)),
+            whole(fresh_other),
+            pl.BlockSpec((fresh_own.shape[0], BLOCK), lambda i: (0, i)),
+        ],
+        out_specs=pl.BlockSpec((rows, BLOCK), lambda i: (0, i)),
         out_shape=jax.ShapeDtypeStruct((rows, columns), jnp.bfloat16),
-        compiler_params=pltpu.CompilerParams(vmem_limit_bytes=24 * MIB),
+        compiler_params=pltpu.CompilerParams(vmem_limit_bytes=16 * MIB),
         cost_estimate=pl.CostEstimate(flops=0, bytes_accessed=0, transcendentals=0),
     )(other, valid, own, fresh_other, fresh_own)
 
@@ -150,7 +146,7 @@
         ),
         out_shape=jax.ShapeDtypeStruct(shape, mine.dtype),
         input_output_aliases={} if whole is None else {3: 0},
-        compiler_params=pltpu.CompilerParams(vmem_limit_bytes=16 * MIB),
+        compiler_params=pltpu.CompilerParams(vmem_limit_bytes=8 * MIB),
         cost_estimate=pl.CostEstimate(
             flops=FILL_FLOPS, bytes_accessed=4 * n * nx * rows_v * width, transcendentals=0
         ),
@@ -214,7 +210,8 @@
     from_x = x ^ jnp.arange(nx, dtype=jnp.int32)
     from_yl = yl ^ jnp.arange(2, dtype=jnp.int32)
     example = dp_index(from_yl[None, :, None], from_x[:, None, None], z, c) * examples + each
-    slot_of = owner[example.reshape(-1)]
+    number = jnp.arange(owner.shape[0], dtype=jnp.int32)
+    slot_of = jnp.sum(jnp.where(example.reshape(-1, 1) == number, owner, 0), axis=1)
     to_z = (z + jnp.arange(nz, dtype=jnp.int32)) % nz
     to = dp_index(yl, x, to_z[:, None], jnp.arange(nc, dtype=jnp.int32))
     slot = (to[:, :, None] * examples + each).reshape(-1)

time: 116 us -> 115 us (level)
  transfers between devices with their start and end apart: 24 -> 24, of which waited for: 11 -> 10; matrix products, arithmetic and copies ran while one was open for 5% -> 5% of each run, Pallas kernels for 10% -> 10%
where the time goes in v4:
time: 115 us; the launch traced here: 113 us
  starting transfers between devices  48.6 us (42%)
  waiting for transfers between devices  37.1 us (32%)
  Pallas kernels  19 us (17%)
  local copies, waits for them, and re-layouts  3.37 us (3%)
  matrix products  3.2 us (3%)
  other arithmetic  1.39 us (1%)
    ppermute x19, starting transfers between devices, shifted(): lax.ppermute(array, axis, [(i, (i + by) % size) for i in range(size)])  40.7 us
    ppermute x19, waiting for transfers between devices, shifted(): lax.ppermute(array, axis, [(i, (i + by) % size) for i in range(size)])  36.7 us
    pallas_call x1, Pallas kernels, last_scores(): pl.pallas_call(functools.partial(last_kernel, factor, examples), grid=(co...  7.75 us
    pallas_call x1, Pallas kernels, own_scores(): pl.pallas_call(own_kernel, grid=(columns // BLOCK,), in_specs=[whole(stor...  6.85 us
    ppermute x3, starting transfers between devices, paired(): return lax.ppermute(array, axis, [(i, i ^ bit) for i in range(size)])  5.12 us
    pallas_call x5, Pallas kernels, filled(): pl.pallas_call(fill_kernel, grid_spec=pltpu.PrefetchScalarGridSpec(num_sc...  4.38 us
  transfers between devices with their start and end apart: 24, of which 10 were waited for; matrix products, arithmetic and copies ran while one was open for 5% of the time, Pallas kernels for 10%

profile of v4, /device:TPU:1, one launch (start us, length us, event | category | flops | bytes accessed | tf_op | source)
XLA Modules:
  0.0 113.2 jit_solution(18279954406347483960)
XLA Ops:
  0.0 2.1 %collective-permute-start.3 = (bf16[16,2048]{1,0:T(8,128)(2,1)}, bf16[16,2048]{1,0:T(8,128)(2,1)S(1)}, u32[]{:S(2)}, u32[]{:S(2)}) collective-permute-start(bf16[16,2048]{1,0:T(8,128)(2,1)} %param.12), channel_id=1, source_target_pairs={{0,128},{128,129},{1,0},{129,1},{2,130},{130,131},{3,2},{131,3},{4... | collective-permute-start | bytes 196616 | tf_op jit(solution)/shard_map/ppermute | solution.py:167
  2.1 0.7 collective-permute-start.4
  2.8 2.0 %convolution_convert_fusion.1 = bf16[128,64]{0,1:T(8,128)(2,1)S(1)} fusion(bf16[128,5120]{1,0:T(8,128)(2,1)} %bitcast.56, bf16[5120,64]{0,1:T(8,128)(2,1)} %param.9), kind=kOutput, calls=%fused_computation.3 | convolution fusion | flops 83894272 | bytes 1982464 | tf_op jit(solution)/shard_map/dot_general | solution.py:36
  4.8 0.1 copy.18
  5.0 0.8 convolution_convert_fusion.2
  5.9 0.1 fusion
  6.1 3.3 %collective-permute-start = (bf16[2,2048]{1,0:T(2,128)(2,1)S(1)}, bf16[2,2048]{1,0:T(2,128)(2,1)S(1)}, u32[]{:S(2)}, u32[]{:S(2)}) collective-permute-start(bf16[2,2048]{1,0:T(2,128)(2,1)S(1)} %convert_element_type.23), channel_id=1, source_target_pairs={{0,128},{128,0},{1,129},{129,1},{2,130},{130,2},{3,131},{131,3},{4... | collective-permute-start | bytes 24584 | tf_op jit(solution)/shard_map/ppermute | solution.py:24
  9.9 0.2 select_reduce_fusion
  10.1 0.4 collective-permute-done
  10.5 1.3 %collective-permute-start.2 = (bf16[4,2048]{1,0:T(4,128)(2,1)S(1)}, bf16[4,2048]{1,0:T(4,128)(2,1)S(1)}, u32[]{:S(2)}, u32[]{:S(2)}) collective-permute-start(bf16[4,2048]{1,0:T(4,128)(2,1)S(1)} %pad_maximum_fusion.12), channel_id=1, source_target_pairs={{0,32},{32,0},{64,96},{96,64},{1,33},{33,1},{65,97},{97,65},{2,34}... | collective-permute-start | bytes 49160 | tf_op jit(solution)/shard_map/ppermute | solution.py:24
  12.4 3.3 %collective-permute-start.1 = (bf16[1024,2048]{1,0:T(8,128)(2,1)}, bf16[1024,2048]{1,0:T(8,128)(2,1)S(1)}, u32[]{:S(2)}, u32[]{:S(2)}) collective-permute-start(bf16[1024,2048]{1,0:T(8,128)(2,1)} %store_ref.1), channel_id=1, source_target_pairs={{0,1},{1,0},{2,3},{3,2},{4,5},{5,4},{6,7},{7,6},{8,9},{9,8},{10,11... | collective-permute-start | bytes 12582920 | tf_op jit(solution)/shard_map/ppermute | solution.py:19
  15.7 0.3 collective-permute-start.5
  16.1 2.7 %collective-permute-start.6 = (bf16[16,4096]{1,0:T(8,128)(2,1)S(1)}, bf16[16,4096]{1,0:T(8,128)(2,1)S(1)}, u32[]{:S(2)}, u32[]{:S(2)}) collective-permute-start(bf16[16,4096]{1,0:T(8,128)(2,1)S(1)} %pad_maximum_fusion.10), channel_id=1, source_target_pairs={{0,64},{32,96},{64,0},{96,32},{1,65},{33,97},{65,1},{97,33},{2,66}... | collective-permute-start | bytes 393224 | tf_op jit(solution)/shard_map/ppermute | solution.py:19
  18.8 1.5 %collective-permute-start.7 = (bf16[16,4096]{1,0:T(8,128)(2,1)S(1)}, bf16[16,4096]{1,0:T(8,128)(2,1)S(1)}, u32[]{:S(2)}, u32[]{:S(2)}) collective-permute-start(bf16[16,4096]{1,0:T(8,128)(2,1)S(1)} %pad_maximum_fusion.10), channel_id=1, source_target_pairs={{0,96},{32,0},{64,32},{96,64},{1,97},{33,1},{65,33},{97,65},{2,98}... | collective-permute-start | bytes 393224 | tf_op jit(solution)/shard_map/ppermute | solution.py:19
  20.3 0.5 collective-permute-start.10
  20.9 0.2 collective-permute-done.5
  21.1 1.7 %collective-permute-done.6 = bf16[16,4096]{1,0:T(8,128)(2,1)S(1)} collective-permute-done((bf16[16,4096]{1,0:T(8,128)(2,1)S(1)}, bf16[16,4096]{1,0:T(8,128)(2,1)S(1)}, u32[]{:S(2)}, u32[]{:S(2)}) %collective-permute-start.6) | collective-permute-done | bytes 131104 | tf_op jit(solution)/shard_map/ppermute | solution.py:19
  22.9 0.2 collective-permute-done.7
  23.1 1.7 %collective-permute-start.8 = (bf16[64,4096]{1,0:T(8,128)(2,1)S(1)}, bf16[64,4096]{1,0:T(8,128)(2,1)S(1)}, u32[]{:S(2)}, u32[]{:S(2)}) collective-permute-start(bf16[64,4096]{1,0:T(8,128)(2,1)S(1)} %bitcast.45), channel_id=1, source_target_pairs={{0,4},{4,8},{8,12},{12,16},{16,20},{20,24},{24,28},{28,0},{1,5},{5... | collective-permute-start | bytes 1572872 | tf_op jit(solution)/shard_map/ppermute | solution.py:19
  24.8 4.0 %collective-permute-start.9 = (bf16[64,4096]{1,0:T(8,128)(2,1)S(1)}, bf16[64,4096]{1,0:T(8,128)(2,1)S(1)}, u32[]{:S(2)}, u32[]{:S(2)}) collective-permute-start(bf16[64,4096]{1,0:T(8,128)(2,1)S(1)} %bitcast.46), channel_id=1, source_target_pairs={{0,28},{4,0},{8,4},{12,8},{16,12},{20,16},{24,20},{28,24},{1,29},{... | collective-permute-start | bytes 1572872 | tf_op jit(solution)/shard_map/ppermute | solution.py:19
  28.9 0.2 convolution_convert_fusion
  29.1 4.0 %collective-permute-start.17 = (bf16[4,4096]{1,0:T(4,128)(2,1)S(1)}, bf16[4,4096]{1,0:T(4,128)(2,1)S(1)}, u32[]{:S(2)}, u32[]{:S(2)}) collective-permute-start(bf16[4,4096]{1,0:T(4,128)(2,1)S(1)} %get-tuple-element.53), channel_id=1, source_target_pairs={{0,16},{4,20},{8,24},{12,28},{16,0},{20,4},{24,8},{28,12},{1,17},{... | collective-permute-start | bytes 98312 | tf_op jit(solution)/shard_map/ppermute | solution.py:19
  33.2 5.0 %collective-permute-start.22 = (bf16[64,4096]{1,0:T(8,128)(2,1)S(1)}, bf16[64,4096]{1,0:T(8,128)(2,1)S(1)}, u32[]{:S(2)}, u32[]{:S(2)}) collective-permute-start(bf16[64,4096]{1,0:T(8,128)(2,1)S(1)} %bitcast.47), channel_id=1, source_target_pairs={{0,2},{2,0},{1,3},{3,1},{4,6},{6,4},{5,7},{7,5},{8,10},{10,8},{9,1... | collective-permute-start | bytes 1572872 | tf_op jit(solution)/shard_map/ppermute | solution.py:19
  38.2 4.3 %collective-permute-start.21 = (bf16[128,4096]{1,0:T(8,128)(2,1)S(1)}, bf16[128,4096]{1,0:T(8,128)(2,1)S(1)}, u32[]{:S(2)}, u32[]{:S(2)}) collective-permute-start(bf16[128,4096]{1,0:T(8,128)(2,1)S(1)} %constant_dynamic-update-slice_fusion), channel_id=1, source_target_pairs={{0,2},{2,0},{1,3},{3,1},{4,6},{6,4},{5,7},{7,5},{8,10},{10,8},{9,1... | collective-permute-start | bytes 3145736 | tf_op jit(solution)/shard_map/ppermute | solution.py:19
  42.7 3.2 %collective-permute-start.12 = (bf16[68,4096]{1,0:T(8,128)(2,1)S(1)}, bf16[68,4096]{1,0:T(8,128)(2,1)S(1)}, u32[]{:S(2)}, u32[]{:S(2)}) collective-permute-start(bf16[68,4096]{1,0:T(8,128)(2,1)S(1)} %get-tuple-element.38), channel_id=1, source_target_pairs={{0,28},{4,0},{8,4},{12,8},{16,12},{20,16},{24,20},{28,24},{1,29},{... | collective-permute-start | bytes 1671176 | tf_op jit(solution)/shard_map/ppermute | solution.py:19
  45.9 0.8 shard_map.73.refs_0_
  46.7 12.8 %collective-permute-done.11 = bf16[68,4096]{1,0:T(8,128)(2,1)S(1)} collective-permute-done((bf16[68,4096]{1,0:T(8,128)(2,1)S(1)}, bf16[68,4096]{1,0:T(8,128)(2,1)S(1)}, u32[]{:S(2)}, u32[]{:S(2)}) %collective-permute-start.11) | collective-permute-done | bytes 557088 | tf_op jit(solution)/shard_map/ppermute | solution.py:19
  59.7 0.9 collective-permute-start.20
  60.7 2.2 %collective-permute-start.13 = (bf16[68,4096]{1,0:T(8,128)(2,1)S(1)}, bf16[68,4096]{1,0:T(8,128)(2,1)S(1)}, u32[]{:S(2)}, u32[]{:S(2)}) collective-permute-start(bf16[68,4096]{1,0:T(8,128)(2,1)S(1)} %pad_maximum_fusion.4), channel_id=1, source_target_pairs={{0,4},{4,8},{8,12},{12,16},{16,20},{20,24},{24,28},{28,0},{1,5},{5... | collective-permute-start | bytes 1671176 | tf_op jit(solution)/shard_map/ppermute | solution.py:19
  62.9 0.8 collective-permute-start.14
  63.7 1.0 shard_map.74.refs_0_
  64.6 12.5 %collective-permute-done.13 = bf16[68,4096]{1,0:T(8,128)(2,1)S(1)} collective-permute-done((bf16[68,4096]{1,0:T(8,128)(2,1)S(1)}, bf16[68,4096]{1,0:T(8,128)(2,1)S(1)}, u32[]{:S(2)}, u32[]{:S(2)}) %collective-permute-start.13) | collective-permute-done | bytes 557088 | tf_op jit(solution)/shard_map/ppermute | solution.py:19
  77.1 0.4 collective-permute-done.14
  77.5 0.8 copy-done.2
  78.5 1.8 %collective-permute-start.15 = (bf16[36,4096]{1,0:T(8,128)(2,1)S(1)}, bf16[36,4096]{1,0:T(8,128)(2,1)S(1)}, u32[]{:S(2)}, u32[]{:S(2)}) collective-permute-start(bf16[36,4096]{1,0:T(8,128)(2,1)S(1)} %pad_maximum_fusion.8), channel_id=1, source_target_pairs={{0,4},{4,8},{8,12},{12,16},{16,20},{20,24},{24,28},{28,0},{1,5},{5... | collective-permute-start | bytes 884744 | tf_op jit(solution)/shard_map/ppermute | solution.py:19
  80.2 1.0 collective-permute-start.16
  81.3 6.5 %collective-permute-done.15 = bf16[36,4096]{1,0:T(8,128)(2,1)S(1)} collective-permute-done((bf16[36,4096]{1,0:T(8,128)(2,1)S(1)}, bf16[36,4096]{1,0:T(8,128)(2,1)S(1)}, u32[]{:S(2)}, u32[]{:S(2)}) %collective-permute-start.15) | collective-permute-done | bytes 294944 | tf_op jit(solution)/shard_map/ppermute | solution.py:19
  87.9 2.0 %collective-permute-start.19 = (bf16[128,4096]{1,0:T(8,128)(2,1)S(1)}, bf16[128,4096]{1,0:T(8,128)(2,1)S(1)}, u32[]{:S(2)}, u32[]{:S(2)}) collective-permute-start(bf16[128,4096]{1,0:T(8,128)(2,1)S(1)} %pad_maximum_fusion), channel_id=1, source_target_pairs={{0,2},{2,0},{1,3},{3,1},{4,6},{6,4},{5,7},{7,5},{8,10},{10,8},{9,1... | collective-permute-start | bytes 3145736 | tf_op jit(solution)/shard_map/ppermute | solution.py:19
  90.1 0.6 collective-permute-start.18
  90.7 1.0 shard_map.75.refs_0_
  91.7 1.4 %collective-permute-done.18 = bf16[66,4096]{1,0:T(8,128)(2,1)S(1)} collective-permute-done((bf16[66,4096]{1,0:T(8,128)(2,1)S(1)}, bf16[66,4096]{1,0:T(8,128)(2,1)S(1)}, u32[]{:S(2)}, u32[]{:S(2)}) %collective-permute-start.18) | collective-permute-done | bytes 540704 | tf_op jit(solution)/shard_map/ppermute | solution.py:19
  93.1 1.3 %collective-permute-start.23 = (bf16[16,2048]{1,0:T(8,128)(2,1)S(1)}, bf16[16,2048]{1,0:T(8,128)(2,1)S(1)}, u32[]{:S(2)}, u32[]{:S(2)}) collective-permute-start(bf16[16,2048]{1,0:T(8,128)(2,1)S(1)} %pad.9.fresh_ref), channel_id=1, source_target_pairs={{0,1},{1,0},{2,3},{3,2},{4,5},{5,4},{6,7},{7,6},{8,9},{9,8},{10,11... | collective-permute-start | bytes 196616 | tf_op jit(solution)/shard_map/ppermute | solution.py:19
  94.5 1.0 shard_map.76.refs_0_
  95.5 0.8 shard_map.77
  96.2 1.4 %copy-done.1 = bf16[1024,2048]{1,0:T(8,128)(2,1)S(1)} copy-done((bf16[1024,2048]{1,0:T(8,128)(2,1)S(1)}, bf16[1024,2048]{1,0:T(8,128)(2,1)}, u32[]{:S(2)}) %copy-start.1) | copy-done | bytes 4194328
  97.6 6.8 %shard_map.78 = (f32[1024,1024]{1,0:T(8,128)S(1)}, f32[16,1024]{1,0:T(8,128)S(1)}) custom-call(bf16[1024,2048]{1,0:T(8,128)(2,1)S(1)} %copy-done.1, bf16[1024,4096]{1,0:T(8,128)(2,1)S(1)} %bitcast.41, bf16[16,2048]{1,0:T(8,128)(2,1)S(1)} %pad.9.fresh_ref), custom_call_target="tpu_custom_call" | custom-call | tf_op jit(solution)/shard_map/pallas_call | solution.py:61
  104.5 1.0 collective-permute-done.23.fresh_other
  105.5 7.7 %shard_map.79 = bf16[1024,1024]{1,0:T(8,128)(2,1)} custom-call(bf16[1024,2048]{1,0:T(8,128)(2,1)S(1)} %collective-permute-done.1.other_ref, bf16[1024,4096]{1,0:T(8,128)(2,1)S(1)} %bitcast.42, f32[1024,1024]{1,0:T(8,128)S(1)} %get-tuple-element.51.own_ref, bf16[16,2048]{1,0:T(8,128)(2,1)S(1)} %collective-permute-done.23.fresh_other, ...), custom_call_target="tpu_custom_call" | custom-call | tf_op jit(solution)/shard_map/pallas_call | solution.py:96
  (82 shorter events, 2.4 us)
Async XLA Ops:
  0.0 5.0 %copy-start = (bf16[2,64,8192]{2,1,0:T(8,128)(2,1)S(1)}, bf16[2,64,8192]{2,1,0:T(8,128)(2,1)}, u32[]{:S(2)}) copy-start(bf16[2,64,8192]{2,1,0:T(8,128)(2,1)} %param.8) | copy-start | bytes 6291460
  0.0 5.0 %copy-start.4 = (bf16[8192,32]{0,1:T(8,128)(2,1)S(1)}, bf16[8192,32]{0,1:T(8,128)(2,1)}, u32[]{:S(2)}) copy-start(bf16[8192,32]{0,1:T(8,128)(2,1)} %param.10) | copy-start | bytes 1572868
  0.0 15.6 %collective-permute-start.3 = (bf16[16,2048]{1,0:T(8,128)(2,1)}, bf16[16,2048]{1,0:T(8,128)(2,1)S(1)}, u32[]{:S(2)}, u32[]{:S(2)}) collective-permute-start(bf16[16,2048]{1,0:T(8,128)(2,1)} %param.12), channel_id=1, source_target_pairs={{0,128},{128,129},{1,0},{129,1},{2,130},{130,131},{3,2},{131,3},{4... | collective-permute-start | bytes 196616 | tf_op jit(solution)/shard_map/ppermute | solution.py:167
  2.1 13.5 %collective-permute-start.4 = (bf16[16,2048]{1,0:T(8,128)(2,1)}, bf16[16,2048]{1,0:T(8,128)(2,1)S(1)}, u32[]{:S(2)}, u32[]{:S(2)}) collective-permute-start(bf16[16,2048]{1,0:T(8,128)(2,1)} %param.12), channel_id=1, source_target_pairs={{128,1},{1,128},{130,3},{3,130},{132,5},{5,132},{134,7},{7,134},{1... | collective-permute-start | bytes 196616 | tf_op jit(solution)/shard_map/ppermute | solution.py:168
  5.0 4.9 %copy-start.6 = (s32[256]{0:T(256)S(1)}, s32[256]{0:T(256)}, u32[]{:S(2)}) copy-start(s32[256]{0:T(256)} %param.13) | copy-start | bytes 3076
  5.0 10.7 %copy-start.5 = (bf16[16,2048]{1,0:T(8,128)(2,1)S(1)}, bf16[16,2048]{1,0:T(8,128)(2,1)}, u32[]{:S(2)}) copy-start(bf16[16,2048]{1,0:T(8,128)(2,1)} %param.12) | copy-start | bytes 196612
  6.1 4.3 %collective-permute-start = (bf16[2,2048]{1,0:T(2,128)(2,1)S(1)}, bf16[2,2048]{1,0:T(2,128)(2,1)S(1)}, u32[]{:S(2)}, u32[]{:S(2)}) collective-permute-start(bf16[2,2048]{1,0:T(2,128)(2,1)S(1)} %convert_element_type.23), channel_id=1, source_target_pairs={{0,128},{128,0},{1,129},{129,1},{2,130},{130,2},{3,131},{131,3},{4... | collective-permute-start | bytes 24584 | tf_op jit(solution)/shard_map/ppermute | solution.py:24
  10.5 5.1 %collective-permute-start.2 = (bf16[4,2048]{1,0:T(4,128)(2,1)S(1)}, bf16[4,2048]{1,0:T(4,128)(2,1)S(1)}, u32[]{:S(2)}, u32[]{:S(2)}) collective-permute-start(bf16[4,2048]{1,0:T(4,128)(2,1)S(1)} %pad_maximum_fusion.12), channel_id=1, source_target_pairs={{0,32},{32,0},{64,96},{96,64},{1,33},{33,1},{65,97},{97,65},{2,34}... | collective-permute-start | bytes 49160 | tf_op jit(solution)/shard_map/ppermute | solution.py:24
  12.4 92.1 %collective-permute-start.1 = (bf16[1024,2048]{1,0:T(8,128)(2,1)}, bf16[1024,2048]{1,0:T(8,128)(2,1)S(1)}, u32[]{:S(2)}, u32[]{:S(2)}) collective-permute-start(bf16[1024,2048]{1,0:T(8,128)(2,1)} %store_ref.1), channel_id=1, source_target_pairs={{0,1},{1,0},{2,3},{3,2},{4,5},{5,4},{6,7},{7,6},{8,9},{9,8},{10,11... | collective-permute-start | bytes 12582920 | tf_op jit(solution)/shard_map/ppermute | solution.py:19
  15.7 5.4 %collective-permute-start.5 = (bf16[16,4096]{1,0:T(8,128)(2,1)S(1)}, bf16[16,4096]{1,0:T(8,128)(2,1)S(1)}, u32[]{:S(2)}, u32[]{:S(2)}) collective-permute-start(bf16[16,4096]{1,0:T(8,128)(2,1)S(1)} %pad_maximum_fusion.10), channel_id=1, source_target_pairs={{0,32},{32,64},{64,96},{96,0},{1,33},{33,65},{65,97},{97,1},{2,34}... | collective-permute-start | bytes 393224 | tf_op jit(solution)/shard_map/ppermute | solution.py:19
  16.1 6.8 %collective-permute-start.6 = (bf16[16,4096]{1,0:T(8,128)(2,1)S(1)}, bf16[16,4096]{1,0:T(8,128)(2,1)S(1)}, u32[]{:S(2)}, u32[]{:S(2)}) collective-permute-start(bf16[16,4096]{1,0:T(8,128)(2,1)S(1)} %pad_maximum_fusion.10), channel_id=1, source_target_pairs={{0,64},{32,96},{64,0},{96,32},{1,65},{33,97},{65,1},{97,33},{2,66}... | collective-permute-start | bytes 393224 | tf_op jit(solution)/shard_map/ppermute | solution.py:19
  18.8 4.3 %collective-permute-start.7 = (bf16[16,4096]{1,0:T(8,128)(2,1)S(1)}, bf16[16,4096]{1,0:T(8,128)(2,1)S(1)}, u32[]{:S(2)}, u32[]{:S(2)}) collective-permute-start(bf16[16,4096]{1,0:T(8,128)(2,1)S(1)} %pad_maximum_fusion.10), channel_id=1, source_target_pairs={{0,96},{32,0},{64,32},{96,64},{1,97},{33,1},{65,33},{97,65},{2,98}... | collective-permute-start | bytes 393224 | tf_op jit(solution)/shard_map/ppermute | solution.py:19
  20.3 8.5 %collective-permute-start.10 = (bf16[8,2048]{1,0:T(8,128)(2,1)S(1)}, bf16[8,2048]{1,0:T(8,128)(2,1)S(1)}, u32[]{:S(2)}, u32[]{:S(2)}) collective-permute-start(bf16[8,2048]{1,0:T(8,128)(2,1)S(1)} %pad_maximum_fusion.11), channel_id=1, source_target_pairs={{0,64},{32,96},{64,0},{96,32},{1,65},{33,97},{65,1},{97,33},{2,66}... | collective-permute-start | bytes 98312 | tf_op jit(solution)/shard_map/ppermute | solution.py:24
  23.1 15.0 %collective-permute-start.8 = (bf16[64,4096]{1,0:T(8,128)(2,1)S(1)}, bf16[64,4096]{1,0:T(8,128)(2,1)S(1)}, u32[]{:S(2)}, u32[]{:S(2)}) collective-permute-start(bf16[64,4096]{1,0:T(8,128)(2,1)S(1)} %bitcast.45), channel_id=1, source_target_pairs={{0,4},{4,8},{8,12},{12,16},{16,20},{20,24},{24,28},{28,0},{1,5},{5... | collective-permute-start | bytes 1572872 | tf_op jit(solution)/shard_map/ppermute | solution.py:19
  24.8 13.3 %collective-permute-start.9 = (bf16[64,4096]{1,0:T(8,128)(2,1)S(1)}, bf16[64,4096]{1,0:T(8,128)(2,1)S(1)}, u32[]{:S(2)}, u32[]{:S(2)}) collective-permute-start(bf16[64,4096]{1,0:T(8,128)(2,1)S(1)} %bitcast.46), channel_id=1, source_target_pairs={{0,28},{4,0},{8,4},{12,8},{16,12},{20,16},{24,20},{28,24},{1,29},{... | collective-permute-start | bytes 1572872 | tf_op jit(solution)/shard_map/ppermute | solution.py:19
  29.1 60.8 %collective-permute-start.17 = (bf16[4,4096]{1,0:T(4,128)(2,1)S(1)}, bf16[4,4096]{1,0:T(4,128)(2,1)S(1)}, u32[]{:S(2)}, u32[]{:S(2)}) collective-permute-start(bf16[4,4096]{1,0:T(4,128)(2,1)S(1)} %get-tuple-element.53), channel_id=1, source_target_pairs={{0,16},{4,20},{8,24},{12,28},{16,0},{20,4},{24,8},{28,12},{1,17},{... | collective-permute-start | bytes 98312 | tf_op jit(solution)/shard_map/ppermute | solution.py:19
  33.2 9.6 %collective-permute-start.22 = (bf16[64,4096]{1,0:T(8,128)(2,1)S(1)}, bf16[64,4096]{1,0:T(8,128)(2,1)S(1)}, u32[]{:S(2)}, u32[]{:S(2)}) collective-permute-start(bf16[64,4096]{1,0:T(8,128)(2,1)S(1)} %bitcast.47), channel_id=1, source_target_pairs={{0,2},{2,0},{1,3},{3,1},{4,6},{6,4},{5,7},{7,5},{8,10},{10,8},{9,1... | collective-permute-start | bytes 1572872 | tf_op jit(solution)/shard_map/ppermute | solution.py:19
  38.2 24.6 %collective-permute-start.21 = (bf16[128,4096]{1,0:T(8,128)(2,1)S(1)}, bf16[128,4096]{1,0:T(8,128)(2,1)S(1)}, u32[]{:S(2)}, u32[]{:S(2)}) collective-permute-start(bf16[128,4096]{1,0:T(8,128)(2,1)S(1)} %constant_dynamic-update-slice_fusion), channel_id=1, source_target_pairs={{0,2},{2,0},{1,3},{3,1},{4,6},{6,4},{5,7},{7,5},{8,10},{10,8},{9,1... | collective-permute-start | bytes 3145736 | tf_op jit(solution)/shard_map/ppermute | solution.py:19
  42.6 16.9 %collective-permute-start.11 = (bf16[68,4096]{1,0:T(8,128)(2,1)S(1)}, bf16[68,4096]{1,0:T(8,128)(2,1)S(1)}, u32[]{:S(2)}, u32[]{:S(2)}) collective-permute-start(bf16[68,4096]{1,0:T(8,128)(2,1)S(1)} %get-tuple-element.37), channel_id=1, source_target_pairs={{0,4},{4,8},{8,12},{12,16},{16,20},{20,24},{24,28},{28,0},{1,5},{5... | collective-permute-start | bytes 1671176 | tf_op jit(solution)/shard_map/ppermute | solution.py:19
  42.7 16.8 %collective-permute-start.12 = (bf16[68,4096]{1,0:T(8,128)(2,1)S(1)}, bf16[68,4096]{1,0:T(8,128)(2,1)S(1)}, u32[]{:S(2)}, u32[]{:S(2)}) collective-permute-start(bf16[68,4096]{1,0:T(8,128)(2,1)S(1)} %get-tuple-element.38), channel_id=1, source_target_pairs={{0,28},{4,0},{8,4},{12,8},{16,12},{20,16},{24,20},{28,24},{1,29},{... | collective-permute-start | bytes 1671176 | tf_op jit(solution)/shard_map/ppermute | solution.py:19
  59.7 31.0 %collective-permute-start.20 = (bf16[128,4096]{1,0:T(8,128)(2,1)S(1)}, bf16[128,4096]{1,0:T(8,128)(2,1)S(1)}, u32[]{:S(2)}, u32[]{:S(2)}) collective-permute-start(bf16[128,4096]{1,0:T(8,128)(2,1)S(1)} %pad_maximum_fusion.1), channel_id=1, source_target_pairs={{0,2},{2,0},{1,3},{3,1},{4,6},{6,4},{5,7},{7,5},{8,10},{10,8},{9,1... | collective-permute-start | bytes 3145736 | tf_op jit(solution)/shard_map/ppermute | solution.py:19
  60.7 16.4 %collective-permute-start.13 = (bf16[68,4096]{1,0:T(8,128)(2,1)S(1)}, bf16[68,4096]{1,0:T(8,128)(2,1)S(1)}, u32[]{:S(2)}, u32[]{:S(2)}) collective-permute-start(bf16[68,4096]{1,0:T(8,128)(2,1)S(1)} %pad_maximum_fusion.4), channel_id=1, source_target_pairs={{0,4},{4,8},{8,12},{12,16},{16,20},{20,24},{24,28},{28,0},{1,5},{5... | collective-permute-start | bytes 1671176 | tf_op jit(solution)/shard_map/ppermute | solution.py:19
  62.9 14.6 %collective-permute-start.14 = (bf16[68,4096]{1,0:T(8,128)(2,1)S(1)}, bf16[68,4096]{1,0:T(8,128)(2,1)S(1)}, u32[]{:S(2)}, u32[]{:S(2)}) collective-permute-start(bf16[68,4096]{1,0:T(8,128)(2,1)S(1)} %pad_maximum_fusion.5), channel_id=1, source_target_pairs={{0,28},{4,0},{8,4},{12,8},{16,12},{20,16},{24,20},{28,24},{1,29},{... | collective-permute-start | bytes 1671176 | tf_op jit(solution)/shard_map/ppermute | solution.py:19
  77.1 1.2 %copy-start.3 = (bf16[68,4096]{1,0:T(8,128)(2,1)}, bf16[68,4096]{1,0:T(8,128)(2,1)S(1)}, u32[]{:S(2)}) copy-start(bf16[68,4096]{1,0:T(8,128)(2,1)S(1)} %collective-permute-done.13) | copy-start | bytes 1671172
  77.5 0.8 copy-start.2
  78.4 2.9 %slice-start = ((bf16[68,4096]{1,0:T(8,128)(2,1)}), bf16[64,4096]{1,0:T(8,128)(2,1)S(1)}, s32[]{:S(2)}) async-start(bf16[68,4096]{1,0:T(8,128)(2,1)} %copy-done.2), calls=%async_computation | async-start | bytes 1048576 | tf_op jit(solution)/shard_map/slice | solution.py:227
  78.4 2.8 %slice-start.1 = ((bf16[68,4096]{1,0:T(8,128)(2,1)}), bf16[64,4096]{1,0:T(8,128)(2,1)S(1)}, s32[]{:S(2)}) async-start(bf16[68,4096]{1,0:T(8,128)(2,1)} %copy-done.3), calls=%async_computation.1 | async-start | bytes 1048576 | tf_op jit(solution)/shard_map/slice | solution.py:227
  78.5 9.4 %collective-permute-start.15 = (bf16[36,4096]{1,0:T(8,128)(2,1)S(1)}, bf16[36,4096]{1,0:T(8,128)(2,1)S(1)}, u32[]{:S(2)}, u32[]{:S(2)}) collective-permute-start(bf16[36,4096]{1,0:T(8,128)(2,1)S(1)} %pad_maximum_fusion.8), channel_id=1, source_target_pairs={{0,4},{4,8},{8,12},{12,16},{16,20},{20,24},{24,28},{28,0},{1,5},{5... | collective-permute-start | bytes 884744 | tf_op jit(solution)/shard_map/ppermute | solution.py:19
  80.2 9.7 %collective-permute-start.16 = (bf16[36,4096]{1,0:T(8,128)(2,1)S(1)}, bf16[36,4096]{1,0:T(8,128)(2,1)S(1)}, u32[]{:S(2)}, u32[]{:S(2)}) collective-permute-start(bf16[36,4096]{1,0:T(8,128)(2,1)S(1)} %pad_maximum_fusion.9), channel_id=1, source_target_pairs={{0,28},{4,0},{8,4},{12,8},{16,12},{20,16},{24,20},{28,24},{1,29},{... | collective-permute-start | bytes 884744 | tf_op jit(solution)/shard_map/ppermute | solution.py:19
  87.9 6.6 %collective-permute-start.19 = (bf16[128,4096]{1,0:T(8,128)(2,1)S(1)}, bf16[128,4096]{1,0:T(8,128)(2,1)S(1)}, u32[]{:S(2)}, u32[]{:S(2)}) collective-permute-start(bf16[128,4096]{1,0:T(8,128)(2,1)S(1)} %pad_maximum_fusion), channel_id=1, source_target_pairs={{0,2},{2,0},{1,3},{3,1},{4,6},{6,4},{5,7},{7,5},{8,10},{10,8},{9,1... | collective-permute-start | bytes 3145736 | tf_op jit(solution)/shard_map/ppermute | solution.py:19
  90.1 2.9 %collective-permute-start.18 = (bf16[66,4096]{1,0:T(8,128)(2,1)S(1)}, bf16[66,4096]{1,0:T(8,128)(2,1)S(1)}, u32[]{:S(2)}, u32[]{:S(2)}) collective-permute-start(bf16[66,4096]{1,0:T(8,128)(2,1)S(1)} %pad_maximum_fusion.6), channel_id=1, source_target_pairs={{0,2},{2,0},{1,3},{3,1},{4,6},{6,4},{5,7},{7,5},{8,10},{10,8},{9,1... | collective-permute-start | bytes 1622024 | tf_op jit(solution)/shard_map/ppermute | solution.py:19
  93.1 12.4 %collective-permute-start.23 = (bf16[16,2048]{1,0:T(8,128)(2,1)S(1)}, bf16[16,2048]{1,0:T(8,128)(2,1)S(1)}, u32[]{:S(2)}, u32[]{:S(2)}) collective-permute-start(bf16[16,2048]{1,0:T(8,128)(2,1)S(1)} %pad.9.fresh_ref), channel_id=1, source_target_pairs={{0,1},{1,0},{2,3},{3,2},{4,5},{5,4},{6,7},{7,6},{8,9},{9,8},{10,11... | collective-permute-start | bytes 196616 | tf_op jit(solution)/shard_map/ppermute | solution.py:19
  95.4 2.2 %copy-start.1 = (bf16[1024,2048]{1,0:T(8,128)(2,1)S(1)}, bf16[1024,2048]{1,0:T(8,128)(2,1)}, u32[]{:S(2)}) copy-start(bf16[1024,2048]{1,0:T(8,128)(2,1)} %store_ref.1) | copy-start | bytes 12582916

commit v5 on v4

--- a/solution.py
+++ b/solution.py
@@ -49,65 +49,54 @@
     return sketch.reshape(examples, -1).astype(jnp.bfloat16)
 
 
-def own_kernel(store_ref, valid_ref, fresh_ref, out_ref, fresh_out_ref):
+def own_kernel(examples, store_ref, valid_ref, fresh_ref, out_ref):
     out_ref[...] = dot_t(store_ref[...], valid_ref[...])
-    fresh_out_ref[...] = dot_t(fresh_ref[...], valid_ref[...])
-
-
-def own_scores(store, valid, fresh):
+    n = fresh_ref.shape[0]
+    value = dot_t(fresh_ref[...], valid_ref[...])
+    row = lax.broadcasted_iota(jnp.int32, value.shape, 0)
+    out_ref[:n] = jnp.where(row < examples, value, out_ref[:n])
+
+
+def own_scores(store, valid, fresh, examples):
     rows, half = store.shape
     columns = valid.shape[0]
     whole = lambda array: pl.BlockSpec(array.shape, lambda i: (0, 0), pipeline_mode=pl.Buffered(1))
     return pl.pallas_call(
-        own_kernel,
+        functools.partial(own_kernel, examples),
         grid=(columns // BLOCK,),
         in_specs=[
             whole(store),
             pl.BlockSpec((BLOCK, half), lambda i: (i, 0)),
             whole(fresh),
         ],
-        out_specs=[
-            pl.BlockSpec((rows, BLOCK), lambda i: (0, i)),
-            pl.BlockSpec((fresh.shape[0], BLOCK), lambda i: (0, i)),
-        ],
-        out_shape=[
-            jax.ShapeDtypeStruct((rows, columns), jnp.float32),
-            jax.ShapeDtypeStruct((fresh.shape[0], columns), jnp.float32),
-        ],
+        out_specs=pl.BlockSpec((rows, BLOCK), lambda i: (0, i)),
+        out_shape=jax.ShapeDtypeStruct((rows, columns), jnp.float32),
         compiler_params=pltpu.CompilerParams(vmem_limit_bytes=16 * MIB),
         cost_estimate=pl.CostEstimate(flops=0, bytes_accessed=0, transcendentals=0),
     )(store, valid, fresh)
 
 
-def last_kernel(factor, examples, other_ref, valid_ref, own_ref, fresh_other, fresh_own, out_ref):
+def last_kernel(factor, other_ref, valid_ref, own_ref, out_ref):
     total = own_ref[...] + dot_t(other_ref[...], valid_ref[...])
     out_ref[...] = (total * factor).astype(out_ref.dtype)
-    n = fresh_own.shape[0]
-    value = fresh_own[...] + dot_t(fresh_other[...], valid_ref[...])
-    value = (value * factor).astype(out_ref.dtype)
-    row = lax.broadcasted_iota(jnp.int32, value.shape, 0)
-    out_ref[:n] = jnp.where(row < examples, value, out_ref[:n])
-
-
-def last_scores(other, valid, own, fresh_other, fresh_own, factor, examples):
+
+
+def last_scores(other, valid, own, factor):
     rows, half = other.shape
     columns = valid.shape[0]
-    whole = lambda array: pl.BlockSpec(array.shape, lambda i: (0, 0), pipeline_mode=pl.Buffered(1))
     return pl.pallas_call(
-        functools.partial(last_kernel, factor, examples),
+        functools.partial(last_kernel, factor),
         grid=(columns // BLOCK,),
         in_specs=[
-            whole(other),
+            pl.BlockSpec((rows, half), lambda i: (0, 0), pipeline_mode=pl.Buffered(1)),
             pl.BlockSpec((BLOCK, half), lambda i: (i, 1)),
             pl.BlockSpec((rows, BLOCK), lambda i: (0, i)),
-            whole(fresh_other),
-            pl.BlockSpec((fresh_own.shape[0], BLOCK), lambda i: (0, i)),
         ],
         out_specs=pl.BlockSpec((rows, BLOCK), lambda i: (0, i)),
         out_shape=jax.ShapeDtypeStruct((rows, columns), jnp.bfloat16),
         compiler_params=pltpu.CompilerParams(vmem_limit_bytes=16 * MIB),
         cost_estimate=pl.CostEstimate(flops=0, bytes_accessed=0, transcendentals=0),
-    )(other, valid, own, fresh_other, fresh_own)
+    )(other, valid, own)
 
 
 def fill_kernel(table_ref, mine_ref, twin_ref, *refs):
@@ -251,11 +240,10 @@
     fresh = jnp.pad(fresh[:, :half], ((0, 16 - examples), (0, 0)))
     fresh_other = shifted(fresh, "yh", 1)
     valid_all = whole[0].reshape(nx * nz * nc * rows_v, 2 * half)
-    own, fresh_own = own_scores(store, valid_all, fresh)
+    own = own_scores(store, valid_all, fresh, examples)
     other, own = lax.optimization_barrier((other, own))
-    return last_scores(
-        other, valid_all, own, fresh_other, fresh_own, (2 * half) ** (-0.5), examples
-    )
+    other = lax.dynamic_update_slice(other, fresh_other[:examples], (0, 0))
+    return last_scores(other, valid_all, own, (2 * half) ** (-0.5))
 
 
 def solution(mesh):

time: 115 us -> 114 us (level)
  transfers between devices with their start and end apart: 24 -> 24, of which waited for: 10 -> 11; matrix products, arithmetic and copies ran while one was open for 5% -> 5% of each run, Pallas kernels for 10% -> 10%
where the time goes in v5:
time: 114 us; the launch traced here: 112 us
  starting transfers between devices  48.6 us (43%)
  waiting for transfers between devices  37.9 us (33%)
  Pallas kernels  17.9 us (16%)
  matrix products  3.21 us (3%)
  local copies, waits for them, and re-layouts  2.65 us (2%)
  other arithmetic  1.39 us (1%)
    ppermute x19, starting transfers between devices, shifted(): lax.ppermute(array, axis, [(i, (i + by) % size) for i in range(size)])  40.7 us
    ppermute x19, waiting for transfers between devices, shifted(): lax.ppermute(array, axis, [(i, (i + by) % size) for i in range(size)])  37.5 us
    pallas_call x1, Pallas kernels, own_scores(): pl.pallas_call(functools.partial(own_kernel, examples), grid=(columns //...  6.83 us
    pallas_call x1, Pallas kernels, last_scores(): pl.pallas_call(functools.partial(last_kernel, factor), grid=(columns // B...  6.68 us
    ppermute x3, starting transfers between devices, paired(): return lax.ppermute(array, axis, [(i, i ^ bit) for i in range(size)])  5.12 us
    pallas_call x5, Pallas kernels, filled(): pl.pallas_call(fill_kernel, grid_spec=pltpu.PrefetchScalarGridSpec(num_sc...  4.38 us
  transfers between devices with their start and end apart: 24, of which 11 were waited for; matrix products, arithmetic and copies ran while one was open for 5% of the time, Pallas kernels for 10%

profile of v5, /device:TPU:1, one launch (start us, length us, event | category | flops | bytes accessed | tf_op | source)
XLA Modules:
  0.0 112.2 jit_solution(11589297255589479335)
XLA Ops:
  0.0 2.1 %collective-permute-start.3 = (bf16[16,2048]{1,0:T(8,128)(2,1)}, bf16[16,2048]{1,0:T(8,128)(2,1)S(1)}, u32[]{:S(2)}, u32[]{:S(2)}) collective-permute-start(bf16[16,2048]{1,0:T(8,128)(2,1)} %param.12), channel_id=1, source_target_pairs={{0,128},{128,129},{1,0},{129,1},{2,130},{130,131},{3,2},{131,3},{4... | collective-permute-start | bytes 196616 | tf_op jit(solution)/shard_map/ppermute | solution.py:156
  2.1 0.7 collective-permute-start.4
  2.8 2.1 %convolution_convert_fusion.1 = bf16[128,64]{0,1:T(8,128)(2,1)S(1)} fusion(bf16[128,5120]{1,0:T(8,128)(2,1)} %bitcast.56, bf16[5120,64]{0,1:T(8,128)(2,1)} %param.9), kind=kOutput, calls=%fused_computation.3 | convolution fusion | flops 83894272 | bytes 1982464 | tf_op jit(solution)/shard_map/dot_general | solution.py:36
  4.9 0.1 copy.18
  5.0 0.8 convolution_convert_fusion.2
  5.9 0.1 fusion
  6.1 3.3 %collective-permute-start = (bf16[2,2048]{1,0:T(2,128)(2,1)S(1)}, bf16[2,2048]{1,0:T(2,128)(2,1)S(1)}, u32[]{:S(2)}, u32[]{:S(2)}) collective-permute-start(bf16[2,2048]{1,0:T(2,128)(2,1)S(1)} %convert_element_type.23), channel_id=1, source_target_pairs={{0,128},{128,0},{1,129},{129,1},{2,130},{130,2},{3,131},{131,3},{4... | collective-permute-start | bytes 24584 | tf_op jit(solution)/shard_map/ppermute | solution.py:24
  9.9 0.2 select_reduce_fusion
  10.1 0.4 collective-permute-done
  10.5 1.3 %collective-permute-start.2 = (bf16[4,2048]{1,0:T(4,128)(2,1)S(1)}, bf16[4,2048]{1,0:T(4,128)(2,1)S(1)}, u32[]{:S(2)}, u32[]{:S(2)}) collective-permute-start(bf16[4,2048]{1,0:T(4,128)(2,1)S(1)} %pad_maximum_fusion.12), channel_id=1, source_target_pairs={{0,32},{32,0},{64,96},{96,64},{1,33},{33,1},{65,97},{97,65},{2,34}... | collective-permute-start | bytes 49160 | tf_op jit(solution)/shard_map/ppermute | solution.py:24
  12.4 3.3 %collective-permute-start.1 = (bf16[1024,2048]{1,0:T(8,128)(2,1)}, bf16[1024,2048]{1,0:T(8,128)(2,1)S(1)}, u32[]{:S(2)}, u32[]{:S(2)}) collective-permute-start(bf16[1024,2048]{1,0:T(8,128)(2,1)} %store_ref.1), channel_id=1, source_target_pairs={{0,1},{1,0},{2,3},{3,2},{4,5},{5,4},{6,7},{7,6},{8,9},{9,8},{10,11... | collective-permute-start | bytes 12582920 | tf_op jit(solution)/shard_map/ppermute | solution.py:19
  15.7 0.3 collective-permute-start.5
  16.1 2.7 %collective-permute-start.6 = (bf16[16,4096]{1,0:T(8,128)(2,1)S(1)}, bf16[16,4096]{1,0:T(8,128)(2,1)S(1)}, u32[]{:S(2)}, u32[]{:S(2)}) collective-permute-start(bf16[16,4096]{1,0:T(8,128)(2,1)S(1)} %pad_maximum_fusion.10), channel_id=1, source_target_pairs={{0,64},{32,96},{64,0},{96,32},{1,65},{33,97},{65,1},{97,33},{2,66}... | collective-permute-start | bytes 393224 | tf_op jit(solution)/shard_map/ppermute | solution.py:19
  18.8 1.5 %collective-permute-start.7 = (bf16[16,4096]{1,0:T(8,128)(2,1)S(1)}, bf16[16,4096]{1,0:T(8,128)(2,1)S(1)}, u32[]{:S(2)}, u32[]{:S(2)}) collective-permute-start(bf16[16,4096]{1,0:T(8,128)(2,1)S(1)} %pad_maximum_fusion.10), channel_id=1, source_target_pairs={{0,96},{32,0},{64,32},{96,64},{1,97},{33,1},{65,33},{97,65},{2,98}... | collective-permute-start | bytes 393224 | tf_op jit(solution)/shard_map/ppermute | solution.py:19
  20.3 0.5 collective-permute-start.10
  20.9 0.2 collective-permute-done.5
  21.1 1.7 %collective-permute-done.6 = bf16[16,4096]{1,0:T(8,128)(2,1)S(1)} collective-permute-done((bf16[16,4096]{1,0:T(8,128)(2,1)S(1)}, bf16[16,4096]{1,0:T(8,128)(2,1)S(1)}, u32[]{:S(2)}, u32[]{:S(2)}) %collective-permute-start.6) | collective-permute-done | bytes 131104 | tf_op jit(solution)/shard_map/ppermute | solution.py:19
  22.9 0.2 collective-permute-done.7
  23.1 1.7 %collective-permute-start.8 = (bf16[64,4096]{1,0:T(8,128)(2,1)S(1)}, bf16[64,4096]{1,0:T(8,128)(2,1)S(1)}, u32[]{:S(2)}, u32[]{:S(2)}) collective-permute-start(bf16[64,4096]{1,0:T(8,128)(2,1)S(1)} %bitcast.45), channel_id=1, source_target_pairs={{0,4},{4,8},{8,12},{12,16},{16,20},{20,24},{24,28},{28,0},{1,5},{5... | collective-permute-start | bytes 1572872 | tf_op jit(solution)/shard_map/ppermute | solution.py:19
  24.8 4.0 %collective-permute-start.9 = (bf16[64,4096]{1,0:T(8,128)(2,1)S(1)}, bf16[64,4096]{1,0:T(8,128)(2,1)S(1)}, u32[]{:S(2)}, u32[]{:S(2)}) collective-permute-start(bf16[64,4096]{1,0:T(8,128)(2,1)S(1)} %bitcast.46), channel_id=1, source_target_pairs={{0,28},{4,0},{8,4},{12,8},{16,12},{20,16},{24,20},{28,24},{1,29},{... | collective-permute-start | bytes 1572872 | tf_op jit(solution)/shard_map/ppermute | solution.py:19
  28.9 0.2 convolution_convert_fusion
  29.1 4.0 %collective-permute-start.17 = (bf16[4,4096]{1,0:T(4,128)(2,1)S(1)}, bf16[4,4096]{1,0:T(4,128)(2,1)S(1)}, u32[]{:S(2)}, u32[]{:S(2)}) collective-permute-start(bf16[4,4096]{1,0:T(4,128)(2,1)S(1)} %get-tuple-element.49), channel_id=1, source_target_pairs={{0,16},{4,20},{8,24},{12,28},{16,0},{20,4},{24,8},{28,12},{1,17},{... | collective-permute-start | bytes 98312 | tf_op jit(solution)/shard_map/ppermute | solution.py:19
  33.2 5.0 %collective-permute-start.22 = (bf16[64,4096]{1,0:T(8,128)(2,1)S(1)}, bf16[64,4096]{1,0:T(8,128)(2,1)S(1)}, u32[]{:S(2)}, u32[]{:S(2)}) collective-permute-start(bf16[64,4096]{1,0:T(8,128)(2,1)S(1)} %bitcast.47), channel_id=1, source_target_pairs={{0,2},{2,0},{1,3},{3,1},{4,6},{6,4},{5,7},{7,5},{8,10},{10,8},{9,1... | collective-permute-start | bytes 1572872 | tf_op jit(solution)/shard_map/ppermute | solution.py:19
  38.2 4.3 %collective-permute-start.21 = (bf16[128,4096]{1,0:T(8,128)(2,1)S(1)}, bf16[128,4096]{1,0:T(8,128)(2,1)S(1)}, u32[]{:S(2)}, u32[]{:S(2)}) collective-permute-start(bf16[128,4096]{1,0:T(8,128)(2,1)S(1)} %constant_dynamic-update-slice_fusion), channel_id=1, source_target_pairs={{0,2},{2,0},{1,3},{3,1},{4,6},{6,4},{5,7},{7,5},{8,10},{10,8},{9,1... | collective-permute-start | bytes 3145736 | tf_op jit(solution)/shard_map/ppermute | solution.py:19
  42.7 3.2 %collective-permute-start.12 = (bf16[68,4096]{1,0:T(8,128)(2,1)S(1)}, bf16[68,4096]{1,0:T(8,128)(2,1)S(1)}, u32[]{:S(2)}, u32[]{:S(2)}) collective-permute-start(bf16[68,4096]{1,0:T(8,128)(2,1)S(1)} %get-tuple-element.36), channel_id=1, source_target_pairs={{0,28},{4,0},{8,4},{12,8},{16,12},{20,16},{24,20},{28,24},{1,29},{... | collective-permute-start | bytes 1671176 | tf_op jit(solution)/shard_map/ppermute | solution.py:19
  45.9 0.8 shard_map.73.refs_0_
  46.7 12.8 %collective-permute-done.11 = bf16[68,4096]{1,0:T(8,128)(2,1)S(1)} collective-permute-done((bf16[68,4096]{1,0:T(8,128)(2,1)S(1)}, bf16[68,4096]{1,0:T(8,128)(2,1)S(1)}, u32[]{:S(2)}, u32[]{:S(2)}) %collective-permute-start.11) | collective-permute-done | bytes 557088 | tf_op jit(solution)/shard_map/ppermute | solution.py:19
  59.7 0.9 collective-permute-start.20
  60.7 2.2 %collective-permute-start.13 = (bf16[68,4096]{1,0:T(8,128)(2,1)S(1)}, bf16[68,4096]{1,0:T(8,128)(2,1)S(1)}, u32[]{:S(2)}, u32[]{:S(2)}) collective-permute-start(bf16[68,4096]{1,0:T(8,128)(2,1)S(1)} %pad_maximum_fusion.4), channel_id=1, source_target_pairs={{0,4},{4,8},{8,12},{12,16},{16,20},{20,24},{24,28},{28,0},{1,5},{5... | collective-permute-start | bytes 1671176 | tf_op jit(solution)/shard_map/ppermute | solution.py:19
  62.9 0.8 collective-permute-start.14
  63.7 1.0 shard_map.74.refs_0_
  64.6 12.5 %collective-permute-done.13 = bf16[68,4096]{1,0:T(8,128)(2,1)S(1)} collective-permute-done((bf16[68,4096]{1,0:T(8,128)(2,1)S(1)}, bf16[68,4096]{1,0:T(8,128)(2,1)S(1)}, u32[]{:S(2)}, u32[]{:S(2)}) %collective-permute-start.13) | collective-permute-done | bytes 557088 | tf_op jit(solution)/shard_map/ppermute | solution.py:19
  77.1 0.4 collective-permute-done.14
  77.8 1.8 %collective-permute-start.15 = (bf16[36,4096]{1,0:T(8,128)(2,1)S(1)}, bf16[36,4096]{1,0:T(8,128)(2,1)S(1)}, u32[]{:S(2)}, u32[]{:S(2)}) collective-permute-start(bf16[36,4096]{1,0:T(8,128)(2,1)S(1)} %pad_maximum_fusion.8), channel_id=1, source_target_pairs={{0,4},{4,8},{8,12},{12,16},{16,20},{20,24},{24,28},{28,0},{1,5},{5... | collective-permute-start | bytes 884744 | tf_op jit(solution)/shard_map/ppermute | solution.py:19
  79.5 1.0 collective-permute-start.16
  80.6 6.5 %collective-permute-done.15 = bf16[36,4096]{1,0:T(8,128)(2,1)S(1)} collective-permute-done((bf16[36,4096]{1,0:T(8,128)(2,1)S(1)}, bf16[36,4096]{1,0:T(8,128)(2,1)S(1)}, u32[]{:S(2)}, u32[]{:S(2)}) %collective-permute-start.15) | collective-permute-done | bytes 294944 | tf_op jit(solution)/shard_map/ppermute | solution.py:19
  87.1 2.0 %collective-permute-start.19 = (bf16[128,4096]{1,0:T(8,128)(2,1)S(1)}, bf16[128,4096]{1,0:T(8,128)(2,1)S(1)}, u32[]{:S(2)}, u32[]{:S(2)}) collective-permute-start(bf16[128,4096]{1,0:T(8,128)(2,1)S(1)} %pad_maximum_fusion), channel_id=1, source_target_pairs={{0,2},{2,0},{1,3},{3,1},{4,6},{6,4},{5,7},{7,5},{8,10},{10,8},{9,1... | collective-permute-start | bytes 3145736 | tf_op jit(solution)/shard_map/ppermute | solution.py:19
  89.4 0.6 collective-permute-start.18
  90.0 1.0 shard_map.75.refs_0_
  90.9 1.4 %collective-permute-done.18 = bf16[66,4096]{1,0:T(8,128)(2,1)S(1)} collective-permute-done((bf16[66,4096]{1,0:T(8,128)(2,1)S(1)}, bf16[66,4096]{1,0:T(8,128)(2,1)S(1)}, u32[]{:S(2)}, u32[]{:S(2)}) %collective-permute-start.18) | collective-permute-done | bytes 540704 | tf_op jit(solution)/shard_map/ppermute | solution.py:19
  92.4 1.3 %collective-permute-start.23 = (bf16[16,2048]{1,0:T(8,128)(2,1)S(1)}, bf16[16,2048]{1,0:T(8,128)(2,1)S(1)}, u32[]{:S(2)}, u32[]{:S(2)}) collective-permute-start(bf16[16,2048]{1,0:T(8,128)(2,1)S(1)} %pad.9.fresh_ref), channel_id=1, source_target_pairs={{0,1},{1,0},{2,3},{3,2},{4,5},{5,4},{6,7},{7,6},{8,9},{9,8},{10,11... | collective-permute-start | bytes 196616 | tf_op jit(solution)/shard_map/ppermute | solution.py:19
  93.7 1.0 shard_map.76.refs_0_
  94.7 0.8 shard_map.77
  95.5 1.4 %copy-done.1 = bf16[1024,2048]{1,0:T(8,128)(2,1)S(1)} copy-done((bf16[1024,2048]{1,0:T(8,128)(2,1)S(1)}, bf16[1024,2048]{1,0:T(8,128)(2,1)}, u32[]{:S(2)}) %copy-start.1) | copy-done | bytes 4194328
  96.9 6.8 %shard_map.78.own_ref = f32[1024,1024]{1,0:T(8,128)S(1)} custom-call(bf16[1024,2048]{1,0:T(8,128)(2,1)S(1)} %copy-done.1, bf16[1024,4096]{1,0:T(8,128)(2,1)S(1)} %bitcast.41, bf16[16,2048]{1,0:T(8,128)(2,1)S(1)} %pad.9.fresh_ref), custom_call_target="tpu_custom_call" | custom-call | tf_op jit(solution)/shard_map/pallas_call | solution.py:64
  103.7 0.3 collective-permute-done.1
  104.1 1.4 %collective-permute-done.23 = bf16[16,2048]{1,0:T(8,128)(2,1)S(1)} collective-permute-done((bf16[16,2048]{1,0:T(8,128)(2,1)S(1)}, bf16[16,2048]{1,0:T(8,128)(2,1)S(1)}, u32[]{:S(2)}, u32[]{:S(2)}) %collective-permute-start.23) | collective-permute-done | bytes 65568 | tf_op jit(solution)/shard_map/ppermute | solution.py:19
  105.5 6.7 %shard_map.79 = bf16[1024,1024]{1,0:T(8,128)(2,1)} custom-call(bf16[1024,2048]{1,0:T(8,128)(2,1)S(1)} %slice_dynamic-update-slice_fusion.other_ref, bf16[1024,4096]{1,0:T(8,128)(2,1)S(1)} %bitcast.42, f32[1024,1024]{1,0:T(8,128)S(1)} %shard_map.78.own_ref), custom_call_target="tpu_custom_call" | custom-call | tf_op jit(solution)/shard_map/pallas_call | solution.py:87
  (77 shorter events, 2.5 us)
Async XLA Ops:
  0.0 5.0 %copy-start = (bf16[2,64,8192]{2,1,0:T(8,128)(2,1)S(1)}, bf16[2,64,8192]{2,1,0:T(8,128)(2,1)}, u32[]{:S(2)}) copy-start(bf16[2,64,8192]{2,1,0:T(8,128)(2,1)} %param.8) | copy-start | bytes 6291460
  0.0 5.0 %copy-start.2 = (bf16[8192,32]{0,1:T(8,128)(2,1)S(1)}, bf16[8192,32]{0,1:T(8,128)(2,1)}, u32[]{:S(2)}) copy-start(bf16[8192,32]{0,1:T(8,128)(2,1)} %param.10) | copy-start | bytes 1572868
  0.0 15.6 %collective-permute-start.3 = (bf16[16,2048]{1,0:T(8,128)(2,1)}, bf16[16,2048]{1,0:T(8,128)(2,1)S(1)}, u32[]{:S(2)}, u32[]{:S(2)}) collective-permute-start(bf16[16,2048]{1,0:T(8,128)(2,1)} %param.12), channel_id=1, source_target_pairs={{0,128},{128,129},{1,0},{129,1},{2,130},{130,131},{3,2},{131,3},{4... | collective-permute-start | bytes 196616 | tf_op jit(solution)/shard_map/ppermute | solution.py:156
  2.1 13.5 %collective-permute-start.4 = (bf16[16,2048]{1,0:T(8,128)(2,1)}, bf16[16,2048]{1,0:T(8,128)(2,1)S(1)}, u32[]{:S(2)}, u32[]{:S(2)}) collective-permute-start(bf16[16,2048]{1,0:T(8,128)(2,1)} %param.12), channel_id=1, source_target_pairs={{128,1},{1,128},{130,3},{3,130},{132,5},{5,132},{134,7},{7,134},{1... | collective-permute-start | bytes 196616 | tf_op jit(solution)/shard_map/ppermute | solution.py:157
  2.8 7.1 %copy-start.4 = (s32[256]{0:T(256)S(1)}, s32[256]{0:T(256)}, u32[]{:S(2)}) copy-start(s32[256]{0:T(256)} %param.13) | copy-start | bytes 3076
  4.9 10.8 %copy-start.3 = (bf16[16,2048]{1,0:T(8,128)(2,1)S(1)}, bf16[16,2048]{1,0:T(8,128)(2,1)}, u32[]{:S(2)}) copy-start(bf16[16,2048]{1,0:T(8,128)(2,1)} %param.12) | copy-start | bytes 196612
  6.1 4.3 %collective-permute-start = (bf16[2,2048]{1,0:T(2,128)(2,1)S(1)}, bf16[2,2048]{1,0:T(2,128)(2,1)S(1)}, u32[]{:S(2)}, u32[]{:S(2)}) collective-permute-start(bf16[2,2048]{1,0:T(2,128)(2,1)S(1)} %convert_element_type.23), channel_id=1, source_target_pairs={{0,128},{128,0},{1,129},{129,1},{2,130},{130,2},{3,131},{131,3},{4... | collective-permute-start | bytes 24584 | tf_op jit(solution)/shard_map/ppermute | solution.py:24
  10.5 5.1 %collective-permute-start.2 = (bf16[4,2048]{1,0:T(4,128)(2,1)S(1)}, bf16[4,2048]{1,0:T(4,128)(2,1)S(1)}, u32[]{:S(2)}, u32[]{:S(2)}) collective-permute-start(bf16[4,2048]{1,0:T(4,128)(2,1)S(1)} %pad_maximum_fusion.12), channel_id=1, source_target_pairs={{0,32},{32,0},{64,96},{96,64},{1,33},{33,1},{65,97},{97,65},{2,34}... | collective-permute-start | bytes 49160 | tf_op jit(solution)/shard_map/ppermute | solution.py:24
  12.4 91.7 %collective-permute-start.1 = (bf16[1024,2048]{1,0:T(8,128)(2,1)}, bf16[1024,2048]{1,0:T(8,128)(2,1)S(1)}, u32[]{:S(2)}, u32[]{:S(2)}) collective-permute-start(bf16[1024,2048]{1,0:T(8,128)(2,1)} %store_ref.1), channel_id=1, source_target_pairs={{0,1},{1,0},{2,3},{3,2},{4,5},{5,4},{6,7},{7,6},{8,9},{9,8},{10,11... | collective-permute-start | bytes 12582920 | tf_op jit(solution)/shard_map/ppermute | solution.py:19
  15.7 5.4 %collective-permute-start.5 = (bf16[16,4096]{1,0:T(8,128)(2,1)S(1)}, bf16[16,4096]{1,0:T(8,128)(2,1)S(1)}, u32[]{:S(2)}, u32[]{:S(2)}) collective-permute-start(bf16[16,4096]{1,0:T(8,128)(2,1)S(1)} %pad_maximum_fusion.10), channel_id=1, source_target_pairs={{0,32},{32,64},{64,96},{96,0},{1,33},{33,65},{65,97},{97,1},{2,34}... | collective-permute-start | bytes 393224 | tf_op jit(solution)/shard_map/ppermute | solution.py:19
  16.1 6.8 %collective-permute-start.6 = (bf16[16,4096]{1,0:T(8,128)(2,1)S(1)}, bf16[16,4096]{1,0:T(8,128)(2,1)S(1)}, u32[]{:S(2)}, u32[]{:S(2)}) collective-permute-start(bf16[16,4096]{1,0:T(8,128)(2,1)S(1)} %pad_maximum_fusion.10), channel_id=1, source_target_pairs={{0,64},{32,96},{64,0},{96,32},{1,65},{33,97},{65,1},{97,33},{2,66}... | collective-permute-start | bytes 393224 | tf_op jit(solution)/shard_map/ppermute | solution.py:19
  18.8 4.3 %collective-permute-start.7 = (bf16[16,4096]{1,0:T(8,128)(2,1)S(1)}, bf16[16,4096]{1,0:T(8,128)(2,1)S(1)}, u32[]{:S(2)}, u32[]{:S(2)}) collective-permute-start(bf16[16,4096]{1,0:T(8,128)(2,1)S(1)} %pad_maximum_fusion.10), channel_id=1, source_target_pairs={{0,96},{32,0},{64,32},{96,64},{1,97},{33,1},{65,33},{97,65},{2,98}... | collective-permute-start | bytes 393224 | tf_op jit(solution)/shard_map/ppermute | solution.py:19
  20.3 8.5 %collective-permute-start.10 = (bf16[8,2048]{1,0:T(8,128)(2,1)S(1)}, bf16[8,2048]{1,0:T(8,128)(2,1)S(1)}, u32[]{:S(2)}, u32[]{:S(2)}) collective-permute-start(bf16[8,2048]{1,0:T(8,128)(2,1)S(1)} %pad_maximum_fusion.11), channel_id=1, source_target_pairs={{0,64},{32,96},{64,0},{96,32},{1,65},{33,97},{65,1},{97,33},{2,66}... | collective-permute-start | bytes 98312 | tf_op jit(solution)/shard_map/ppermute | solution.py:24
  23.1 15.0 %collective-permute-start.8 = (bf16[64,4096]{1,0:T(8,128)(2,1)S(1)}, bf16[64,4096]{1,0:T(8,128)(2,1)S(1)}, u32[]{:S(2)}, u32[]{:S(2)}) collective-permute-start(bf16[64,4096]{1,0:T(8,128)(2,1)S(1)} %bitcast.45), channel_id=1, source_target_pairs={{0,4},{4,8},{8,12},{12,16},{16,20},{20,24},{24,28},{28,0},{1,5},{5... | collective-permute-start | bytes 1572872 | tf_op jit(solution)/shard_map/ppermute | solution.py:19
  24.8 13.3 %collective-permute-start.9 = (bf16[64,4096]{1,0:T(8,128)(2,1)S(1)}, bf16[64,4096]{1,0:T(8,128)(2,1)S(1)}, u32[]{:S(2)}, u32[]{:S(2)}) collective-permute-start(bf16[64,4096]{1,0:T(8,128)(2,1)S(1)} %bitcast.46), channel_id=1, source_target_pairs={{0,28},{4,0},{8,4},{12,8},{16,12},{20,16},{24,20},{28,24},{1,29},{... | collective-permute-start | bytes 1572872 | tf_op jit(solution)/shard_map/ppermute | solution.py:19
  29.1 60.0 %collective-permute-start.17 = (bf16[4,4096]{1,0:T(4,128)(2,1)S(1)}, bf16[4,4096]{1,0:T(4,128)(2,1)S(1)}, u32[]{:S(2)}, u32[]{:S(2)}) collective-permute-start(bf16[4,4096]{1,0:T(4,128)(2,1)S(1)} %get-tuple-element.49), channel_id=1, source_target_pairs={{0,16},{4,20},{8,24},{12,28},{16,0},{20,4},{24,8},{28,12},{1,17},{... | collective-permute-start | bytes 98312 | tf_op jit(solution)/shard_map/ppermute | solution.py:19
  33.2 9.6 %collective-permute-start.22 = (bf16[64,4096]{1,0:T(8,128)(2,1)S(1)}, bf16[64,4096]{1,0:T(8,128)(2,1)S(1)}, u32[]{:S(2)}, u32[]{:S(2)}) collective-permute-start(bf16[64,4096]{1,0:T(8,128)(2,1)S(1)} %bitcast.47), channel_id=1, source_target_pairs={{0,2},{2,0},{1,3},{3,1},{4,6},{6,4},{5,7},{7,5},{8,10},{10,8},{9,1... | collective-permute-start | bytes 1572872 | tf_op jit(solution)/shard_map/ppermute | solution.py:19
  38.2 24.6 %collective-permute-start.21 = (bf16[128,4096]{1,0:T(8,128)(2,1)S(1)}, bf16[128,4096]{1,0:T(8,128)(2,1)S(1)}, u32[]{:S(2)}, u32[]{:S(2)}) collective-permute-start(bf16[128,4096]{1,0:T(8,128)(2,1)S(1)} %constant_dynamic-update-slice_fusion), channel_id=1, source_target_pairs={{0,2},{2,0},{1,3},{3,1},{4,6},{6,4},{5,7},{7,5},{8,10},{10,8},{9,1... | collective-permute-start | bytes 3145736 | tf_op jit(solution)/shard_map/ppermute | solution.py:19
  42.6 16.9 %collective-permute-start.11 = (bf16[68,4096]{1,0:T(8,128)(2,1)S(1)}, bf16[68,4096]{1,0:T(8,128)(2,1)S(1)}, u32[]{:S(2)}, u32[]{:S(2)}) collective-permute-start(bf16[68,4096]{1,0:T(8,128)(2,1)S(1)} %get-tuple-element.35), channel_id=1, source_target_pairs={{0,4},{4,8},{8,12},{12,16},{16,20},{20,24},{24,28},{28,0},{1,5},{5... | collective-permute-start | bytes 1671176 | tf_op jit(solution)/shard_map/ppermute | solution.py:19
  42.7 16.8 %collective-permute-start.12 = (bf16[68,4096]{1,0:T(8,128)(2,1)S(1)}, bf16[68,4096]{1,0:T(8,128)(2,1)S(1)}, u32[]{:S(2)}, u32[]{:S(2)}) collective-permute-start(bf16[68,4096]{1,0:T(8,128)(2,1)S(1)} %get-tuple-element.36), channel_id=1, source_target_pairs={{0,28},{4,0},{8,4},{12,8},{16,12},{20,16},{24,20},{28,24},{1,29},{... | collective-permute-start | bytes 1671176 | tf_op jit(solution)/shard_map/ppermute | solution.py:19
  59.7 30.2 %collective-permute-start.20 = (bf16[128,4096]{1,0:T(8,128)(2,1)S(1)}, bf16[128,4096]{1,0:T(8,128)(2,1)S(1)}, u32[]{:S(2)}, u32[]{:S(2)}) collective-permute-start(bf16[128,4096]{1,0:T(8,128)(2,1)S(1)} %pad_maximum_fusion.1), channel_id=1, source_target_pairs={{0,2},{2,0},{1,3},{3,1},{4,6},{6,4},{5,7},{7,5},{8,10},{10,8},{9,1... | collective-permute-start | bytes 3145736 | tf_op jit(solution)/shard_map/ppermute | solution.py:19
  60.7 16.4 %collective-permute-start.13 = (bf16[68,4096]{1,0:T(8,128)(2,1)S(1)}, bf16[68,4096]{1,0:T(8,128)(2,1)S(1)}, u32[]{:S(2)}, u32[]{:S(2)}) collective-permute-start(bf16[68,4096]{1,0:T(8,128)(2,1)S(1)} %pad_maximum_fusion.4), channel_id=1, source_target_pairs={{0,4},{4,8},{8,12},{12,16},{16,20},{20,24},{24,28},{28,0},{1,5},{5... | collective-permute-start | bytes 1671176 | tf_op jit(solution)/shard_map/ppermute | solution.py:19
  62.9 14.6 %collective-permute-start.14 = (bf16[68,4096]{1,0:T(8,128)(2,1)S(1)}, bf16[68,4096]{1,0:T(8,128)(2,1)S(1)}, u32[]{:S(2)}, u32[]{:S(2)}) collective-permute-start(bf16[68,4096]{1,0:T(8,128)(2,1)S(1)} %pad_maximum_fusion.5), channel_id=1, source_target_pairs={{0,28},{4,0},{8,4},{12,8},{16,12},{20,16},{24,20},{28,24},{1,29},{... | collective-permute-start | bytes 1671176 | tf_op jit(solution)/shard_map/ppermute | solution.py:19
  77.8 9.4 %collective-permute-start.15 = (bf16[36,4096]{1,0:T(8,128)(2,1)S(1)}, bf16[36,4096]{1,0:T(8,128)(2,1)S(1)}, u32[]{:S(2)}, u32[]{:S(2)}) collective-permute-start(bf16[36,4096]{1,0:T(8,128)(2,1)S(1)} %pad_maximum_fusion.8), channel_id=1, source_target_pairs={{0,4},{4,8},{8,12},{12,16},{16,20},{20,24},{24,28},{28,0},{1,5},{5... | collective-permute-start | bytes 884744 | tf_op jit(solution)/shard_map/ppermute | solution.py:19
  79.5 9.7 %collective-permute-start.16 = (bf16[36,4096]{1,0:T(8,128)(2,1)S(1)}, bf16[36,4096]{1,0:T(8,128)(2,1)S(1)}, u32[]{:S(2)}, u32[]{:S(2)}) collective-permute-start(bf16[36,4096]{1,0:T(8,128)(2,1)S(1)} %pad_maximum_fusion.9), channel_id=1, source_target_pairs={{0,28},{4,0},{8,4},{12,8},{16,12},{20,16},{24,20},{28,24},{1,29},{... | collective-permute-start | bytes 884744 | tf_op jit(solution)/shard_map/ppermute | solution.py:19
  87.1 6.6 %collective-permute-start.19 = (bf16[128,4096]{1,0:T(8,128)(2,1)S(1)}, bf16[128,4096]{1,0:T(8,128)(2,1)S(1)}, u32[]{:S(2)}, u32[]{:S(2)}) collective-permute-start(bf16[128,4096]{1,0:T(8,128)(2,1)S(1)} %pad_maximum_fusion), channel_id=1, source_target_pairs={{0,2},{2,0},{1,3},{3,1},{4,6},{6,4},{5,7},{7,5},{8,10},{10,8},{9,1... | collective-permute-start | bytes 3145736 | tf_op jit(solution)/shard_map/ppermute | solution.py:19
  89.4 2.9 %collective-permute-start.18 = (bf16[66,4096]{1,0:T(8,128)(2,1)S(1)}, bf16[66,4096]{1,0:T(8,128)(2,1)S(1)}, u32[]{:S(2)}, u32[]{:S(2)}) collective-permute-start(bf16[66,4096]{1,0:T(8,128)(2,1)S(1)} %pad_maximum_fusion.6), channel_id=1, source_target_pairs={{0,2},{2,0},{1,3},{3,1},{4,6},{6,4},{5,7},{7,5},{8,10},{10,8},{9,1... | collective-permute-start | bytes 1622024 | tf_op jit(solution)/shard_map/ppermute | solution.py:19
  92.4 13.1 %collective-permute-start.23 = (bf16[16,2048]{1,0:T(8,128)(2,1)S(1)}, bf16[16,2048]{1,0:T(8,128)(2,1)S(1)}, u32[]{:S(2)}, u32[]{:S(2)}) collective-permute-start(bf16[16,2048]{1,0:T(8,128)(2,1)S(1)} %pad.9.fresh_ref), channel_id=1, source_target_pairs={{0,1},{1,0},{2,3},{3,2},{4,5},{5,4},{6,7},{7,6},{8,9},{9,8},{10,11... | collective-permute-start | bytes 196616 | tf_op jit(solution)/shard_map/ppermute | solution.py:19
  94.7 2.2 %copy-start.1 = (bf16[1024,2048]{1,0:T(8,128)(2,1)S(1)}, bf16[1024,2048]{1,0:T(8,128)(2,1)}, u32[]{:S(2)}) copy-start(bf16[1024,2048]{1,0:T(8,128)(2,1)} %store_ref.1) | copy-start | bytes 12582916

commit v6 on v5

--- a/solution.py
+++ b/solution.py
@@ -11,6 +11,7 @@
 SIZES = {"yl": 2, "x": 4, "z": 8, "c": 2, "yh": 2}
 MIB = 1024 * 1024
 BLOCK = 256
+WIDE = 512
 FILL_FLOPS = 20_000_000_000
 
 
@@ -86,15 +87,15 @@
     columns = valid.shape[0]
     return pl.pallas_call(
         functools.partial(last_kernel, factor),
-        grid=(columns // BLOCK,),
+        grid=(columns // WIDE,),
         in_specs=[
             pl.BlockSpec((rows, half), lambda i: (0, 0), pipeline_mode=pl.Buffered(1)),
-            pl.BlockSpec((BLOCK, half), lambda i: (i, 1)),
-            pl.BlockSpec((rows, BLOCK), lambda i: (0, i)),
+            pl.BlockSpec((WIDE, half), lambda i: (i, 1)),
+            pl.BlockSpec((rows, WIDE), lambda i: (0, i)),
         ],
-        out_specs=pl.BlockSpec((rows, BLOCK), lambda i: (0, i)),
+        out_specs=pl.BlockSpec((rows, WIDE), lambda i: (0, i)),
         out_shape=jax.ShapeDtypeStruct((rows, columns), jnp.bfloat16),
-        compiler_params=pltpu.CompilerParams(vmem_limit_bytes=16 * MIB),
+        compiler_params=pltpu.CompilerParams(vmem_limit_bytes=24 * MIB),
         cost_estimate=pl.CostEstimate(flops=0, bytes_accessed=0, transcendentals=0),
     )(other, valid, own)
 

time: 114 us -> 114 us (level)
  no operation moved by 1% of the time
where the time goes in v6:
time: 114 us; the launch traced here: 112 us
  starting transfers between devices  48.6 us (43%)
  waiting for transfers between devices  37.9 us (33%)
  Pallas kernels  17.5 us (15%)
  matrix products  3.21 us (3%)
  local copies, waits for them, and re-layouts  2.65 us (2%)
  other arithmetic  1.42 us (1%)
    ppermute x19, starting transfers between devices, shifted(): lax.ppermute(array, axis, [(i, (i + by) % size) for i in range(size)])  40.7 us
    ppermute x19, waiting for transfers between devices, shifted(): lax.ppermute(array, axis, [(i, (i + by) % size) for i in range(size)])  37.5 us
    pallas_call x1, Pallas kernels, own_scores(): pl.pallas_call(functools.partial(own_kernel, examples), grid=(columns //...  6.81 us
    pallas_call x1, Pallas kernels, last_scores(): pl.pallas_call(functools.partial(last_kernel, factor), grid=(columns // W...  6.29 us
    ppermute x3, starting transfers between devices, paired(): return lax.ppermute(array, axis, [(i, i ^ bit) for i in range(size)])  5.12 us
    pallas_call x5, Pallas kernels, filled(): pl.pallas_call(fill_kernel, grid_spec=pltpu.PrefetchScalarGridSpec(num_sc...  4.38 us
  transfers between devices with their start and end apart: 24, of which 11 were waited for; matrix products, arithmetic and copies ran while one was open for 5% of the time, Pallas kernels for 10%

profile of v6, /device:TPU:1, one launch (start us, length us, event | category | flops | bytes accessed | tf_op | source)
XLA Modules:
  0.0 111.8 jit_solution(6675121040780900041)
XLA Ops:
  0.0 2.1 %collective-permute-start.3 = (bf16[16,2048]{1,0:T(8,128)(2,1)}, bf16[16,2048]{1,0:T(8,128)(2,1)S(1)}, u32[]{:S(2)}, u32[]{:S(2)}) collective-permute-start(bf16[16,2048]{1,0:T(8,128)(2,1)} %param.12), channel_id=1, source_target_pairs={{0,128},{128,129},{1,0},{129,1},{2,130},{130,131},{3,2},{131,3},{4... | collective-permute-start | bytes 196616 | tf_op jit(solution)/shard_map/ppermute | solution.py:157
  2.1 0.7 collective-permute-start.4
  2.8 2.1 %convolution_convert_fusion.1 = bf16[128,64]{0,1:T(8,128)(2,1)S(1)} fusion(bf16[128,5120]{1,0:T(8,128)(2,1)} %bitcast.56, bf16[5120,64]{0,1:T(8,128)(2,1)} %param.9), kind=kOutput, calls=%fused_computation.3 | convolution fusion | flops 83894272 | bytes 1982464 | tf_op jit(solution)/shard_map/dot_general | solution.py:37
  4.9 0.1 copy.18
  5.0 0.8 convolution_convert_fusion.2
  5.9 0.1 fusion
  6.1 3.3 %collective-permute-start = (bf16[2,2048]{1,0:T(2,128)(2,1)S(1)}, bf16[2,2048]{1,0:T(2,128)(2,1)S(1)}, u32[]{:S(2)}, u32[]{:S(2)}) collective-permute-start(bf16[2,2048]{1,0:T(2,128)(2,1)S(1)} %convert_element_type.23), channel_id=1, source_target_pairs={{0,128},{128,0},{1,129},{129,1},{2,130},{130,2},{3,131},{131,3},{4... | collective-permute-start | bytes 24584 | tf_op jit(solution)/shard_map/ppermute | solution.py:25
  9.9 0.2 select_reduce_fusion
  10.1 0.4 collective-permute-done
  10.5 1.3 %collective-permute-start.2 = (bf16[4,2048]{1,0:T(4,128)(2,1)S(1)}, bf16[4,2048]{1,0:T(4,128)(2,1)S(1)}, u32[]{:S(2)}, u32[]{:S(2)}) collective-permute-start(bf16[4,2048]{1,0:T(4,128)(2,1)S(1)} %pad_maximum_fusion.12), channel_id=1, source_target_pairs={{0,32},{32,0},{64,96},{96,64},{1,33},{33,1},{65,97},{97,65},{2,34}... | collective-permute-start | bytes 49160 | tf_op jit(solution)/shard_map/ppermute | solution.py:25
  12.4 3.3 %collective-permute-start.1 = (bf16[1024,2048]{1,0:T(8,128)(2,1)}, bf16[1024,2048]{1,0:T(8,128)(2,1)S(1)}, u32[]{:S(2)}, u32[]{:S(2)}) collective-permute-start(bf16[1024,2048]{1,0:T(8,128)(2,1)} %store_ref.1), channel_id=1, source_target_pairs={{0,1},{1,0},{2,3},{3,2},{4,5},{5,4},{6,7},{7,6},{8,9},{9,8},{10,11... | collective-permute-start | bytes 12582920 | tf_op jit(solution)/shard_map/ppermute | solution.py:20
  15.7 0.3 collective-permute-start.5
  16.1 2.7 %collective-permute-start.6 = (bf16[16,4096]{1,0:T(8,128)(2,1)S(1)}, bf16[16,4096]{1,0:T(8,128)(2,1)S(1)}, u32[]{:S(2)}, u32[]{:S(2)}) collective-permute-start(bf16[16,4096]{1,0:T(8,128)(2,1)S(1)} %pad_maximum_fusion.10), channel_id=1, source_target_pairs={{0,64},{32,96},{64,0},{96,32},{1,65},{33,97},{65,1},{97,33},{2,66}... | collective-permute-start | bytes 393224 | tf_op jit(solution)/shard_map/ppermute | solution.py:20
  18.8 1.5 %collective-permute-start.7 = (bf16[16,4096]{1,0:T(8,128)(2,1)S(1)}, bf16[16,4096]{1,0:T(8,128)(2,1)S(1)}, u32[]{:S(2)}, u32[]{:S(2)}) collective-permute-start(bf16[16,4096]{1,0:T(8,128)(2,1)S(1)} %pad_maximum_fusion.10), channel_id=1, source_target_pairs={{0,96},{32,0},{64,32},{96,64},{1,97},{33,1},{65,33},{97,65},{2,98}... | collective-permute-start | bytes 393224 | tf_op jit(solution)/shard_map/ppermute | solution.py:20
  20.3 0.5 collective-permute-start.10
  20.9 0.2 collective-permute-done.5
  21.1 1.7 %collective-permute-done.6 = bf16[16,4096]{1,0:T(8,128)(2,1)S(1)} collective-permute-done((bf16[16,4096]{1,0:T(8,128)(2,1)S(1)}, bf16[16,4096]{1,0:T(8,128)(2,1)S(1)}, u32[]{:S(2)}, u32[]{:S(2)}) %collective-permute-start.6) | collective-permute-done | bytes 131104 | tf_op jit(solution)/shard_map/ppermute | solution.py:20
  22.9 0.2 collective-permute-done.7
  23.1 1.7 %collective-permute-start.8 = (bf16[64,4096]{1,0:T(8,128)(2,1)S(1)}, bf16[64,4096]{1,0:T(8,128)(2,1)S(1)}, u32[]{:S(2)}, u32[]{:S(2)}) collective-permute-start(bf16[64,4096]{1,0:T(8,128)(2,1)S(1)} %bitcast.45), channel_id=1, source_target_pairs={{0,4},{4,8},{8,12},{12,16},{16,20},{20,24},{24,28},{28,0},{1,5},{5... | collective-permute-start | bytes 1572872 | tf_op jit(solution)/shard_map/ppermute | solution.py:20
  24.8 4.0 %collective-permute-start.9 = (bf16[64,4096]{1,0:T(8,128)(2,1)S(1)}, bf16[64,4096]{1,0:T(8,128)(2,1)S(1)}, u32[]{:S(2)}, u32[]{:S(2)}) collective-permute-start(bf16[64,4096]{1,0:T(8,128)(2,1)S(1)} %bitcast.46), channel_id=1, source_target_pairs={{0,28},{4,0},{8,4},{12,8},{16,12},{20,16},{24,20},{28,24},{1,29},{... | collective-permute-start | bytes 1572872 | tf_op jit(solution)/shard_map/ppermute | solution.py:20
  28.9 0.2 convolution_convert_fusion
  29.1 4.0 %collective-permute-start.17 = (bf16[4,4096]{1,0:T(4,128)(2,1)S(1)}, bf16[4,4096]{1,0:T(4,128)(2,1)S(1)}, u32[]{:S(2)}, u32[]{:S(2)}) collective-permute-start(bf16[4,4096]{1,0:T(4,128)(2,1)S(1)} %get-tuple-element.49), channel_id=1, source_target_pairs={{0,16},{4,20},{8,24},{12,28},{16,0},{20,4},{24,8},{28,12},{1,17},{... | collective-permute-start | bytes 98312 | tf_op jit(solution)/shard_map/ppermute | solution.py:20
  33.2 5.0 %collective-permute-start.22 = (bf16[64,4096]{1,0:T(8,128)(2,1)S(1)}, bf16[64,4096]{1,0:T(8,128)(2,1)S(1)}, u32[]{:S(2)}, u32[]{:S(2)}) collective-permute-start(bf16[64,4096]{1,0:T(8,128)(2,1)S(1)} %bitcast.47), channel_id=1, source_target_pairs={{0,2},{2,0},{1,3},{3,1},{4,6},{6,4},{5,7},{7,5},{8,10},{10,8},{9,1... | collective-permute-start | bytes 1572872 | tf_op jit(solution)/shard_map/ppermute | solution.py:20
  38.2 4.3 %collective-permute-start.21 = (bf16[128,4096]{1,0:T(8,128)(2,1)S(1)}, bf16[128,4096]{1,0:T(8,128)(2,1)S(1)}, u32[]{:S(2)}, u32[]{:S(2)}) collective-permute-start(bf16[128,4096]{1,0:T(8,128)(2,1)S(1)} %constant_dynamic-update-slice_fusion), channel_id=1, source_target_pairs={{0,2},{2,0},{1,3},{3,1},{4,6},{6,4},{5,7},{7,5},{8,10},{10,8},{9,1... | collective-permute-start | bytes 3145736 | tf_op jit(solution)/shard_map/ppermute | solution.py:20
  42.8 3.2 %collective-permute-start.12 = (bf16[68,4096]{1,0:T(8,128)(2,1)S(1)}, bf16[68,4096]{1,0:T(8,128)(2,1)S(1)}, u32[]{:S(2)}, u32[]{:S(2)}) collective-permute-start(bf16[68,4096]{1,0:T(8,128)(2,1)S(1)} %get-tuple-element.36), channel_id=1, source_target_pairs={{0,28},{4,0},{8,4},{12,8},{16,12},{20,16},{24,20},{28,24},{1,29},{... | collective-permute-start | bytes 1671176 | tf_op jit(solution)/shard_map/ppermute | solution.py:20
  45.9 0.8 shard_map.73.refs_0_
  46.7 12.8 %collective-permute-done.11 = bf16[68,4096]{1,0:T(8,128)(2,1)S(1)} collective-permute-done((bf16[68,4096]{1,0:T(8,128)(2,1)S(1)}, bf16[68,4096]{1,0:T(8,128)(2,1)S(1)}, u32[]{:S(2)}, u32[]{:S(2)}) %collective-permute-start.11) | collective-permute-done | bytes 557088 | tf_op jit(solution)/shard_map/ppermute | solution.py:20
  59.8 0.9 collective-permute-start.20
  60.7 2.2 %collective-permute-start.13 = (bf16[68,4096]{1,0:T(8,128)(2,1)S(1)}, bf16[68,4096]{1,0:T(8,128)(2,1)S(1)}, u32[]{:S(2)}, u32[]{:S(2)}) collective-permute-start(bf16[68,4096]{1,0:T(8,128)(2,1)S(1)} %pad_maximum_fusion.4), channel_id=1, source_target_pairs={{0,4},{4,8},{8,12},{12,16},{16,20},{20,24},{24,28},{28,0},{1,5},{5... | collective-permute-start | bytes 1671176 | tf_op jit(solution)/shard_map/ppermute | solution.py:20
  62.9 0.8 collective-permute-start.14
  63.7 1.0 shard_map.74.refs_0_
  64.6 12.5 %collective-permute-done.13 = bf16[68,4096]{1,0:T(8,128)(2,1)S(1)} collective-permute-done((bf16[68,4096]{1,0:T(8,128)(2,1)S(1)}, bf16[68,4096]{1,0:T(8,128)(2,1)S(1)}, u32[]{:S(2)}, u32[]{:S(2)}) %collective-permute-start.13) | collective-permute-done | bytes 557088 | tf_op jit(solution)/shard_map/ppermute | solution.py:20
  77.2 0.4 collective-permute-done.14
  77.8 1.8 %collective-permute-start.15 = (bf16[36,4096]{1,0:T(8,128)(2,1)S(1)}, bf16[36,4096]{1,0:T(8,128)(2,1)S(1)}, u32[]{:S(2)}, u32[]{:S(2)}) collective-permute-start(bf16[36,4096]{1,0:T(8,128)(2,1)S(1)} %pad_maximum_fusion.8), channel_id=1, source_target_pairs={{0,4},{4,8},{8,12},{12,16},{16,20},{20,24},{24,28},{28,0},{1,5},{5... | collective-permute-start | bytes 884744 | tf_op jit(solution)/shard_map/ppermute | solution.py:20
  79.5 1.0 collective-permute-start.16
  80.6 6.5 %collective-permute-done.15 = bf16[36,4096]{1,0:T(8,128)(2,1)S(1)} collective-permute-done((bf16[36,4096]{1,0:T(8,128)(2,1)S(1)}, bf16[36,4096]{1,0:T(8,128)(2,1)S(1)}, u32[]{:S(2)}, u32[]{:S(2)}) %collective-permute-start.15) | collective-permute-done | bytes 294944 | tf_op jit(solution)/shard_map/ppermute | solution.py:20
  87.2 2.0 %collective-permute-start.19 = (bf16[128,4096]{1,0:T(8,128)(2,1)S(1)}, bf16[128,4096]{1,0:T(8,128)(2,1)S(1)}, u32[]{:S(2)}, u32[]{:S(2)}) collective-permute-start(bf16[128,4096]{1,0:T(8,128)(2,1)S(1)} %pad_maximum_fusion), channel_id=1, source_target_pairs={{0,2},{2,0},{1,3},{3,1},{4,6},{6,4},{5,7},{7,5},{8,10},{10,8},{9,1... | collective-permute-start | bytes 3145736 | tf_op jit(solution)/shard_map/ppermute | solution.py:20
  89.4 0.6 collective-permute-start.18
  90.0 1.0 shard_map.75.refs_0_
  91.0 1.4 %collective-permute-done.18 = bf16[66,4096]{1,0:T(8,128)(2,1)S(1)} collective-permute-done((bf16[66,4096]{1,0:T(8,128)(2,1)S(1)}, bf16[66,4096]{1,0:T(8,128)(2,1)S(1)}, u32[]{:S(2)}, u32[]{:S(2)}) %collective-permute-start.18) | collective-permute-done | bytes 540704 | tf_op jit(solution)/shard_map/ppermute | solution.py:20
  92.4 1.3 %collective-permute-start.23 = (bf16[16,2048]{1,0:T(8,128)(2,1)S(1)}, bf16[16,2048]{1,0:T(8,128)(2,1)S(1)}, u32[]{:S(2)}, u32[]{:S(2)}) collective-permute-start(bf16[16,2048]{1,0:T(8,128)(2,1)S(1)} %pad.9.fresh_ref), channel_id=1, source_target_pairs={{0,1},{1,0},{2,3},{3,2},{4,5},{5,4},{6,7},{7,6},{8,9},{9,8},{10,11... | collective-permute-start | bytes 196616 | tf_op jit(solution)/shard_map/ppermute | solution.py:20
  93.8 1.0 shard_map.76.refs_0_
  94.7 0.8 shard_map.77
  95.5 1.4 %copy-done.1 = bf16[1024,2048]{1,0:T(8,128)(2,1)S(1)} copy-done((bf16[1024,2048]{1,0:T(8,128)(2,1)S(1)}, bf16[1024,2048]{1,0:T(8,128)(2,1)}, u32[]{:S(2)}) %copy-start.1) | copy-done | bytes 4194328
  96.9 6.8 %shard_map.78.own_ref = f32[1024,1024]{1,0:T(8,128)S(1)} custom-call(bf16[1024,2048]{1,0:T(8,128)(2,1)S(1)} %copy-done.1, bf16[1024,4096]{1,0:T(8,128)(2,1)S(1)} %bitcast.41, bf16[16,2048]{1,0:T(8,128)(2,1)S(1)} %pad.9.fresh_ref), custom_call_target="tpu_custom_call" | custom-call | tf_op jit(solution)/shard_map/pallas_call | solution.py:65
  103.7 0.3 collective-permute-done.1
  104.1 1.4 %collective-permute-done.23 = bf16[16,2048]{1,0:T(8,128)(2,1)S(1)} collective-permute-done((bf16[16,2048]{1,0:T(8,128)(2,1)S(1)}, bf16[16,2048]{1,0:T(8,128)(2,1)S(1)}, u32[]{:S(2)}, u32[]{:S(2)}) %collective-permute-start.23) | collective-permute-done | bytes 65568 | tf_op jit(solution)/shard_map/ppermute | solution.py:20
  105.5 6.3 %shard_map.79 = bf16[1024,1024]{1,0:T(8,128)(2,1)} custom-call(bf16[1024,2048]{1,0:T(8,128)(2,1)S(1)} %slice_dynamic-update-slice_fusion.other_ref, bf16[1024,4096]{1,0:T(8,128)(2,1)S(1)} %bitcast.42, f32[1024,1024]{1,0:T(8,128)S(1)} %shard_map.78.own_ref), custom_call_target="tpu_custom_call" | custom-call | tf_op jit(solution)/shard_map/pallas_call | solution.py:88
  (77 shorter events, 2.5 us)
Async XLA Ops:
  0.0 5.0 %copy-start = (bf16[2,64,8192]{2,1,0:T(8,128)(2,1)S(1)}, bf16[2,64,8192]{2,1,0:T(8,128)(2,1)}, u32[]{:S(2)}) copy-start(bf16[2,64,8192]{2,1,0:T(8,128)(2,1)} %param.8) | copy-start | bytes 6291460
  0.0 5.0 %copy-start.2 = (bf16[8192,32]{0,1:T(8,128)(2,1)S(1)}, bf16[8192,32]{0,1:T(8,128)(2,1)}, u32[]{:S(2)}) copy-start(bf16[8192,32]{0,1:T(8,128)(2,1)} %param.10) | copy-start | bytes 1572868
  0.0 15.6 %collective-permute-start.3 = (bf16[16,2048]{1,0:T(8,128)(2,1)}, bf16[16,2048]{1,0:T(8,128)(2,1)S(1)}, u32[]{:S(2)}, u32[]{:S(2)}) collective-permute-start(bf16[16,2048]{1,0:T(8,128)(2,1)} %param.12), channel_id=1, source_target_pairs={{0,128},{128,129},{1,0},{129,1},{2,130},{130,131},{3,2},{131,3},{4... | collective-permute-start | bytes 196616 | tf_op jit(solution)/shard_map/ppermute | solution.py:157
  2.1 13.5 %collective-permute-start.4 = (bf16[16,2048]{1,0:T(8,128)(2,1)}, bf16[16,2048]{1,0:T(8,128)(2,1)S(1)}, u32[]{:S(2)}, u32[]{:S(2)}) collective-permute-start(bf16[16,2048]{1,0:T(8,128)(2,1)} %param.12), channel_id=1, source_target_pairs={{128,1},{1,128},{130,3},{3,130},{132,5},{5,132},{134,7},{7,134},{1... | collective-permute-start | bytes 196616 | tf_op jit(solution)/shard_map/ppermute | solution.py:158
  2.8 7.1 %copy-start.4 = (s32[256]{0:T(256)S(1)}, s32[256]{0:T(256)}, u32[]{:S(2)}) copy-start(s32[256]{0:T(256)} %param.13) | copy-start | bytes 3076
  4.9 10.8 %copy-start.3 = (bf16[16,2048]{1,0:T(8,128)(2,1)S(1)}, bf16[16,2048]{1,0:T(8,128)(2,1)}, u32[]{:S(2)}) copy-start(bf16[16,2048]{1,0:T(8,128)(2,1)} %param.12) | copy-start | bytes 196612
  6.1 4.3 %collective-permute-start = (bf16[2,2048]{1,0:T(2,128)(2,1)S(1)}, bf16[2,2048]{1,0:T(2,128)(2,1)S(1)}, u32[]{:S(2)}, u32[]{:S(2)}) collective-permute-start(bf16[2,2048]{1,0:T(2,128)(2,1)S(1)} %convert_element_type.23), channel_id=1, source_target_pairs={{0,128},{128,0},{1,129},{129,1},{2,130},{130,2},{3,131},{131,3},{4... | collective-permute-start | bytes 24584 | tf_op jit(solution)/shard_map/ppermute | solution.py:25
  10.5 5.1 %collective-permute-start.2 = (bf16[4,2048]{1,0:T(4,128)(2,1)S(1)}, bf16[4,2048]{1,0:T(4,128)(2,1)S(1)}, u32[]{:S(2)}, u32[]{:S(2)}) collective-permute-start(bf16[4,2048]{1,0:T(4,128)(2,1)S(1)} %pad_maximum_fusion.12), channel_id=1, source_target_pairs={{0,32},{32,0},{64,96},{96,64},{1,33},{33,1},{65,97},{97,65},{2,34}... | collective-permute-start | bytes 49160 | tf_op jit(solution)/shard_map/ppermute | solution.py:25
  12.4 91.7 %collective-permute-start.1 = (bf16[1024,2048]{1,0:T(8,128)(2,1)}, bf16[1024,2048]{1,0:T(8,128)(2,1)S(1)}, u32[]{:S(2)}, u32[]{:S(2)}) collective-permute-start(bf16[1024,2048]{1,0:T(8,128)(2,1)} %store_ref.1), channel_id=1, source_target_pairs={{0,1},{1,0},{2,3},{3,2},{4,5},{5,4},{6,7},{7,6},{8,9},{9,8},{10,11... | collective-permute-start | bytes 12582920 | tf_op jit(solution)/shard_map/ppermute | solution.py:20
  15.7 5.4 %collective-permute-start.5 = (bf16[16,4096]{1,0:T(8,128)(2,1)S(1)}, bf16[16,4096]{1,0:T(8,128)(2,1)S(1)}, u32[]{:S(2)}, u32[]{:S(2)}) collective-permute-start(bf16[16,4096]{1,0:T(8,128)(2,1)S(1)} %pad_maximum_fusion.10), channel_id=1, source_target_pairs={{0,32},{32,64},{64,96},{96,0},{1,33},{33,65},{65,97},{97,1},{2,34}... | collective-permute-start | bytes 393224 | tf_op jit(solution)/shard_map/ppermute | solution.py:20
  16.1 6.8 %collective-permute-start.6 = (bf16[16,4096]{1,0:T(8,128)(2,1)S(1)}, bf16[16,4096]{1,0:T(8,128)(2,1)S(1)}, u32[]{:S(2)}, u32[]{:S(2)}) collective-permute-start(bf16[16,4096]{1,0:T(8,128)(2,1)S(1)} %pad_maximum_fusion.10), channel_id=1, source_target_pairs={{0,64},{32,96},{64,0},{96,32},{1,65},{33,97},{65,1},{97,33},{2,66}... | collective-permute-start | bytes 393224 | tf_op jit(solution)/shard_map/ppermute | solution.py:20
  18.8 4.3 %collective-permute-start.7 = (bf16[16,4096]{1,0:T(8,128)(2,1)S(1)}, bf16[16,4096]{1,0:T(8,128)(2,1)S(1)}, u32[]{:S(2)}, u32[]{:S(2)}) collective-permute-start(bf16[16,4096]{1,0:T(8,128)(2,1)S(1)} %pad_maximum_fusion.10), channel_id=1, source_target_pairs={{0,96},{32,0},{64,32},{96,64},{1,97},{33,1},{65,33},{97,65},{2,98}... | collective-permute-start | bytes 393224 | tf_op jit(solution)/shard_map/ppermute | solution.py:20
  20.3 8.5 %collective-permute-start.10 = (bf16[8,2048]{1,0:T(8,128)(2,1)S(1)}, bf16[8,2048]{1,0:T(8,128)(2,1)S(1)}, u32[]{:S(2)}, u32[]{:S(2)}) collective-permute-start(bf16[8,2048]{1,0:T(8,128)(2,1)S(1)} %pad_maximum_fusion.11), channel_id=1, source_target_pairs={{0,64},{32,96},{64,0},{96,32},{1,65},{33,97},{65,1},{97,33},{2,66}... | collective-permute-start | bytes 98312 | tf_op jit(solution)/shard_map/ppermute | solution.py:25
  23.1 15.0 %collective-permute-start.8 = (bf16[64,4096]{1,0:T(8,128)(2,1)S(1)}, bf16[64,4096]{1,0:T(8,128)(2,1)S(1)}, u32[]{:S(2)}, u32[]{:S(2)}) collective-permute-start(bf16[64,4096]{1,0:T(8,128)(2,1)S(1)} %bitcast.45), channel_id=1, source_target_pairs={{0,4},{4,8},{8,12},{12,16},{16,20},{20,24},{24,28},{28,0},{1,5},{5... | collective-permute-start | bytes 1572872 | tf_op jit(solution)/shard_map/ppermute | solution.py:20
  24.8 13.3 %collective-permute-start.9 = (bf16[64,4096]{1,0:T(8,128)(2,1)S(1)}, bf16[64,4096]{1,0:T(8,128)(2,1)S(1)}, u32[]{:S(2)}, u32[]{:S(2)}) collective-permute-start(bf16[64,4096]{1,0:T(8,128)(2,1)S(1)} %bitcast.46), channel_id=1, source_target_pairs={{0,28},{4,0},{8,4},{12,8},{16,12},{20,16},{24,20},{28,24},{1,29},{... | collective-permute-start | bytes 1572872 | tf_op jit(solution)/shard_map/ppermute | solution.py:20
  29.1 60.1 %collective-permute-start.17 = (bf16[4,4096]{1,0:T(4,128)(2,1)S(1)}, bf16[4,4096]{1,0:T(4,128)(2,1)S(1)}, u32[]{:S(2)}, u32[]{:S(2)}) collective-permute-start(bf16[4,4096]{1,0:T(4,128)(2,1)S(1)} %get-tuple-element.49), channel_id=1, source_target_pairs={{0,16},{4,20},{8,24},{12,28},{16,0},{20,4},{24,8},{28,12},{1,17},{... | collective-permute-start | bytes 98312 | tf_op jit(solution)/shard_map/ppermute | solution.py:20
  33.2 9.6 %collective-permute-start.22 = (bf16[64,4096]{1,0:T(8,128)(2,1)S(1)}, bf16[64,4096]{1,0:T(8,128)(2,1)S(1)}, u32[]{:S(2)}, u32[]{:S(2)}) collective-permute-start(bf16[64,4096]{1,0:T(8,128)(2,1)S(1)} %bitcast.47), channel_id=1, source_target_pairs={{0,2},{2,0},{1,3},{3,1},{4,6},{6,4},{5,7},{7,5},{8,10},{10,8},{9,1... | collective-permute-start | bytes 1572872 | tf_op jit(solution)/shard_map/ppermute | solution.py:20
  38.2 24.6 %collective-permute-start.21 = (bf16[128,4096]{1,0:T(8,128)(2,1)S(1)}, bf16[128,4096]{1,0:T(8,128)(2,1)S(1)}, u32[]{:S(2)}, u32[]{:S(2)}) collective-permute-start(bf16[128,4096]{1,0:T(8,128)(2,1)S(1)} %constant_dynamic-update-slice_fusion), channel_id=1, source_target_pairs={{0,2},{2,0},{1,3},{3,1},{4,6},{6,4},{5,7},{7,5},{8,10},{10,8},{9,1... | collective-permute-start | bytes 3145736 | tf_op jit(solution)/shard_map/ppermute | solution.py:20
  42.7 16.9 %collective-permute-start.11 = (bf16[68,4096]{1,0:T(8,128)(2,1)S(1)}, bf16[68,4096]{1,0:T(8,128)(2,1)S(1)}, u32[]{:S(2)}, u32[]{:S(2)}) collective-permute-start(bf16[68,4096]{1,0:T(8,128)(2,1)S(1)} %get-tuple-element.35), channel_id=1, source_target_pairs={{0,4},{4,8},{8,12},{12,16},{16,20},{20,24},{24,28},{28,0},{1,5},{5... | collective-permute-start | bytes 1671176 | tf_op jit(solution)/shard_map/ppermute | solution.py:20
  42.8 16.8 %collective-permute-start.12 = (bf16[68,4096]{1,0:T(8,128)(2,1)S(1)}, bf16[68,4096]{1,0:T(8,128)(2,1)S(1)}, u32[]{:S(2)}, u32[]{:S(2)}) collective-permute-start(bf16[68,4096]{1,0:T(8,128)(2,1)S(1)} %get-tuple-element.36), channel_id=1, source_target_pairs={{0,28},{4,0},{8,4},{12,8},{16,12},{20,16},{24,20},{28,24},{1,29},{... | collective-permute-start | bytes 1671176 | tf_op jit(solution)/shard_map/ppermute | solution.py:20
  59.8 30.2 %collective-permute-start.20 = (bf16[128,4096]{1,0:T(8,128)(2,1)S(1)}, bf16[128,4096]{1,0:T(8,128)(2,1)S(1)}, u32[]{:S(2)}, u32[]{:S(2)}) collective-permute-start(bf16[128,4096]{1,0:T(8,128)(2,1)S(1)} %pad_maximum_fusion.1), channel_id=1, source_target_pairs={{0,2},{2,0},{1,3},{3,1},{4,6},{6,4},{5,7},{7,5},{8,10},{10,8},{9,1... | collective-permute-start | bytes 3145736 | tf_op jit(solution)/shard_map/ppermute | solution.py:20
  60.7 16.4 %collective-permute-start.13 = (bf16[68,4096]{1,0:T(8,128)(2,1)S(1)}, bf16[68,4096]{1,0:T(8,128)(2,1)S(1)}, u32[]{:S(2)}, u32[]{:S(2)}) collective-permute-start(bf16[68,4096]{1,0:T(8,128)(2,1)S(1)} %pad_maximum_fusion.4), channel_id=1, source_target_pairs={{0,4},{4,8},{8,12},{12,16},{16,20},{20,24},{24,28},{28,0},{1,5},{5... | collective-permute-start | bytes 1671176 | tf_op jit(solution)/shard_map/ppermute | solution.py:20
  62.9 14.6 %collective-permute-start.14 = (bf16[68,4096]{1,0:T(8,128)(2,1)S(1)}, bf16[68,4096]{1,0:T(8,128)(2,1)S(1)}, u32[]{:S(2)}, u32[]{:S(2)}) collective-permute-start(bf16[68,4096]{1,0:T(8,128)(2,1)S(1)} %pad_maximum_fusion.5), channel_id=1, source_target_pairs={{0,28},{4,0},{8,4},{12,8},{16,12},{20,16},{24,20},{28,24},{1,29},{... | collective-permute-start | bytes 1671176 | tf_op jit(solution)/shard_map/ppermute | solution.py:20
  77.8 9.4 %collective-permute-start.15 = (bf16[36,4096]{1,0:T(8,128)(2,1)S(1)}, bf16[36,4096]{1,0:T(8,128)(2,1)S(1)}, u32[]{:S(2)}, u32[]{:S(2)}) collective-permute-start(bf16[36,4096]{1,0:T(8,128)(2,1)S(1)} %pad_maximum_fusion.8), channel_id=1, source_target_pairs={{0,4},{4,8},{8,12},{12,16},{16,20},{20,24},{24,28},{28,0},{1,5},{5... | collective-permute-start | bytes 884744 | tf_op jit(solution)/shard_map/ppermute | solution.py:20
  79.5 9.7 %collective-permute-start.16 = (bf16[36,4096]{1,0:T(8,128)(2,1)S(1)}, bf16[36,4096]{1,0:T(8,128)(2,1)S(1)}, u32[]{:S(2)}, u32[]{:S(2)}) collective-permute-start(bf16[36,4096]{1,0:T(8,128)(2,1)S(1)} %pad_maximum_fusion.9), channel_id=1, source_target_pairs={{0,28},{4,0},{8,4},{12,8},{16,12},{20,16},{24,20},{28,24},{1,29},{... | collective-permute-start | bytes 884744 | tf_op jit(solution)/shard_map/ppermute | solution.py:20
  87.2 6.6 %collective-permute-start.19 = (bf16[128,4096]{1,0:T(8,128)(2,1)S(1)}, bf16[128,4096]{1,0:T(8,128)(2,1)S(1)}, u32[]{:S(2)}, u32[]{:S(2)}) collective-permute-start(bf16[128,4096]{1,0:T(8,128)(2,1)S(1)} %pad_maximum_fusion), channel_id=1, source_target_pairs={{0,2},{2,0},{1,3},{3,1},{4,6},{6,4},{5,7},{7,5},{8,10},{10,8},{9,1... | collective-permute-start | bytes 3145736 | tf_op jit(solution)/shard_map/ppermute | solution.py:20
  89.4 2.9 %collective-permute-start.18 = (bf16[66,4096]{1,0:T(8,128)(2,1)S(1)}, bf16[66,4096]{1,0:T(8,128)(2,1)S(1)}, u32[]{:S(2)}, u32[]{:S(2)}) collective-permute-start(bf16[66,4096]{1,0:T(8,128)(2,1)S(1)} %pad_maximum_fusion.6), channel_id=1, source_target_pairs={{0,2},{2,0},{1,3},{3,1},{4,6},{6,4},{5,7},{7,5},{8,10},{10,8},{9,1... | collective-permute-start | bytes 1622024 | tf_op jit(solution)/shard_map/ppermute | solution.py:20
  92.4 13.1 %collective-permute-start.23 = (bf16[16,2048]{1,0:T(8,128)(2,1)S(1)}, bf16[16,2048]{1,0:T(8,128)(2,1)S(1)}, u32[]{:S(2)}, u32[]{:S(2)}) collective-permute-start(bf16[16,2048]{1,0:T(8,128)(2,1)S(1)} %pad.9.fresh_ref), channel_id=1, source_target_pairs={{0,1},{1,0},{2,3},{3,2},{4,5},{5,4},{6,7},{7,6},{8,9},{9,8},{10,11... | collective-permute-start | bytes 196616 | tf_op jit(solution)/shard_map/ppermute | solution.py:20
  94.7 2.2 %copy-start.1 = (bf16[1024,2048]{1,0:T(8,128)(2,1)S(1)}, bf16[1024,2048]{1,0:T(8,128)(2,1)}, u32[]{:S(2)}) copy-start(bf16[1024,2048]{1,0:T(8,128)(2,1)} %store_ref.1) | copy-start | bytes 12582916
